TPU v7x, 128 devices: a whole 4x4x4 slice. The times are simulated.
128 devices in a mesh: section: 4 (over y), tp: 32 (over z, x, core).
Axes of the slice: x: 4, y: 4, z: 4, core: 2. Of those that a mesh axis runs over, the one named last changes fastest.
Arguments:
- forward_inputs: bfloat16 [4, 1024, 8192], P('section', None, 'tp'), may hold values from -6 to 6
- backward_inputs: bfloat16 [4, 1024, 8192], P('section', None, 'tp'), may hold values from -6 to 6
- backward_cotangents: bfloat16 [4, 1024, 8192], P('section', None, 'tp'), may hold values from -0.75 to 0.75
- frozen_weight: bfloat16 [4, 8192, 8192], P('section', None, 'tp'), may hold values from -0.125 to 0.125
- adapter_down_weight: bfloat16 [4, 64, 8192, 128], P('section', 'tp'), may hold values from -0.0625 to 0.0625
- adapter_up_weight: bfloat16 [4, 64, 128, 8192], P('section', 'tp'), may hold values from -0.5 to 0.5
- forward_counts: int32 [4, 64], P('section'), may hold values from 1 to 32, 1024 in all within a row
- backward_counts: int32 [4, 64], P('section'), may hold values from 1 to 32, 1024 in all within a row
- ranks: int32 [64], replicated, may hold values from 16 to 128, as said below
- adapter_slot: int32 [64], replicated, may hold values from 0 to 63, each once
Outputs:
- next_fwd: bfloat16 [4, 1024, 8192], P('section', None, 'tp')
- next_bwd: bfloat16 [4, 1024, 8192], P('section', None, 'tp')
- grad_a: bfloat16 [4, 64, 8192, 128], P('section', 'tp')
- grad_b: bfloat16 [4, 64, 128, 8192], P('section', 'tp')
Inputs may be any that keep to these rules, and one draw needn't show every extreme that they name: `forward_counts`: each section's row sums to 1024; its largest entry is exactly 32. `backward_counts`: each section's row sums to 1024; its largest entry is exactly 32. `ranks`: some adapter has rank 128 and some other has the least rank. `adapter_slot`: A permutation: slot k of the adapter dimension lies on device k // 2 of tp.
All inputs are finite; a program needn't handle non-finite values.
Results may differ from a plain program's by a relative error of at most 0.005.
Values may be sent and summed in bfloat16 or wider, within the bound.
No kernel may reach another device: no remote copies, remote signals or barrier semaphores. Data moves between devices by JAX's collectives and lax.ppermute only.
A program may use at most 192 MiB of HBM per device.

v0:
```python
import jax
import jax.numpy as jnp
from jax import lax
from jax.sharding import PartitionSpec as P


def shifted(value, axis, steps):
    count = lax.axis_size(axis)
    pairs = [(source, (source + steps) % count) for source in range(count)]
    return lax.ppermute(value, axis, pairs)


def packing(counts, ranks, adapter_slot, tokens, window, largest_rank):
    adapters = adapter_slot.shape[0]
    lengths = counts[0]
    end_rows = jnp.cumsum(lengths)
    starts = end_rows - lengths
    token_ids = jnp.arange(tokens, dtype=jnp.int32)
    token_adapter = jnp.sum((end_rows[None, :] <= token_ids[:, None]).astype(jnp.int32), axis=1)
    begins = jnp.minimum(starts, tokens - window)
    adapter_ids = jnp.arange(adapters, dtype=jnp.int32)
    placed = (adapter_slot[:, None] == adapter_ids[None, :]).astype(jnp.int32)
    slot_begin = jnp.sum(placed * begins[:, None], axis=0)
    slot_start = jnp.sum(placed * starts[:, None], axis=0)
    slot_length = jnp.sum(placed * lengths[:, None], axis=0)
    slot_rank = jnp.sum(placed * ranks[:, None], axis=0)
    chosen = (token_adapter[:, None] == adapter_ids[None, :]).astype(jnp.int32)
    token_slot = jnp.sum(chosen * adapter_slot[None, :], axis=1)
    token_begin = jnp.sum(chosen * begins[None, :], axis=1)
    token_place = token_slot * window + token_ids - token_begin
    offsets = jnp.arange(window, dtype=jnp.int32)
    positions = slot_begin[:, None] + offsets[None, :]
    inside = (positions >= slot_start[:, None]) & (positions < (slot_start + slot_length)[:, None])
    rank_ids = jnp.arange(largest_rank, dtype=jnp.int32)
    alive = inside[:, :, None] & (rank_ids[None, None, :] < slot_rank[:, None, None])
    factor = 8.0 / jnp.sqrt(slot_rank.astype(jnp.float32))
    weights = jnp.where(alive, factor[:, None, None], jnp.zeros((), jnp.float32))
    return (positions.reshape(-1), token_slot, token_place, slot_begin, weights)


def shards(
    forward_inputs,
    backward_inputs,
    backward_cotangents,
    frozen_weight,
    adapter_down_weight,
    adapter_up_weight,
    forward_counts,
    backward_counts,
    ranks,
    adapter_slot,
):
    tokens = forward_inputs.shape[1]
    shard_cols = forward_inputs.shape[2]
    adapters = adapter_slot.shape[0]
    number_of_slots = adapter_down_weight.shape[1]
    largest_rank = adapter_down_weight.shape[3]
    window = 2 * tokens // adapters
    device = lax.axis_index("tp")
    first_slot = device * number_of_slots
    weight = frozen_weight[0]
    down_matrix = adapter_down_weight[0]
    up_matrix = adapter_up_weight[0]
    fwd_positions, fwd_token_slot, fwd_place, fwd_begin, fwd_weights = packing(
        forward_counts, ranks, adapter_slot, tokens, window, largest_rank
    )
    own_begin = lax.dynamic_slice_in_dim(fwd_begin, first_slot, number_of_slots)
    own_weights = lax.dynamic_slice_in_dim(fwd_weights, first_slot, number_of_slots, 0)
    layer_in = forward_inputs[0]

    def accumulate(shard_piece):
        base_out = jnp.dot(shard_piece, weight, preferred_element_type=jnp.float32)
        blocks = jnp.stack(
            [
                lax.dynamic_slice_in_dim(shard_piece, own_begin[slot_index], window, 0)
                for slot_index in range(number_of_slots)
            ]
        )
        code_sum = jnp.einsum(
            "kmn,knr->kmr", blocks, down_matrix, preferred_element_type=jnp.float32
        )
        return (base_out, code_sum)

    base_out, code_sum = accumulate(lax.all_gather(layer_in, "tp", axis=1, tiled=True))
    own_codes = (code_sum * own_weights).astype(jnp.bfloat16)
    local_index = jnp.clip(fwd_place - first_slot * window, 0, number_of_slots * window - 1)
    is_mine = fwd_token_slot // number_of_slots == device
    spread = jnp.take(
        own_codes.reshape(number_of_slots * window, largest_rank), local_index, axis=0
    ).astype(jnp.float32)
    spread = jnp.where(is_mine[:, None], spread, jnp.zeros((), jnp.float32))
    all_codes = lax.psum(spread.astype(jnp.bfloat16), "tp")
    up_columns = lax.all_to_all(up_matrix, "tp", split_axis=2, concat_axis=0, tiled=True)
    code_windows = jnp.take(all_codes, fwd_positions, axis=0).reshape(
        adapters, window, largest_rank
    )
    code_windows = jnp.where(fwd_weights > 0.0, code_windows, jnp.zeros_like(code_windows))
    adapter_windows = jnp.einsum(
        "amr,ard->amd", code_windows, up_columns, preferred_element_type=jnp.float32
    ).astype(jnp.bfloat16)
    adapter_rows = jnp.take(
        adapter_windows.reshape(adapters * window, shard_cols), fwd_place, axis=0
    )
    layer_out = (layer_in.astype(jnp.float32) + base_out + adapter_rows.astype(jnp.float32)).astype(
        jnp.bfloat16
    )
    next_fwd = shifted(layer_out, "section", 1)[None]
    bwd_positions, bwd_token_slot, bwd_place, bwd_begin, bwd_weights = packing(
        backward_counts, ranks, adapter_slot, tokens, window, largest_rank
    )
    own_bbegin = lax.dynamic_slice_in_dim(bwd_begin, first_slot, number_of_slots)
    own_bweights = lax.dynamic_slice_in_dim(bwd_weights, first_slot, number_of_slots, 0)
    stash = backward_inputs[0]
    cotangent = backward_cotangents[0]
    stash_windows = jnp.take(stash, bwd_positions, axis=0).reshape(adapters, window, shard_cols)
    grad_windows = jnp.take(cotangent, bwd_positions, axis=0).reshape(adapters, window, shard_cols)
    stash_rows, grad_rows = (
        lax.all_to_all(stash_windows, "tp", split_axis=0, concat_axis=2, tiled=True),
        lax.all_to_all(grad_windows, "tp", split_axis=0, concat_axis=2, tiled=True),
    )
    back_codes = (
        jnp.einsum("kmd,kdr->kmr", stash_rows, down_matrix, preferred_element_type=jnp.float32)
        * own_bweights
    ).astype(jnp.bfloat16)
    code_grads = (
        jnp.einsum("kmd,krd->kmr", grad_rows, up_matrix, preferred_element_type=jnp.float32)
        * own_bweights
    ).astype(jnp.bfloat16)
    grad_up = jnp.einsum(
        "kmr,kmd->krd", back_codes, grad_rows, preferred_element_type=jnp.float32
    ).astype(jnp.bfloat16)
    grad_down = jnp.einsum(
        "kmd,kmr->kdr", stash_rows, code_grads, preferred_element_type=jnp.float32
    ).astype(jnp.bfloat16)
    returned = jnp.einsum(
        "kmr,kdr->kmd", code_grads, down_matrix, preferred_element_type=jnp.float32
    )
    grad_down, grad_up, returned = (grad_down, grad_up, returned)
    partial_sum = lax.dot_general(
        cotangent, weight, (((1,), (1,)), ((), ())), preferred_element_type=jnp.float32
    )
    for slot_index in range(number_of_slots):
        current = lax.dynamic_slice_in_dim(partial_sum, own_bbegin[slot_index], window, 0)
        partial_sum = lax.dynamic_update_slice_in_dim(
            partial_sum, current + returned[slot_index], own_bbegin[slot_index], 0
        )
    input_grad = lax.psum_scatter(partial_sum, "tp", scatter_dimension=1, tiled=True)
    back_out = (cotangent.astype(jnp.float32) + input_grad).astype(jnp.bfloat16)
    next_bwd = shifted(back_out, "section", -1)[None]
    return (next_fwd, next_bwd, grad_down[None], grad_up[None])


def solution(mesh):
    placed = (
        P("section", None, "tp"),
        P("section", None, "tp"),
        P("section", None, "tp"),
        P("section", None, "tp"),
        P("section", "tp", None, None),
        P("section", "tp", None, None),
        P("section", None),
        P("section", None),
        P(),
        P(),
    )
    return jax.shard_map(
        shards,
        mesh=mesh,
        in_specs=placed,
        out_specs=(
            P("section", None, "tp"),
            P("section", None, "tp"),
            P("section", "tp", None, None),
            P("section", "tp", None, None),
        ),
        check_vma=False,
    )
```

profile of v0, /device:TPU:0, one launch (start us, length us, event | category | flops | bytes accessed | tf_op | source)
XLA Modules:
  0.0 437.5 jit_solution(1435310061422269580)
XLA Ops:
  7.2 0.7 all-gather.3.cloned.1.call-update
  7.9 0.7 copy.32
  8.8 0.1 reduce.2
  8.9 0.8 copy.29
  9.8 0.7 broadcast_minimum_fusion
  10.5 0.7 broadcast_minimum_fusion.1
  11.2 0.9 select_reduce_fusion.2
  12.2 7.5 %gather_fusion.4 = bf16[2048,256]{1,0:T(8,128)(2,1)S(1)} fusion(bf16[1024,256]{1,0:T(8,128)(2,1)S(1)} %bitcast.111, s32[2048]{0:T(1024)S(1)} %fusion.72), kind=kCustom, calls=%fused_computation.1.clone | custom fusion | bytes 2105344 | tf_op jit(solution)/shard_map/jit(_take)/gather | solution.py:115
  19.7 7.5 %gather_fusion.3 = bf16[2048,256]{1,0:T(8,128)(2,1)S(1)} fusion(bf16[1024,256]{1,0:T(8,128)(2,1)S(1)} %bitcast.113, s32[2048]{0:T(1024)S(1)} %fusion.72), kind=kCustom, calls=%fused_computation.clone | custom fusion | bytes 2105344 | tf_op jit(solution)/shard_map/jit(_take)/gather | solution.py:116
  27.2 1.5 broadcast_select_fusion
  28.8 8.3 %all-to-all-start.1 = ((bf16[64,32,256]{2,1,0:T(8,128)(2,1)}), bf16[64,32,256]{2,1,0:T(8,128)(2,1)S(1)}, u32[]{:S(2)}, u32[]{:S(2)}) async-start(bf16[64,32,256]{2,1,0:T(8,128)(2,1)} %bitcast.26), calls=%async_computation.1 | async-start | bytes 2097152 | tf_op jit(solution)/shard_map/all_to_all | solution.py:119
  37.2 0.6 fusion.85
  40.4 0.6 fusion.84
  43.7 11.2 %copy.30 = bf16[1,2,128,8192]{2,1,3,0:T(2,128)(2,1)} copy(bf16[1,2,128,8192]{3,2,1,0:T(8,128)(2,1)} %param.17) | data formatting | bytes 8388608 | tf_op args[5]
  58.0 0.1 select_reduce_fusion.1
  58.3 1.3 and_select_fusion
  59.7 16.7 %fusion.10 = f32[1024,8192]{1,0:T(8,128)} fusion(bf16[1,8192,256]{2,1,0:T(8,128)(2,1)} %param.15, bf16[1,1024,256]{2,1,0:T(8,128)(2,1)S(1)} %copy-done.2), kind=kOutput, calls=%fused_computation.17 | convolution fusion | flops 4294967296 | bytes 38273024 | tf_op jit(solution)/shard_map/dot_general | solution.py:139
  76.4 1.0 copy-done.5
  77.4 3.6 fusion.39
  81.0 1.5 fusion.6
  82.5 2.4 fusion.49
  85.0 4.6 %dynamic_update_slice.6 = f32[1024,8192]{1,0:T(8,128)} dynamic-update-slice(f32[1024,8192]{1,0:T(8,128)} %fusion.10, f32[32,8192]{1,0:T(8,128)} %fusion.49, s32[]{:T(128)S(6)} %select_n.126, s32[]{:T(128)} %constant.85.clone.1) | dynamic-update-slice | bytes 2097156 | tf_op jit(solution)/shard_map/dynamic_update_slice | solution.py:144
  89.6 11.7 %all-gather.3.cloned.1.call-done = bf16[1,1024,8192]{2,1,0:T(8,128)(2,1)} async-done(((bf16[1,1024,256]{2,1,0:T(8,128)(2,1)}), bf16[1,1024,8192]{2,1,0:T(8,128)(2,1)}) %all-gather.3.cloned.1.call-update) | async-done | bytes 16777232 | tf_op jit(solution)/shard_map/all_gather | solution.py:84
  101.3 1.6 constant_dynamic-slice_fusion.2
  102.9 3.0 fusion.45
  105.9 3.2 gather_fusion
  109.1 1.0 select_convert_fusion
  110.2 2.4 fusion.48
  112.7 4.3 dynamic_update_slice.7
  117.0 1.2 copy-done.4
  118.2 23.5 %all_to_all.54 = bf16[64,32,256]{2,1,0:T(8,128)(2,1)S(1)} all-to-all(bf16[64,32,256]{2,1,0:T(8,128)(2,1)S(1)} %bitcast.122), channel_id=1, replica_groups=mesh['section'=4,'tp'=32] {'tp'}, dimensions={0} | all-to-all | bytes 2097152 | tf_op jit(solution)/shard_map/all_to_all | solution.py:118
  141.7 5.0 %all-to-all-start = ((bf16[2,128,8192]{1,0,2:T(2,128)(2,1)}), bf16[2,128,8192]{1,0,2:T(2,128)(2,1)}, u32[]{:S(2)}, u32[]{:S(2)}) async-start(bf16[2,128,8192]{1,0,2:T(2,128)(2,1)} %bitcast.116), calls=%async_computation | async-start | bytes 8388608 | tf_op jit(solution)/shard_map/all_to_all | solution.py:93
  147.0 53.3 %all-to-all-done = bf16[2,128,8192]{1,0,2:T(2,128)(2,1)} async-done(((bf16[2,128,8192]{1,0,2:T(2,128)(2,1)}), bf16[2,128,8192]{1,0,2:T(2,128)(2,1)}, u32[]{:S(2)}, u32[]{:S(2)}) %all-to-all-start) | async-done | bytes 4194336 | tf_op jit(solution)/shard_map/all_to_all | solution.py:93
  200.2 11.0 %copy.31 = bf16[2,128,32,256]{3,1,0,2:T(8,128)(2,1)} copy(bf16[2,128,32,256]{1,0,3,2:T(2,128)(2,1)} %bitcast.16) | data formatting | bytes 8388608 | tf_op jit(solution)/shard_map/all_to_all | solution.py:93
  211.2 32.3 %all-reduce.2.cloned.1.call-done = bf16[1024,128]{1,0:T(8,128)(2,1)} async-done(((bf16[1024,128]{1,0:T(8,128)(2,1)}), bf16[1024,128]{1,0:T(8,128)(2,1)}) %all-reduce.2.cloned.1.call-update) | async-done | bytes 262160 | tf_op jit(solution)/shard_map/psum | solution.py:92
  243.5 6.6 %gather_fusion.1 = bf16[2048,128]{1,0:T(8,128)(2,1)S(1)} fusion(bf16[1024,128]{1,0:T(8,128)(2,1)} %all-reduce.2.cloned.1.call-done, s32[2048]{0:T(1024)S(1)} %broadcast_clamp_fusion), kind=kCustom, calls=%fused_computation.3 | custom fusion | bytes 1056768 | tf_op jit(solution)/shard_map/jit(_take)/gather | solution.py:94
  250.1 2.8 convolution_convert_fusion.2
  252.8 5.0 %gather_fusion.2 = bf16[1024,256]{1,0:T(8,128)(2,1)} fusion(bf16[2048,256]{1,0:T(8,128)(2,1)S(1)} %bitcast.114, s32[1024]{0:T(1024)S(1)} %broadcast_clamp_fusion.1), kind=kCustom, calls=%fused_computation.4 | custom fusion | bytes 1052672 | tf_op jit(solution)/shard_map/jit(_take)/gather | solution.py:101
  257.8 16.2 %fusion.25 = bf16[1024,256]{1,0:T(8,128)(2,1)} fusion(bf16[1,8192,256]{2,1,0:T(8,128)(2,1)} %param.15, bf16[1,1024,8192]{2,1,0:T(8,128)(2,1)} %all-gather.3.cloned.1.call-done, bf16[1,1024,256]{2,1,0:T(8,128)(2,1)S(1)} %copy-done.7, bf16[1024,256]{1,0:T(8,128)(2,1)} %gather_fusion.2, pred[1024]{0:T(1024)(128)(4,1)S(1)} %get-tuple-element.20), kind=kOutput, calls=%fused_computation.25 | convolution fusion | flops 4296540160 | bytes 22545408 | tf_op jit(solution)/shard_map/dot_general | solution.py:72
  274.0 1.6 collective-permute-start
  275.6 136.8 %reduce-scatter.2.cloned.1.call-done = f32[1024,256]{1,0:T(8,128)} async-done(((f32[1024,8192]{1,0:T(8,128)}), f32[1024,256]{1,0:T(8,128)}) %reduce-scatter.2.cloned.1.call-update) | async-done | bytes 1048592 | tf_op jit(solution)/shard_map/reduce_scatter | solution.py:147
  412.4 2.1 add_convert_fusion
  414.5 2.8 collective-permute-start.1
  417.3 3.7 fusion.2
  421.1 6.1 %fusion.3 = bf16[1,2,128,8192]{3,2,1,0:T(8,128)(2,1)} fusion(bf16[2,32,8192]{2,1,0:T(8,128)(2,1)S(1)} %bitcast.124, bf16[2,32,8192]{2,1,0:T(8,128)(2,1)S(1)} %bitcast.119, bf16[1,2,8192,128]{3,2,1,0:T(8,128)(2,1)} %param.16, f32[2]{0:T(128)S(1)} %dynamic-slice.4, pred[2,128]{1,0:T(4,128)(4,1)S(1)} %constant_dynamic-slice_fusion, ...), kind=kOutput, calls=%fused_computation.10 | convolution fusion | flops 270565376 | bytes 10486088 | tf_op jit(solution)/shard_map/kmr,kmd->krd/dot_general | solution.py:129
  427.1 1.2 collective-permute-done.1
  428.3 1.9 copy.49
  430.2 0.8 copy.50
  (55 shorter events, 1.6 us)
Async XLA Ops:
  7.2 5.0 %copy-start = (bf16[1,1024,256]{2,1,0:T(8,128)(2,1)S(1)}, bf16[1,1024,256]{2,1,0:T(8,128)(2,1)}, u32[]{:S(2)}) copy-start(bf16[1,1024,256]{2,1,0:T(8,128)(2,1)} %param.13) | copy-start | bytes 1572868
  7.2 94.1 %all-gather.3.cloned.1.call-start = ((), (), s32[]{:S(2)}) async-start(), calls=%async_computation.6 | async-start | bytes 17301504 | tf_op jit(solution)/shard_map/all_gather | solution.py:84
  12.2 7.5 %copy-start.2 = (bf16[1,1024,256]{2,1,0:T(8,128)(2,1)S(1)}, bf16[1,1024,256]{2,1,0:T(8,128)(2,1)}, u32[]{:S(2)}) copy-start(bf16[1,1024,256]{2,1,0:T(8,128)(2,1)} %param.14) | copy-start | bytes 1572868
  28.8 47.6 %all-to-all-start.1 = ((bf16[64,32,256]{2,1,0:T(8,128)(2,1)}), bf16[64,32,256]{2,1,0:T(8,128)(2,1)S(1)}, u32[]{:S(2)}, u32[]{:S(2)}) async-start(bf16[64,32,256]{2,1,0:T(8,128)(2,1)} %bitcast.26), calls=%async_computation.1 | async-start | bytes 2097152 | tf_op jit(solution)/shard_map/all_to_all | solution.py:119
  37.0 206.4 %all-reduce.2.cloned.1.call-start = ((), (), s32[]{:S(2)}) async-start(), calls=%async_computation.4 | async-start | bytes 524288 | tf_op jit(solution)/shard_map/psum | solution.py:92
  43.7 14.3 %copy-start.8 = (s32[1,64]{1,0:T(1,128)S(1)}, s32[1,64]{1,0:T(1,128)}, u32[]{:S(2)}) copy-start(s32[1,64]{1,0:T(1,128)} %param.18) | copy-start | bytes 772
  43.7 14.3 %copy-start.9 = (s32[64]{0:T(128)S(1)}, s32[64]{0:T(128)}, u32[]{:S(2)}) copy-start(s32[64]{0:T(128)} %param.21) | copy-start | bytes 772
  76.3 4.6 %copy-start.3 = (bf16[1,2,8192,128]{3,2,1,0:T(8,128)(2,1)S(1)}, bf16[1,2,8192,128]{3,2,1,0:T(8,128)(2,1)}, u32[]{:S(2)}) copy-start(bf16[1,2,8192,128]{3,2,1,0:T(8,128)(2,1)} %param.16) | copy-start | bytes 12582916
  76.4 1.0 copy-start.5
  110.2 302.2 %reduce-scatter.2.cloned.1.call-start = ((), (), s32[]{:S(2)}) async-start(), calls=%async_computation.5 | async-start | bytes 34603008 | tf_op jit(solution)/shard_map/reduce_scatter | solution.py:147
  117.0 1.2 copy-start.4
  141.7 58.5 %all-to-all-start = ((bf16[2,128,8192]{1,0,2:T(2,128)(2,1)}), bf16[2,128,8192]{1,0,2:T(2,128)(2,1)}, u32[]{:S(2)}, u32[]{:S(2)}) async-start(bf16[2,128,8192]{1,0,2:T(2,128)(2,1)} %bitcast.116), calls=%async_computation | async-start | bytes 8388608 | tf_op jit(solution)/shard_map/all_to_all | solution.py:93
  252.8 5.0 %copy-start.7 = (bf16[1,1024,256]{2,1,0:T(8,128)(2,1)S(1)}, bf16[1,1024,256]{2,1,0:T(8,128)(2,1)}, u32[]{:S(2)}) copy-start(bf16[1,1024,256]{2,1,0:T(8,128)(2,1)} %param.12) | copy-start | bytes 1572868
  274.0 147.1 %copy-start.6 = (bf16[32,2,4,8,256]{4,3,0,2,1:T(8,128)(2,1)S(1)}, bf16[32,2,4,8,256]{4,3,0,2,1:T(8,128)(2,1)}, u32[]{:S(2)}) copy-start(bf16[32,2,4,8,256]{4,3,0,2,1:T(8,128)(2,1)} %copy-done.5) | copy-start | bytes 3145732
  274.0 153.1 %collective-permute-start = (bf16[1024,256]{1,0:T(8,128)(2,1)}, bf16[1024,256]{1,0:T(8,128)(2,1)}, u32[]{:S(2)}, u32[]{:S(2)}) collective-permute-start(bf16[1024,256]{1,0:T(8,128)(2,1)} %fusion.25), channel_id=1, source_target_pairs={{0,32},{32,64},{64,96},{96,0},{1,33},{33,65},{65,97},{97,1},{2,34}... | collective-permute-start | bytes 1572872 | tf_op jit(solution)/shard_map/ppermute | solution.py:10
  414.5 13.8 %collective-permute-start.1 = (bf16[1024,256]{1,0:T(8,128)(2,1)}, bf16[1024,256]{1,0:T(8,128)(2,1)S(1)}, u32[]{:S(2)}, u32[]{:S(2)}) collective-permute-start(bf16[1024,256]{1,0:T(8,128)(2,1)} %add_convert_fusion), channel_id=1, source_target_pairs={{0,96},{32,0},{64,32},{96,64},{1,97},{33,1},{65,33},{97,65},{2,98}... | collective-permute-start | bytes 1572872 | tf_op jit(solution)/shard_map/ppermute | solution.py:10
  417.3 13.6 %copy-start.1 = (bf16[1,1024,256]{2,1,0:T(8,128)(2,1)S(1)}, bf16[1,1024,256]{2,1,0:T(8,128)(2,1)}, u32[]{:S(2)}) copy-start(bf16[1,1024,256]{2,1,0:T(8,128)(2,1)} %param.13) | copy-start | bytes 1572868
Sparse Core Ops, SparseCore 0:
  10.2 91.0 all-gather.2
  110.3 133.1 all-reduce.1
  247.9 164.4 reduce-scatter.1
where the time goes:
time: 440 us; the launch traced here: 437 us
  waiting for transfers between devices  236 us (54%)
  local copies, waits for them, and re-layouts  70.5 us (16%)
  matrix products  53.6 us (12%)
  blocking collectives  23.5 us (5%)
  between operations  22 us (5%)
  starting transfers between devices  17.8 us (4%)
  other arithmetic  14.1 us (3%)
    reduce_scatter x1, waiting for transfers between devices, shards(): lax.psum_scatter(partial_sum, 'tp', scatter_dimension=1, tiled=True)  137 us
    all_to_all x1, waiting for transfers between devices, shards(): lax.all_to_all(up_matrix, 'tp', split_axis=2, concat_axis=0, tiled=True)  53.3 us
    psum x1, waiting for transfers between devices, shards(): all_codes = lax.psum(spread.astype(jnp.bfloat16), 'tp')  32.3 us
    all_to_all x1, blocking collectives, shards(): lax.all_to_all(stash_windows, 'tp', split_axis=0, concat_axis=2, tiled=True)  23.5 us
    dot_general x1, matrix products, shards(): lax.dot_general(cotangent, weight, (((1,), (1,)), ((), ())), preferred_el...  16.7 us
    dot_general x1, matrix products, accumulate(): base_out = jnp.dot(shard_piece, weight, preferred_element_type=jnp.float32)  16.2 us
    unnamed x23, local copies, waits for them, and re-layouts  16 us
    all_gather x1, waiting for transfers between devices, shards(): lax.all_gather(layer_in, 'tp', axis=1, tiled=True)  11.7 us
  transfers between devices with their start and end apart: 7, of which 5 were waited for; matrix products, arithmetic and copies ran while one was open for 28% of the time, Pallas kernels for 0%

commit v1 on v0

v1 whole, which is shorter than its diff:
```python
import functools

import jax
import jax.numpy as jnp
from jax import lax
from jax.experimental import pallas as pl
from jax.experimental.pallas import tpu as pltpu
from jax.sharding import PartitionSpec as P

BF16 = jnp.bfloat16
F32 = jnp.float32
SIDE = 4
CHIPS = 16
CORES = 2
BLOCK = 256
VMEM = 56 * 1024 * 1024


def place(z, x, core):
    return (z * SIDE + x) * CORES + core


def ring_pairs(first, step):
    pairs = []
    for z in range(SIDE):
        for x in range(SIDE):
            for core in range(CORES):
                along_x = (core == 0) == first
                target = place(z, (x + step) % SIDE, core) if along_x else place((z + step) % SIDE, x, core)
                pairs.append((place(z, x, core), target))
    return pairs


FIRST_UP, FIRST_DOWN = ring_pairs(True, 1), ring_pairs(True, -1)
SECOND_UP, SECOND_DOWN = ring_pairs(False, 1), ring_pairs(False, -1)
OTHER_CORE = [(index, index ^ 1) for index in range(CHIPS * CORES)]
SAME_CORE = [[chip * CORES + core for chip in range(CHIPS)] for core in range(CORES)]


def send(value, pairs):
    return lax.ppermute(value, "tp", pairs)


def shifted(value, axis, steps):
    count = lax.axis_size(axis)
    pairs = [(source, (source + steps) % count) for source in range(count)]
    return lax.ppermute(value, axis, pairs)


def slots(counts, ranks, adapter_slot, window):
    adapters = adapter_slot.shape[0]
    lengths = counts[0]
    ids = jnp.arange(adapters, dtype=jnp.int32)
    starts = jnp.sum(jnp.where(ids[None, :] < ids[:, None], lengths[None, :], 0), axis=1)
    placed = adapter_slot[:, None] == ids[None, :]
    slot_start = jnp.sum(jnp.where(placed, starts[:, None], 0), axis=0)
    slot_length = jnp.sum(jnp.where(placed, lengths[:, None], 0), axis=0)
    slot_rank = jnp.sum(jnp.where(placed, ranks[:, None], 0), axis=0)
    offsets = jnp.arange(window, dtype=jnp.int32)
    token = jnp.where(offsets[None, :] < slot_length[:, None], slot_start[:, None] + offsets[None, :], -1)
    return token.reshape(-1), slot_rank


def forward_body(core_ref, x_ref, own_w_ref, other_w_ref, rows_ref, own_ref, other_ref, window_ref):
    step = pl.program_id(0)

    @pl.when(step == 0)
    def _():
        own_ref[...] = jnp.zeros_like(own_ref)
        other_ref[...] = jnp.zeros_like(other_ref)

    x = x_ref[0]
    own_ref[...] += jnp.dot(x, own_w_ref[0, 0], preferred_element_type=F32)
    other_ref[...] += jnp.dot(x, other_w_ref[0], preferred_element_type=F32)
    window_ref[0] = jnp.dot(rows_ref[...], x, preferred_element_type=F32).astype(BF16)


def forward_product(core, gathered, weight, other_weight, rows):
    tokens = gathered.shape[1]
    return pl.pallas_call(
        forward_body,
        grid_spec=pltpu.PrefetchScalarGridSpec(
            num_scalar_prefetch=1,
            grid=(CHIPS,),
            in_specs=[
                pl.BlockSpec((1, tokens, BLOCK), lambda k, core: (k, 0, 0)),
                pl.BlockSpec((1, 1, BLOCK, BLOCK), lambda k, core: (k, core[0], 0, 0)),
                pl.BlockSpec((1, BLOCK, BLOCK), lambda k, core: (k, 0, 0)),
                pl.BlockSpec(rows.shape, lambda k, core: (0, 0)),
            ],
            out_specs=[
                pl.BlockSpec((tokens, BLOCK), lambda k, core: (0, 0)),
                pl.BlockSpec((tokens, BLOCK), lambda k, core: (0, 0)),
                pl.BlockSpec((1, rows.shape[0], BLOCK), lambda k, core: (k, 0, 0)),
            ],
        ),
        out_shape=[
            jax.ShapeDtypeStruct((tokens, BLOCK), F32),
            jax.ShapeDtypeStruct((tokens, BLOCK), F32),
            jax.ShapeDtypeStruct((CHIPS, rows.shape[0], BLOCK), BF16),
        ],
        compiler_params=pltpu.CompilerParams(vmem_limit_bytes=VMEM),
        cost_estimate=pl.CostEstimate(flops=10 * 10**9, bytes_accessed=16 * 2**20, transcendentals=0),
        name="forward_product",
    )(core, gathered, weight, other_weight, rows)


def backward_body(takes, order_ref, own_g_ref, other_g_ref, own_w_ref, other_w_ref, spread_ref, returned_ref, *rest):
    received, out_ref = rest[:-1], rest[-1]
    step = pl.program_id(0)
    contract = (((1,), (1,)), ((), ()))
    total = lax.dot_general(own_g_ref[...], own_w_ref[0, 0], contract, preferred_element_type=F32)
    total += lax.dot_general(other_g_ref[...], other_w_ref[0], contract, preferred_element_type=F32)
    total += jnp.dot(spread_ref[...], returned_ref[0], preferred_element_type=F32)
    if not received:
        out_ref[0] = total.astype(BF16)
        return
    for ref, (low, high) in zip(received, takes):
        inside = (step >= low) & (step < high)
        total += jnp.where(inside, ref[0].astype(F32), 0.0)
    out_ref[0] = total.astype(BF16)


def backward_product(order, grads, weight, other_weight, spread, returned, received=(), takes=()):
    own_grad, other_grad = grads
    tokens = own_grad.shape[0]
    blocks = order.shape[0] - 1

    def taken(bounds):
        low, high = bounds
        return pl.BlockSpec((1, tokens, BLOCK), lambda j, order: (jnp.clip(j - low, 0, high - low - 1), 0, 0))

    whole = lambda shape: pl.BlockSpec(shape, lambda j, order: (0, 0))
    return pl.pallas_call(
        functools.partial(backward_body, takes),
        grid_spec=pltpu.PrefetchScalarGridSpec(
            num_scalar_prefetch=1,
            grid=(blocks,),
            in_specs=[
                whole((tokens, BLOCK)),
                whole((tokens, BLOCK)),
                pl.BlockSpec((1, 1, BLOCK, BLOCK), lambda j, order: (order[j], order[blocks], 0, 0)),
                pl.BlockSpec((1, BLOCK, BLOCK), lambda j, order: (order[j], 0, 0)),
                whole(spread.shape),
                pl.BlockSpec((1, returned.shape[1], BLOCK), lambda j, order: (order[j], 0, 0)),
            ]
            + [taken(bounds) for bounds in takes],
            out_specs=pl.BlockSpec((1, tokens, BLOCK), lambda j, order: (j, 0, 0)),
        ),
        out_shape=jax.ShapeDtypeStruct((blocks, tokens, BLOCK), BF16),
        compiler_params=pltpu.CompilerParams(vmem_limit_bytes=VMEM),
        cost_estimate=pl.CostEstimate(flops=blocks * 34 * 10**7, bytes_accessed=blocks * 2**20, transcendentals=0),
        name="backward_product",
    )(order, own_grad, other_grad, weight, other_weight, spread, returned, *received)


def add_rounded(*values):
    total = values[0].astype(F32)
    for value in values[1:]:
        total = total + value.astype(F32)
    return total.astype(BF16)


def shards(
    forward_inputs,
    backward_inputs,
    backward_cotangents,
    frozen_weight,
    adapter_down_weight,
    adapter_up_weight,
    forward_counts,
    backward_counts,
    ranks,
    adapter_slot,
):
    tokens = forward_inputs.shape[1]
    adapters = adapter_slot.shape[0]
    owned = adapter_down_weight.shape[1]
    rank = adapter_down_weight.shape[3]
    window = 2 * tokens // adapters
    rows = owned * window
    devices = CHIPS * CORES
    half = tokens // 2
    device = lax.axis_index("tp")
    core = device % CORES
    chip = device // CORES
    chip_z, chip_x = chip // SIDE, chip % SIDE

    layer_in = forward_inputs[0]
    stash = backward_inputs[0]
    cotangent = backward_cotangents[0]
    weight = frozen_weight[0].reshape(CHIPS, CORES, BLOCK, BLOCK)
    down = adapter_down_weight[0]
    up = adapter_up_weight[0]

    gathered = lax.all_gather(layer_in, "tp", axis=0, axis_index_groups=SAME_CORE)

    for_other = lax.dynamic_index_in_dim(weight, 1 - core, axis=1, keepdims=False)
    other_weight = send(for_other, OTHER_CORE)
    other_cotangent = send(cotangent, OTHER_CORE)

    fwd_token, slot_rank = slots(forward_counts, ranks, adapter_slot, window)
    bwd_token, _ = slots(backward_counts, ranks, adapter_slot, window)
    token_ids = jnp.arange(tokens, dtype=jnp.int32)
    own_rank = lax.dynamic_slice_in_dim(slot_rank, device * owned, owned)
    live = jnp.arange(rank, dtype=jnp.int32)[None, :] < own_rank[:, None]
    scale = jnp.where(live, 8.0 / jnp.sqrt(own_rank.astype(F32))[:, None], 0.0)[:, None, :]

    def of_chip(token):
        mine = lax.dynamic_slice_in_dim(token, device * rows, rows)
        other = lax.dynamic_slice_in_dim(token, (device ^ 1) * rows, rows)
        return jnp.concatenate([mine, other])

    pick = (bwd_token[:, None] == token_ids[None, :]).astype(BF16)
    both = jnp.concatenate([stash, cotangent], axis=1)
    windows = jnp.dot(pick, both, preferred_element_type=F32).astype(BF16)
    windows = windows.reshape(devices, rows, CORES * BLOCK)
    windows = lax.all_to_all(windows, "tp", split_axis=0, concat_axis=0, tiled=True)
    windows = windows.reshape(devices, owned, window, 2, BLOCK).transpose(3, 1, 2, 0, 4)
    windows = windows.reshape(2, owned, window, devices * BLOCK)
    stash_rows, grad_rows = windows[0], windows[1]

    back_codes = jnp.einsum("kmd,kdr->kmr", stash_rows, down, preferred_element_type=F32)
    back_codes = (back_codes * scale).astype(BF16)
    code_grads = jnp.einsum("kmd,krd->kmr", grad_rows, up, preferred_element_type=F32)
    code_grads = (code_grads * scale).astype(BF16)
    returned = jnp.einsum("kmr,kdr->kmd", code_grads, down, preferred_element_type=F32).astype(BF16)
    returned = returned.reshape(rows, CHIPS, CORES, BLOCK).transpose(2, 1, 0, 3)
    own_returned = lax.dynamic_index_in_dim(returned, core, axis=0, keepdims=False)
    other_returned = send(lax.dynamic_index_in_dim(returned, 1 - core, axis=0, keepdims=False), OTHER_CORE)
    returned = jnp.concatenate([own_returned, other_returned], axis=1)

    spread = (token_ids[:, None] == of_chip(bwd_token)[None, :]).astype(BF16)

    def block_at(second, first):
        z = jnp.where(core == 0, chip_z + second, chip_z + first) % SIDE
        x = jnp.where(core == 0, chip_x + first, chip_x + second) % SIDE
        return z * SIDE + x

    def partial_sums(second, firsts, received=(), takes=()):
        order = jnp.stack([block_at(second, first) for first in firsts] + [core]).astype(jnp.int32)
        grads = (cotangent, other_cotangent)
        return backward_product(order, grads, weight, other_weight, spread, returned, received, takes)

    firsts = (2, 1, 3, 0)
    far_up = send(partial_sums(2, firsts[:2]), SECOND_UP)
    far_down = send(partial_sums(2, firsts[2:]), SECOND_DOWN)
    near_up = send(partial_sums(1, firsts, (far_up,), ((0, 2),)), SECOND_UP)
    near_down = send(partial_sums(3, firsts, (far_down,), ((2, 4),)), SECOND_DOWN)
    sums = partial_sums(0, firsts, (near_up, near_down), ((0, 4), (0, 4)))
    far_up = send(sums[0, :half], FIRST_UP)
    far_down = send(sums[0, half:], FIRST_DOWN)
    near_up = jnp.concatenate([add_rounded(sums[1, :half], far_up), sums[1, half:]])
    near_down = jnp.concatenate([sums[2, :half], add_rounded(sums[2, half:], far_down)])
    near_up = send(near_up, FIRST_UP)
    near_down = send(near_down, FIRST_DOWN)
    back_out = add_rounded(cotangent, sums[3], near_up, near_down)
    next_bwd = shifted(back_out, "section", -1)[None]

    fwd_rows = (of_chip(fwd_token)[:, None] == token_ids[None, :]).astype(BF16)
    core_index = core.astype(jnp.int32).reshape(1)
    own_out, for_other_out, fwd_windows = forward_product(core_index, gathered, weight, other_weight, fwd_rows)
    other_out = send(for_other_out, OTHER_CORE)
    other_windows = send(fwd_windows[:, rows:], OTHER_CORE)
    own_windows = fwd_windows[:, :rows]
    low = jnp.where(core == 0, own_windows, other_windows)
    high = jnp.where(core == 0, other_windows, own_windows)
    fwd_windows = jnp.stack([low, high], axis=1).reshape(devices, owned, window, BLOCK)
    fwd_windows = fwd_windows.transpose(1, 2, 0, 3).reshape(owned, window, devices * BLOCK)
    codes = jnp.einsum("kmd,kdr->kmr", fwd_windows, down, preferred_element_type=F32)
    codes = (codes * scale).astype(BF16)
    adapter_out = jnp.einsum("kmr,krd->kmd", codes, up, preferred_element_type=F32).astype(BF16)
    adapter_out = adapter_out.reshape(rows, devices, BLOCK).transpose(1, 0, 2)
    adapter_out = lax.all_to_all(adapter_out, "tp", split_axis=0, concat_axis=0, tiled=True)
    put = (token_ids[:, None] == fwd_token[None, :]).astype(BF16)
    adapter_rows = jnp.dot(put, adapter_out.reshape(devices * rows, BLOCK), preferred_element_type=F32)
    layer_out = (layer_in.astype(F32) + (own_out + other_out) + adapter_rows).astype(BF16)
    next_fwd = shifted(layer_out, "section", 1)[None]

    grad_up = jnp.einsum("kmr,kmd->krd", back_codes, grad_rows, preferred_element_type=F32).astype(BF16)
    grad_down = jnp.einsum("kmd,kmr->kdr", stash_rows, code_grads, preferred_element_type=F32).astype(BF16)
    return (next_fwd, next_bwd, grad_down[None], grad_up[None])


def solution(mesh):
    placed = (
        P("section", None, "tp"),
        P("section", None, "tp"),
        P("section", None, "tp"),
        P("section", None, "tp"),
        P("section", "tp", None, None),
        P("section", "tp", None, None),
        P("section", None),
        P("section", None),
        P(),
        P(),
    )
    return jax.shard_map(
        shards,
        mesh=mesh,
        in_specs=placed,
        out_specs=(
            P("section", None, "tp"),
            P("section", None, "tp"),
            P("section", "tp", None, None),
            P("section", "tp", None, None),
        ),
        check_vma=False,
    )
```

time: 440 us -> 262 us (0.60)
  waiting for transfers between devices: 236 us -> 87.1 us
  Pallas kernels: 0 us -> 43.8 us
  local copies, waits for them, and re-layouts: 70.5 us -> 38.2 us
  matrix products: 53.6 us -> 28.8 us
  blocking collectives: 23.5 us -> 0 us
  starting transfers between devices: 17.8 us -> 33.1 us
  between operations: 22 us -> 14.5 us
    reduce_scatter x1 -> x0, waiting for transfers between devices: 137 us -> none  [shards(): lax.psum_scatter(partial_sum, 'tp', scatter_dimension=1, tiled=True)]
    ppermute x0 -> x13, waiting for transfers between devices: none -> 48.3 us  [send(): return lax.ppermute(value, 'tp', pairs)]
    pallas_call x0 -> x6, Pallas kernels: none -> 43.8 us  [the longest x5 28 us: backward_product(): pl.pallas_call(functools.partial(backward_body, takes), grid_spec=pltpu.P...]
    psum x1 -> x0, waiting for transfers between devices: 32.3 us -> none  [shards(): all_codes = lax.psum(spread.astype(jnp.bfloat16), 'tp')]
    gather x5 -> x0, local copies, waits for them, and re-layouts: 29.8 us -> none  [the longest x1 7.5 us: shards(): jnp.take(stash, bwd_positions, axis=0).reshape(adapters, window, shard_cols)]
    dot_general x6 -> x5, matrix products: 43.8 us -> 19 us  [the longest x1 4.78 us: shards(): windows = jnp.dot(pick, both, preferred_element_type=F32).astype(BF16)]
    all_to_all x1 -> x0, blocking collectives: 23.5 us -> none  [shards(): lax.all_to_all(stash_windows, 'tp', split_axis=0, concat_axis=2, tiled=True)]
    all_to_all x2, waiting for transfers between devices: 53.3 us -> 32.7 us  [the longest x1 32.7 us: shards(): lax.all_to_all(windows, 'tp', split_axis=0, concat_axis=0, tiled=True)]
  transfers between devices with their start and end apart: 7 -> 18, of which waited for: 5 -> 8; matrix products, arithmetic and copies ran while one was open for 28% -> 26% of each run, Pallas kernels for 0% -> 11%
where the time goes in v1:
time: 262 us; the launch traced here: 261 us
  waiting for transfers between devices  87.1 us (33%)
  Pallas kernels  43.8 us (17%)
  local copies, waits for them, and re-layouts  38.2 us (15%)
  starting transfers between devices  33.1 us (13%)
  matrix products  28.8 us (11%)
  other arithmetic  15.3 us (6%)
  between operations  14.5 us (6%)
    ppermute x13, waiting for transfers between devices, send(): return lax.ppermute(value, 'tp', pairs)  48.3 us
    all_to_all x1, waiting for transfers between devices, shards(): lax.all_to_all(windows, 'tp', split_axis=0, concat_axis=0, tiled=True)  32.7 us
    pallas_call x5, Pallas kernels, backward_product(): pl.pallas_call(functools.partial(backward_body, takes), grid_spec=pltpu.P...  28 us
    pallas_call x1, Pallas kernels, forward_product(): pl.pallas_call(forward_body, grid_spec=pltpu.PrefetchScalarGridSpec(num_s...  15.8 us
    ppermute x13, starting transfers between devices, send(): return lax.ppermute(value, 'tp', pairs)  13.3 us
    unnamed x37, local copies, waits for them, and re-layouts  10.2 us
    all_to_all x1, starting transfers between devices, shards(): lax.all_to_all(windows, 'tp', split_axis=0, concat_axis=0, tiled=True)  8.51 us
    all_to_all x1, starting transfers between devices, shards(): lax.all_to_all(adapter_out, 'tp', split_axis=0, concat_axis=0, tiled=True)  8.15 us
  transfers between devices with their start and end apart: 18, of which 8 were waited for; matrix products, arithmetic and copies ran while one was open for 26% of the time, Pallas kernels for 11%

profile of v1, /device:TPU:0, one launch (start us, length us, event | category | flops | bytes accessed | tf_op | source)
XLA Modules:
  0.0 260.8 jit_solution(16246104575834803541)
XLA Ops:
  10.5 4.8 %fusion.14 = bf16[2048,512]{1,0:T(8,128)(2,1)} fusion(s32[2048]{0:T(1024)S(1)} %select_n.348, bf16[1024,256]{1,0:T(8,128)(2,1)} %bitcast.134, bf16[1024,256]{1,0:T(8,128)(2,1)} %bitcast.152), kind=kOutput, calls=%fused_computation.20 | convolution fusion | flops 2152726528 | bytes 3153920 | tf_op jit(solution)/shard_map/dot_general | solution.py:216
  15.3 8.5 %all-to-all-start.1 = ((bf16[32,64,512]{2,1,0:T(8,128)(2,1)}), bf16[32,64,512]{2,1,0:T(8,128)(2,1)}, u32[]{:S(2)}, u32[]{:S(2)}) async-start(bf16[32,64,512]{2,1,0:T(8,128)(2,1)} %bitcast.21), calls=%async_computation.1 | async-start | bytes 4194304 | tf_op jit(solution)/shard_map/all_to_all | solution.py:218
  24.1 3.1 %dynamic-slice_bitcast_fusion = bf16[16,256,256]{2,1,0:T(8,128)(2,1)} fusion(bf16[16,2,256,256]{3,2,1,0:T(8,128)(2,1)} %bitcast.127, s32[]{:T(128)S(6)} %select_n.313), kind=kLoop, calls=%fused_computation.22 | loop fusion | bytes 4194308 | tf_op jit(solution)/shard_map/jit(dynamic_index_in_dim)/squeeze | solution.py:198
  27.6 32.7 %all-to-all-done.1 = bf16[32,64,512]{2,1,0:T(8,128)(2,1)} async-done(((bf16[32,64,512]{2,1,0:T(8,128)(2,1)}), bf16[32,64,512]{2,1,0:T(8,128)(2,1)}, u32[]{:S(2)}, u32[]{:S(2)}) %all-to-all-start.1) | async-done | bytes 2097184 | tf_op jit(solution)/shard_map/all_to_all | solution.py:218
  60.4 4.0 %reshape.165 = bf16[32,2,32,2,256]{4,3,2,1,0:T(2,128)(2,1)} reshape(bf16[32,64,512]{2,1,0:T(8,128)(2,1)} %all-to-all-done.1) | data formatting | bytes 4194304 | tf_op jit(solution)/shard_map/reshape | solution.py:219
  64.3 2.8 %copy.41 = bf16[32,2,32,2,256]{4,0,2,1,3:T(8,128)(2,1)S(1)} copy(bf16[32,2,32,2,256]{4,3,2,1,0:T(2,128)(2,1)} %reshape.165) | data formatting | bytes 4194304 | tf_op jit(solution)/shard_map/reshape | solution.py:219
  67.1 1.5 fusion.52
  68.6 2.3 squeeze.50
  70.9 4.2 %fusion.24 = bf16[2,32,128]{2,1,0:T(8,128)(2,1)S(1)} fusion(bf16[2,32,8192]{2,1,0:T(8,128)(2,1)} %squeeze.50, bf16[1,2,128,8192]{3,2,1,0:T(8,128)(2,1)} %param.15, f32[2,128]{1,0:T(2,128)S(1)} %compare_select_fusion), kind=kOutput, calls=%fused_computation.26 | convolution fusion | flops 134234112 | bytes 5260288 | tf_op jit(solution)/shard_map/kmd,krd->kmr/dot_general | solution.py:225
  75.1 2.5 convolution_convert_fusion.2
  77.6 2.6 %reshape.166 = bf16[64,16,2,256]{3,2,1,0:T(2,128)(2,1)} reshape(bf16[2,32,8192]{2,1,0:T(8,128)(2,1)} %convolution_convert_fusion.2) | data formatting | bytes 2097152 | tf_op jit(solution)/shard_map/reshape | solution.py:228
  80.2 5.4 %constant_dynamic-slice_fusion.1 = (bf16[64,16,1,256]{3,2,1,0:T(2,128)(2,1)}, bf16[64,16,1,256]{3,2,1,0:T(2,128)(2,1)S(1)}) fusion(bf16[64,16,2,256]{3,2,1,0:T(2,128)(2,1)} %reshape.166, s32[]{:T(128)S(6)} %select_n.349, s32[]{:T(128)S(6)} %select_n.313), kind=kLoop, calls=%fused_computation.80 | loop fusion | bytes 2097160 | tf_op jit(solution)/shard_map/dynamic-slice
  85.6 1.4 copy.43
  88.7 1.8 copy.44
  90.5 2.2 pad_maximum_fusion.1.returned_ref
  93.5 1.3 copy-done
  94.8 4.2 %backward_product.5 = bf16[2,1024,256]{2,1,0:T(8,128)(2,1)} custom-call(s32[3]{0:T(128)} %add_add_fusion.order_ref, bf16[1024,256]{1,0:T(8,128)(2,1)} %bitcast.135, bf16[1024,256]{1,0:T(8,128)(2,1)} %copy-done.4, bf16[16,2,256,256]{3,2,1,0:T(8,128)(2,1)} %bitcast.128, bf16[16,256,256]{2,1,0:T(8,128)(2,1)} %copy-done, bf16[1024,128]{1,0:T(8,128)(2,1)} %fusion.48.spread_ref, ...), custom_call_target="tpu_custom_call" | custom-call | flops 680000000 | bytes 2097152 | tf_op jit(solution)/shard_map/backward_product/pallas_call | solution.py:134
  99.6 4.2 %backward_product.7 = bf16[2,1024,256]{2,1,0:T(8,128)(2,1)} custom-call(s32[3]{0:T(128)} %add_add_fusion.1.order_ref, bf16[1024,256]{1,0:T(8,128)(2,1)} %bitcast.136, bf16[1024,256]{1,0:T(8,128)(2,1)} %copy-done.4, bf16[16,2,256,256]{3,2,1,0:T(8,128)(2,1)} %bitcast.129, bf16[16,256,256]{2,1,0:T(8,128)(2,1)} %copy-done, bf16[1024,128]{1,0:T(8,128)(2,1)} %fusion.48.spread_ref, ...), custom_call_target="tpu_custom_call" | custom-call | flops 680000000 | bytes 2097152 | tf_op jit(solution)/shard_map/backward_product/pallas_call | solution.py:134
  103.8 3.2 %collective-permute-start.8 = (bf16[2,1024,256]{2,1,0:T(8,128)(2,1)}, bf16[2,1024,256]{2,1,0:T(8,128)(2,1)S(1)}, u32[]{:S(2)}, u32[]{:S(2)}) collective-permute-start(bf16[2,1024,256]{2,1,0:T(8,128)(2,1)} %backward_product.7), channel_id=1, source_target_pairs={{0,24},{1,7},{2,26},{3,1},{4,28},{5,3},{6,30},{7,5},{8,0},{9,15},{... | collective-permute-start | bytes 3145736 | tf_op jit(solution)/shard_map/ppermute | solution.py:41
  108.2 7.0 %collective-permute-done.6.rest_0_ = bf16[2,1024,256]{2,1,0:T(8,128)(2,1)S(1)} collective-permute-done((bf16[2,1024,256]{2,1,0:T(8,128)(2,1)}, bf16[2,1024,256]{2,1,0:T(8,128)(2,1)S(1)}, u32[]{:S(2)}, u32[]{:S(2)}) %collective-permute-start.6) | collective-permute-done | bytes 1048608 | tf_op jit(solution)/shard_map/ppermute | solution.py:41
  115.2 1.0 copy-done.11
  116.2 6.2 %backward_product.6 = bf16[4,1024,256]{2,1,0:T(8,128)(2,1)} custom-call(s32[5]{0:T(128)} %stack.89.order_ref, bf16[1024,256]{1,0:T(8,128)(2,1)} %bitcast.137, bf16[1024,256]{1,0:T(8,128)(2,1)} %copy-done.4, bf16[16,2,256,256]{3,2,1,0:T(8,128)(2,1)} %bitcast.130, bf16[16,256,256]{2,1,0:T(8,128)(2,1)} %copy-done, bf16[1024,128]{1,0:T(8,128)(2,1)} %fusion.48.spread_ref, ...), custom_call_target="tpu_custom_call" | custom-call | flops 1360000000 | bytes 4194304 | tf_op jit(solution)/shard_map/backward_product/pallas_call | solution.py:134
  122.4 1.0 copy-done.10
  123.4 6.4 %backward_product.8 = bf16[4,1024,256]{2,1,0:T(8,128)(2,1)} custom-call(s32[5]{0:T(128)} %stack.97.order_ref, bf16[1024,256]{1,0:T(8,128)(2,1)} %bitcast.138, bf16[1024,256]{1,0:T(8,128)(2,1)} %copy-done.4, bf16[16,2,256,256]{3,2,1,0:T(8,128)(2,1)} %bitcast.131, bf16[16,256,256]{2,1,0:T(8,128)(2,1)} %copy-done, bf16[1024,128]{1,0:T(8,128)(2,1)} %fusion.48.spread_ref, ...), custom_call_target="tpu_custom_call" | custom-call | flops 1360000000 | bytes 4194304 | tf_op jit(solution)/shard_map/backward_product/pallas_call | solution.py:134
  129.8 3.2 %collective-permute-start.9 = (bf16[4,1024,256]{2,1,0:T(8,128)(2,1)}, bf16[4,1024,256]{2,1,0:T(8,128)(2,1)}, u32[]{:S(2)}, u32[]{:S(2)}) collective-permute-start(bf16[4,1024,256]{2,1,0:T(8,128)(2,1)} %backward_product.8), channel_id=1, source_target_pairs={{0,24},{1,7},{2,26},{3,1},{4,28},{5,3},{6,30},{7,5},{8,0},{9,15},{... | collective-permute-start | bytes 6291464 | tf_op jit(solution)/shard_map/ppermute | solution.py:41
  134.8 15.1 %collective-permute-done.7.rest_0_ = bf16[4,1024,256]{2,1,0:T(8,128)(2,1)S(1)} collective-permute-done((bf16[4,1024,256]{2,1,0:T(8,128)(2,1)}, bf16[4,1024,256]{2,1,0:T(8,128)(2,1)S(1)}, u32[]{:S(2)}, u32[]{:S(2)}) %collective-permute-start.7) | collective-permute-done | bytes 2097184 | tf_op jit(solution)/shard_map/ppermute | solution.py:41
  149.9 7.1 %collective-permute-done.9.rest_1_ = bf16[4,1024,256]{2,1,0:T(8,128)(2,1)} collective-permute-done((bf16[4,1024,256]{2,1,0:T(8,128)(2,1)}, bf16[4,1024,256]{2,1,0:T(8,128)(2,1)}, u32[]{:S(2)}, u32[]{:S(2)}) %collective-permute-start.9) | collective-permute-done | bytes 2097184 | tf_op jit(solution)/shard_map/ppermute | solution.py:41
  156.9 6.9 %backward_product.9 = bf16[4,1024,256]{2,1,0:T(8,128)(2,1)} custom-call(s32[5]{0:T(128)} %stack.84.order_ref, bf16[1024,256]{1,0:T(8,128)(2,1)} %bitcast.139, bf16[1024,256]{1,0:T(8,128)(2,1)} %copy-done.4, bf16[16,2,256,256]{3,2,1,0:T(8,128)(2,1)} %bitcast.132, bf16[16,256,256]{2,1,0:T(8,128)(2,1)} %copy-done, bf16[1024,128]{1,0:T(8,128)(2,1)} %fusion.48.spread_ref, ...), custom_call_target="tpu_custom_call" | custom-call | flops 1360000000 | bytes 4194304 | tf_op jit(solution)/shard_map/backward_product/pallas_call | solution.py:134
  163.9 15.8 %forward_product.1 = (f32[1024,256]{1,0:T(8,128)}, f32[1024,256]{1,0:T(8,128)}, bf16[16,128,256]{2,1,0:T(8,128)(2,1)}) custom-call(s32[1]{0:T(128)} %bitcast.1.core_ref, bf16[16,1024,256]{2,1,0:T(8,128)(2,1)} %all-gather.2.cloned.1.call-done.x_ref, bf16[16,2,256,256]{3,2,1,0:T(8,128)(2,1)} %bitcast.133, bf16[16,256,256]{2,1,0:T(8,128)(2,1)} %copy-done, ...), custom_call_target="tpu_custom_call" | custom-call | flops 10000000000 | bytes 16777216 | tf_op jit(solution)/shard_map/forward_product/pallas_call | solution.py:80
  179.7 1.2 slice.36
  180.9 0.9 slice_bitcast_fusion.5
  182.5 2.5 collective-permute-start.12
  185.1 4.3 %collective-permute-done.10 = bf16[512,256]{1,0:T(8,128)(2,1)S(1)} collective-permute-done((bf16[512,256]{1,0:T(8,128)(2,1)S(1)}, bf16[512,256]{1,0:T(8,128)(2,1)S(1)}, u32[]{:S(2)}, u32[]{:S(2)}) %collective-permute-start.10) | collective-permute-done | bytes 262176 | tf_op jit(solution)/shard_map/ppermute | solution.py:41
  190.6 4.8 %convolution_convert_fusion.3 = bf16[2,32,8192]{2,1,0:T(8,128)(2,1)S(1)} fusion(bf16[1,2,128,8192]{3,2,1,0:T(8,128)(2,1)} %param.15, bf16[2,32,8192]{2,1,0:T(8,128)(2,1)S(1)} %bitcast.144, bf16[1,2,8192,128]{3,2,1,0:T(8,128)(2,1)} %param.14, f32[2,128]{1,0:T(2,128)S(1)} %compare_select_fusion), kind=kOutput, calls=%fused_computation.5 | convolution fusion | flops 268976128 | bytes 10486784 | tf_op jit(solution)/shard_map/kmr,krd->kmd/dot_general | solution.py:272
  195.7 1.6 copy.42
  197.3 8.2 %all-to-all-start = ((bf16[32,64,256]{2,1,0:T(8,128)(2,1)}), bf16[32,64,256]{2,1,0:T(8,128)(2,1)}, u32[]{:S(2)}, u32[]{:S(2)}) async-start(bf16[32,64,256]{2,1,0:T(8,128)(2,1)} %bitcast.124), calls=%async_computation | async-start | bytes 2097152 | tf_op jit(solution)/shard_map/all_to_all | solution.py:274
  205.4 1.8 pad_maximum_fusion.3
  207.2 2.9 %collective-permute-start.13 = (bf16[1024,256]{1,0:T(8,128)(2,1)}, bf16[1024,256]{1,0:T(8,128)(2,1)}, u32[]{:S(2)}, u32[]{:S(2)}) collective-permute-start(bf16[1024,256]{1,0:T(8,128)(2,1)} %pad_maximum_fusion.3), channel_id=1, source_target_pairs={{0,6},{1,25},{2,0},{3,27},{4,2},{5,29},{6,4},{7,31},{8,14},{9,1},{... | collective-permute-start | bytes 1572872 | tf_op jit(solution)/shard_map/ppermute | solution.py:41
  211.5 13.6 %collective-permute-done.13 = bf16[1024,256]{1,0:T(8,128)(2,1)} collective-permute-done((bf16[1024,256]{1,0:T(8,128)(2,1)}, bf16[1024,256]{1,0:T(8,128)(2,1)}, u32[]{:S(2)}, u32[]{:S(2)}) %collective-permute-start.13) | collective-permute-done | bytes 524320 | tf_op jit(solution)/shard_map/ppermute | solution.py:41
  225.1 1.1 collective-permute-done.11
  226.2 1.5 fusion.38
  227.7 3.1 %collective-permute-start.14 = (bf16[1024,256]{1,0:T(8,128)(2,1)S(1)}, bf16[1024,256]{1,0:T(8,128)(2,1)S(1)}, u32[]{:S(2)}, u32[]{:S(2)}) collective-permute-start(bf16[1024,256]{1,0:T(8,128)(2,1)S(1)} %fusion.38), channel_id=1, source_target_pairs={{0,96},{32,0},{64,32},{96,64},{1,97},{33,1},{65,33},{97,65},{2,98}... | collective-permute-start | bytes 1572872 | tf_op jit(solution)/shard_map/ppermute | solution.py:47
  230.8 2.8 %fusion.2 = f32[1024,256]{1,0:T(8,128)S(1)} fusion(bf16[2048,256]{1,0:T(8,128)(2,1)} %bitcast.12, s32[2048]{0:T(1024)S(1)} %select_n.318), kind=kOutput, calls=%fused_computation.8 | convolution fusion | flops 1075838976 | bytes 2105344 | tf_op jit(solution)/shard_map/dot_general | solution.py:276
  233.6 2.5 fusion.40
  236.1 3.7 %fusion = bf16[1,2,8192,128]{3,2,1,0:T(8,128)(2,1)} fusion(bf16[2,32,8192]{2,1,0:T(8,128)(2,1)S(1)} %squeeze.57, bf16[2,32,128]{2,1,0:T(8,128)(2,1)S(1)} %fusion.24), kind=kOutput, calls=%fused_computation.2 | convolution fusion | flops 136314880 | bytes 5259264 | tf_op jit(solution)/shard_map/kmd,kmr->kdr/dot_general | solution.py:281
  239.8 6.0 %fusion.1 = bf16[1,2,128,8192]{3,2,1,0:T(8,128)(2,1)} fusion(bf16[2,32,8192]{2,1,0:T(8,128)(2,1)S(1)} %copy-done.5, bf16[2,32,8192]{2,1,0:T(8,128)(2,1)S(1)} %squeeze.57, bf16[1,2,8192,128]{3,2,1,0:T(8,128)(2,1)} %param.14, f32[2,128]{1,0:T(2,128)S(1)} %compare_select_fusion), kind=kOutput, calls=%fused_computation.3 | convolution fusion | flops 270548992 | bytes 10486784 | tf_op jit(solution)/shard_map/kmr,kmd->krd/dot_general | solution.py:280
  245.9 5.4 %collective-permute-done.3 = bf16[1024,256]{1,0:T(8,128)(2,1)} collective-permute-done((bf16[1024,256]{1,0:T(8,128)(2,1)}, bf16[1024,256]{1,0:T(8,128)(2,1)}, u32[]{:S(2)}, u32[]{:S(2)}) %collective-permute-start.3) | collective-permute-done | bytes 524320 | tf_op jit(solution)/shard_map/ppermute | solution.py:47
  251.3 1.9 copy.47
  (79 shorter events, 14.4 us)
Async XLA Ops:
  7.2 156.7 %all-gather.2.cloned.1.call-start = ((), (), s32[]{:S(2)}) async-start(), calls=%async_computation.2 | async-start | bytes 8912896 | tf_op jit(solution)/shard_map/all_gather | solution.py:196
  15.3 8.5 %copy-start.2 = (bf16[1,1024,256]{2,1,0:T(8,128)(2,1)S(1)}, bf16[1,1024,256]{2,1,0:T(8,128)(2,1)}, u32[]{:S(2)}) copy-start(bf16[1,1024,256]{2,1,0:T(8,128)(2,1)} %param.12) | copy-start | bytes 1572868
  15.3 45.1 %all-to-all-start.1 = ((bf16[32,64,512]{2,1,0:T(8,128)(2,1)}), bf16[32,64,512]{2,1,0:T(8,128)(2,1)}, u32[]{:S(2)}, u32[]{:S(2)}) async-start(bf16[32,64,512]{2,1,0:T(8,128)(2,1)} %bitcast.21), calls=%async_computation.1 | async-start | bytes 4194304 | tf_op jit(solution)/shard_map/all_to_all | solution.py:218
  23.8 68.9 %collective-permute-start.4 = (bf16[1024,256]{1,0:T(8,128)(2,1)S(1)}, bf16[1024,256]{1,0:T(8,128)(2,1)S(1)}, u32[]{:S(2)}, u32[]{:S(2)}) collective-permute-start(bf16[1024,256]{1,0:T(8,128)(2,1)S(1)} %bitcast.140), channel_id=1, source_target_pairs={{0,1},{1,0},{2,3},{3,2},{4,5},{5,4},{6,7},{7,6},{8,9},{9,8},{10,11... | collective-permute-start | bytes 1572872 | tf_op jit(solution)/shard_map/ppermute | solution.py:41
  27.2 65.5 %collective-permute-start = (bf16[16,256,256]{2,1,0:T(8,128)(2,1)}, bf16[16,256,256]{2,1,0:T(8,128)(2,1)S(1)}, u32[]{:S(2)}, u32[]{:S(2)}) collective-permute-start(bf16[16,256,256]{2,1,0:T(8,128)(2,1)} %dynamic-slice_bitcast_fusion), channel_id=1, source_target_pairs={{0,1},{1,0},{2,3},{3,2},{4,5},{5,4},{6,7},{7,6},{8,9},{9,8},{10,11... | collective-permute-start | bytes 6291464 | tf_op jit(solution)/shard_map/ppermute | solution.py:41
  70.9 4.2 %copy-start.1 = (bf16[1,2,8192,128]{3,2,1,0:T(8,128)(2,1)S(1)}, bf16[1,2,8192,128]{3,2,1,0:T(8,128)(2,1)}, u32[]{:S(2)}) copy-start(bf16[1,2,8192,128]{3,2,1,0:T(8,128)(2,1)} %param.14) | copy-start | bytes 12582916
  86.9 3.5 %collective-permute-start.5 = (bf16[16,64,256]{2,1,0:T(8,128)(2,1)}, bf16[16,64,256]{2,1,0:T(8,128)(2,1)}, u32[]{:S(2)}, u32[]{:S(2)}) collective-permute-start(bf16[16,64,256]{2,1,0:T(8,128)(2,1)} %bitcast.125), channel_id=1, source_target_pairs={{0,1},{1,0},{2,3},{3,2},{4,5},{5,4},{6,7},{7,6},{8,9},{9,8},{10,11... | collective-permute-start | bytes 1572872 | tf_op jit(solution)/shard_map/ppermute | solution.py:41
  92.7 0.8 copy-start.4
  93.5 1.3 copy-start
  99.0 16.2 %collective-permute-start.6 = (bf16[2,1024,256]{2,1,0:T(8,128)(2,1)}, bf16[2,1024,256]{2,1,0:T(8,128)(2,1)S(1)}, u32[]{:S(2)}, u32[]{:S(2)}) collective-permute-start(bf16[2,1024,256]{2,1,0:T(8,128)(2,1)} %backward_product.5), channel_id=1, source_target_pairs={{0,8},{1,3},{2,10},{3,5},{4,12},{5,7},{6,14},{7,1},{8,16},{9,11},{... | collective-permute-start | bytes 3145736 | tf_op jit(solution)/shard_map/ppermute | solution.py:41
  103.8 18.6 %collective-permute-start.8 = (bf16[2,1024,256]{2,1,0:T(8,128)(2,1)}, bf16[2,1024,256]{2,1,0:T(8,128)(2,1)S(1)}, u32[]{:S(2)}, u32[]{:S(2)}) collective-permute-start(bf16[2,1024,256]{2,1,0:T(8,128)(2,1)} %backward_product.7), channel_id=1, source_target_pairs={{0,24},{1,7},{2,26},{3,1},{4,28},{5,3},{6,30},{7,5},{8,0},{9,15},{... | collective-permute-start | bytes 3145736 | tf_op jit(solution)/shard_map/ppermute | solution.py:41
  115.2 1.0 copy-start.11
  122.4 27.5 %collective-permute-start.7 = (bf16[4,1024,256]{2,1,0:T(8,128)(2,1)}, bf16[4,1024,256]{2,1,0:T(8,128)(2,1)S(1)}, u32[]{:S(2)}, u32[]{:S(2)}) collective-permute-start(bf16[4,1024,256]{2,1,0:T(8,128)(2,1)} %backward_product.6), channel_id=1, source_target_pairs={{0,8},{1,3},{2,10},{3,5},{4,12},{5,7},{6,14},{7,1},{8,16},{9,11},{... | collective-permute-start | bytes 6291464 | tf_op jit(solution)/shard_map/ppermute | solution.py:41
  122.4 1.0 copy-start.10
  129.8 27.1 %collective-permute-start.9 = (bf16[4,1024,256]{2,1,0:T(8,128)(2,1)}, bf16[4,1024,256]{2,1,0:T(8,128)(2,1)}, u32[]{:S(2)}, u32[]{:S(2)}) collective-permute-start(bf16[4,1024,256]{2,1,0:T(8,128)(2,1)} %backward_product.8), channel_id=1, source_target_pairs={{0,24},{1,7},{2,26},{3,1},{4,28},{5,3},{6,30},{7,5},{8,0},{9,15},{... | collective-permute-start | bytes 6291464 | tf_op jit(solution)/shard_map/ppermute | solution.py:41
  149.9 7.1 %copy-start.8 = (bf16[4,1024,256]{2,1,0:T(8,128)(2,1)}, bf16[4,1024,256]{2,1,0:T(8,128)(2,1)S(1)}, u32[]{:S(2)}) copy-start(bf16[4,1024,256]{2,1,0:T(8,128)(2,1)S(1)} %collective-permute-done.7.rest_0_) | copy-start | bytes 6291460
  163.9 17.1 %copy-start.6 = (bf16[4,1024,256]{2,1,0:T(8,128)(2,1)S(1)}, bf16[4,1024,256]{2,1,0:T(8,128)(2,1)}, u32[]{:S(2)}) copy-start(bf16[4,1024,256]{2,1,0:T(8,128)(2,1)} %backward_product.9) | copy-start | bytes 6291460
  179.7 10.6 %copy-start.12 = (bf16[16,128,256]{2,1,0:T(8,128)(2,1)S(1)}, bf16[16,128,256]{2,1,0:T(8,128)(2,1)}, u32[]{:S(2)}) copy-start(bf16[16,128,256]{2,1,0:T(8,128)(2,1)} %get-tuple-element.9) | copy-start | bytes 3145732
  180.8 9.4 %collective-permute-start.2 = (bf16[16,64,256]{2,1,0:T(8,128)(2,1)S(1)}, bf16[16,64,256]{2,1,0:T(8,128)(2,1)S(1)}, u32[]{:S(2)}, u32[]{:S(2)}) collective-permute-start(bf16[16,64,256]{2,1,0:T(8,128)(2,1)S(1)} %slice.36), channel_id=1, source_target_pairs={{0,1},{1,0},{2,3},{3,2},{4,5},{5,4},{6,7},{7,6},{8,9},{9,8},{10,11... | collective-permute-start | bytes 1572872 | tf_op jit(solution)/shard_map/ppermute | solution.py:41
  181.8 7.6 %collective-permute-start.10 = (bf16[512,256]{1,0:T(8,128)(2,1)S(1)}, bf16[512,256]{1,0:T(8,128)(2,1)S(1)}, u32[]{:S(2)}, u32[]{:S(2)}) collective-permute-start(bf16[512,256]{1,0:T(8,128)(2,1)S(1)} %get-tuple-element.21), channel_id=1, source_target_pairs={{0,2},{1,9},{2,4},{3,11},{4,6},{5,13},{6,0},{7,15},{8,10},{9,17},{... | collective-permute-start | bytes 786440 | tf_op jit(solution)/shard_map/ppermute | solution.py:41
  182.5 6.9 %collective-permute-start.12 = (bf16[512,256]{1,0:T(8,128)(2,1)S(1)}, bf16[512,256]{1,0:T(8,128)(2,1)S(1)}, u32[]{:S(2)}, u32[]{:S(2)}) collective-permute-start(bf16[512,256]{1,0:T(8,128)(2,1)S(1)} %get-tuple-element.22), channel_id=1, source_target_pairs={{0,6},{1,25},{2,0},{3,27},{4,2},{5,29},{6,4},{7,31},{8,14},{9,1},{... | collective-permute-start | bytes 786440 | tf_op jit(solution)/shard_map/ppermute | solution.py:41
  195.4 10.0 %copy-start.14 = (bf16[512,256]{1,0:T(8,128)(2,1)S(1)}, bf16[512,256]{1,0:T(8,128)(2,1)}, u32[]{:S(2)}) copy-start(bf16[512,256]{1,0:T(8,128)(2,1)} %get-tuple-element.20) | copy-start | bytes 786436
  195.4 14.7 %copy-start.15 = (bf16[512,256]{1,0:T(8,128)(2,1)S(1)}, bf16[512,256]{1,0:T(8,128)(2,1)}, u32[]{:S(2)}) copy-start(bf16[512,256]{1,0:T(8,128)(2,1)} %get-tuple-element.24) | copy-start | bytes 786436
  195.4 15.6 %copy-start.7 = (bf16[1,2,32,32,256]{4,3,2,1,0:T(8,128)(2,1)S(1)}, bf16[1,2,32,32,256]{4,3,2,1,0:T(8,128)(2,1)}, u32[]{:S(2)}) copy-start(bf16[1,2,32,32,256]{4,3,2,1,0:T(8,128)(2,1)} %get-tuple-element.17) | copy-start | bytes 3145732
  195.7 30.6 %copy-start.3 = (bf16[1,1024,256]{2,1,0:T(8,128)(2,1)S(1)}, bf16[1,1024,256]{2,1,0:T(8,128)(2,1)}, u32[]{:S(2)}) copy-start(bf16[1,1024,256]{2,1,0:T(8,128)(2,1)} %param.12) | copy-start | bytes 1572868
  197.3 33.5 %all-to-all-start = ((bf16[32,64,256]{2,1,0:T(8,128)(2,1)}), bf16[32,64,256]{2,1,0:T(8,128)(2,1)}, u32[]{:S(2)}, u32[]{:S(2)}) async-start(bf16[32,64,256]{2,1,0:T(8,128)(2,1)} %bitcast.124), calls=%async_computation | async-start | bytes 2097152 | tf_op jit(solution)/shard_map/all_to_all | solution.py:274
  207.2 17.9 %collective-permute-start.13 = (bf16[1024,256]{1,0:T(8,128)(2,1)}, bf16[1024,256]{1,0:T(8,128)(2,1)}, u32[]{:S(2)}, u32[]{:S(2)}) collective-permute-start(bf16[1024,256]{1,0:T(8,128)(2,1)} %pad_maximum_fusion.3), channel_id=1, source_target_pairs={{0,6},{1,25},{2,0},{3,27},{4,2},{5,29},{6,4},{7,31},{8,14},{9,1},{... | collective-permute-start | bytes 1572872 | tf_op jit(solution)/shard_map/ppermute | solution.py:41
  211.0 15.3 %collective-permute-start.11 = (bf16[1024,256]{1,0:T(8,128)(2,1)}, bf16[1024,256]{1,0:T(8,128)(2,1)S(1)}, u32[]{:S(2)}, u32[]{:S(2)}) collective-permute-start(bf16[1024,256]{1,0:T(8,128)(2,1)} %pad_maximum_fusion.2), channel_id=1, source_target_pairs={{0,2},{1,9},{2,4},{3,11},{4,6},{5,13},{6,0},{7,15},{8,10},{9,17},{... | collective-permute-start | bytes 1572872 | tf_op jit(solution)/shard_map/ppermute | solution.py:41
  211.0 22.6 %collective-permute-start.1 = (f32[1024,256]{1,0:T(8,128)}, f32[1024,256]{1,0:T(8,128)}, u32[]{:S(2)}, u32[]{:S(2)}) collective-permute-start(f32[1024,256]{1,0:T(8,128)} %get-tuple-element.8), channel_id=1, source_target_pairs={{0,1},{1,0},{2,3},{3,2},{4,5},{5,4},{6,7},{7,6},{8,9},{9,8},{10,11... | collective-permute-start | bytes 3145736 | tf_op jit(solution)/shard_map/ppermute | solution.py:41
  227.7 18.2 %collective-permute-start.14 = (bf16[1024,256]{1,0:T(8,128)(2,1)S(1)}, bf16[1024,256]{1,0:T(8,128)(2,1)S(1)}, u32[]{:S(2)}, u32[]{:S(2)}) collective-permute-start(bf16[1024,256]{1,0:T(8,128)(2,1)S(1)} %fusion.38), channel_id=1, source_target_pairs={{0,96},{32,0},{64,32},{96,64},{1,97},{33,1},{65,33},{97,65},{2,98}... | collective-permute-start | bytes 1572872 | tf_op jit(solution)/shard_map/ppermute | solution.py:47
  230.8 2.8 %copy-start.9 = (bf16[1,1024,256]{2,1,0:T(8,128)(2,1)S(1)}, bf16[1,1024,256]{2,1,0:T(8,128)(2,1)}, u32[]{:S(2)}) copy-start(bf16[1,1024,256]{2,1,0:T(8,128)(2,1)} %param.10) | copy-start | bytes 1572868
  230.8 2.8 %copy-start.13 = (f32[1024,256]{1,0:T(8,128)S(1)}, f32[1024,256]{1,0:T(8,128)}, u32[]{:S(2)}) copy-start(f32[1024,256]{1,0:T(8,128)} %get-tuple-element.7) | copy-start | bytes 3145732
  233.6 6.2 %copy-start.5 = (bf16[2,32,8192]{2,1,0:T(8,128)(2,1)S(1)}, bf16[2,32,8192]{2,1,0:T(8,128)(2,1)}, u32[]{:S(2)}) copy-start(bf16[2,32,8192]{2,1,0:T(8,128)(2,1)} %squeeze.50) | copy-start | bytes 3145732
  236.1 15.2 %collective-permute-start.3 = (bf16[1024,256]{1,0:T(8,128)(2,1)}, bf16[1024,256]{1,0:T(8,128)(2,1)}, u32[]{:S(2)}, u32[]{:S(2)}) collective-permute-start(bf16[1024,256]{1,0:T(8,128)(2,1)} %fusion.40), channel_id=1, source_target_pairs={{0,32},{32,64},{64,96},{96,0},{1,33},{33,65},{65,97},{97,1},{2,34}... | collective-permute-start | bytes 1572872 | tf_op jit(solution)/shard_map/ppermute | solution.py:47
Sparse Core Ops, SparseCore 0:
  10.1 93.5 all-gather.1

commit v2 on v1

v2 whole, which is shorter than its diff:
```python
import functools
import math

import jax
import jax.numpy as jnp
from jax import lax
from jax.experimental import pallas as pl
from jax.experimental.pallas import tpu as pltpu
from jax.sharding import PartitionSpec as P

BF16 = jnp.bfloat16
F32 = jnp.float32
SIDE = 4
CHIPS = 16
CORES = 2
BLOCK = 256
SUBLANES = 8
VMEM = 16 * 1024 * 1024


def place(z, x, core):
    return (z * SIDE + x) * CORES + core


def ring_pairs(first, step):
    pairs = []
    for z in range(SIDE):
        for x in range(SIDE):
            for core in range(CORES):
                along_x = (core == 0) == first
                target = place(z, (x + step) % SIDE, core) if along_x else place((z + step) % SIDE, x, core)
                pairs.append((place(z, x, core), target))
    return pairs


FIRST_UP, FIRST_DOWN = ring_pairs(True, 1), ring_pairs(True, -1)
SECOND_UP, SECOND_DOWN = ring_pairs(False, 1), ring_pairs(False, -1)
OTHER_CORE = [(index, index ^ 1) for index in range(CHIPS * CORES)]


def send(value, pairs):
    return lax.ppermute(value, "tp", pairs)


def shifted(value, axis, steps):
    count = lax.axis_size(axis)
    pairs = [(source, (source + steps) % count) for source in range(count)]
    return lax.ppermute(value, axis, pairs)


def whole(shape):
    return pl.BlockSpec(shape, lambda *_: (0,) * len(shape))


def kernel(body, name, grid, prefetched, in_specs, outs, flops, scratch=()):
    out_shape = [jax.ShapeDtypeStruct(shape, dtype) for _, shape, dtype in outs]
    size = sum(2 * math.prod(shape) for _, shape, _ in outs)
    return pl.pallas_call(
        body,
        grid_spec=pltpu.PrefetchScalarGridSpec(
            num_scalar_prefetch=prefetched,
            grid=grid,
            in_specs=in_specs,
            out_specs=[spec for spec, _, _ in outs],
            scratch_shapes=list(scratch),
        ),
        out_shape=out_shape,
        compiler_params=pltpu.CompilerParams(vmem_limit_bytes=VMEM),
        cost_estimate=pl.CostEstimate(flops=flops, bytes_accessed=2 * size, transcendentals=0),
        name=name,
    )


def slots_body(fwd_ref, bwd_ref, ranks_ref, slot_ref, info_ref):
    adapters = slot_ref.shape[0]

    def step(adapter, starts):
        slot = slot_ref[adapter]
        fwd, bwd = fwd_ref[adapter], bwd_ref[adapter]
        for row, value in enumerate((starts[0], fwd, starts[1], bwd, ranks_ref[adapter])):
            info_ref[row * adapters + slot] = value
        return starts[0] + fwd, starts[1] + bwd

    zero = jnp.int32(0)
    lax.fori_loop(0, adapters, step, (zero, zero))


def slots(forward_counts, backward_counts, ranks, adapter_slot):
    adapters = adapter_slot.shape[0]
    scalars = pl.BlockSpec(memory_space=pltpu.SMEM)
    return pl.pallas_call(
        slots_body,
        in_specs=[scalars] * 4,
        out_specs=scalars,
        out_shape=jax.ShapeDtypeStruct((5 * adapters,), jnp.int32),
        name="slots",
    )(forward_counts[0], backward_counts[0], ranks, adapter_slot)


def slot_rows(ref, start, length, window):
    past = lax.rem(start, SUBLANES)
    size = window + SUBLANES
    rows = ref[pl.ds(pl.multiple_of(start - past, SUBLANES), size), :]
    rows = pltpu.roll(rows, lax.rem(size - past, size), 0)[:window]
    held = lax.broadcasted_iota(jnp.int32, rows.shape, 0) < length
    return jnp.where(held, rows, 0.0).astype(BF16)


def windows_body(adapters, window, each, info_ref, stash_ref, cotangent_ref, out_ref, wide_ref):
    tokens = stash_ref.shape[0]
    step = pl.program_id(0)
    owned = out_ref.shape[1] // window

    @pl.when(step == 0)
    def _():
        wide_ref[:tokens, :BLOCK] = stash_ref[...].astype(F32)
        wide_ref[:tokens, BLOCK:] = cotangent_ref[...].astype(F32)

    for index in range(each):
        slot = step * each + index
        rows = slot_rows(wide_ref, info_ref[2 * adapters + slot], info_ref[3 * adapters + slot], window)
        low = index % owned * window
        out_ref[index // owned, low : low + window] = rows


def windows_of(info, stash, cotangent, adapters, window, rows):
    devices = adapters * window // rows
    tokens = stash.shape[0]
    each = 16
    owners = each * window // rows
    out = pl.BlockSpec((owners, rows, 2 * BLOCK), lambda i, info: (i, 0, 0))
    return kernel(
        functools.partial(windows_body, adapters, window, each),
        "windows",
        (adapters // each,),
        1,
        [whole(stash.shape), whole(cotangent.shape)],
        [(out, (devices, rows, 2 * BLOCK), BF16)],
        2 * 10**9,
        [pltpu.VMEM((tokens + window + SUBLANES, 2 * BLOCK), F32)],
    )(info, stash, cotangent)[0]


NT = (((1,), (1,)), ((), ()))
TN = (((0,), (0,)), ((), ()))
GROUP = 8


def lanes(ref, *index):
    return jnp.concatenate([ref[(slot,) + index] for slot in range(ref.shape[0])], axis=1)


def codes_body(windows_ref, down_ref, up_ref, scale_ref, codes_ref, grads_ref, code_sum, grad_sum):
    step = pl.program_id(0)

    @pl.when(step == 0)
    def _():
        code_sum[...] = jnp.zeros_like(code_sum)
        grad_sum[...] = jnp.zeros_like(grad_sum)

    stash = jnp.concatenate([windows_ref[s, :, :BLOCK] for s in range(GROUP)], axis=1)
    grad = jnp.concatenate([windows_ref[s, :, BLOCK:] for s in range(GROUP)], axis=1)
    up = up_ref[...].reshape(-1, up_ref.shape[2])
    code_sum[...] += jnp.dot(stash, lanes(down_ref), preferred_element_type=F32)
    grad_sum[...] += lax.dot_general(grad, up, NT, preferred_element_type=F32)

    @pl.when(step == pl.num_programs(0) - 1)
    def _():
        codes_ref[...] = (code_sum[...] * scale_ref[...]).astype(BF16)
        grads_ref[...] = (grad_sum[...] * scale_ref[...]).astype(BF16)


def codes_of(windows, down, up, scale):
    devices, rows, _ = windows.shape
    owned, _, rank = down.shape
    shape = scale.shape
    return kernel(
        codes_body,
        "codes",
        (devices // GROUP,),
        0,
        [
            pl.BlockSpec((GROUP, rows, 2 * BLOCK), lambda i: (i, 0, 0)),
            pl.BlockSpec((owned, GROUP * BLOCK, rank), lambda i: (0, i, 0)),
            pl.BlockSpec((owned, rank, GROUP * BLOCK), lambda i: (0, 0, i)),
            whole(shape),
        ],
        [(whole(shape), shape, BF16)] * 2,
        2 * 10**9,
        [pltpu.VMEM(shape, F32)] * 2,
    )(windows, down, up, scale)


def halves(down):
    owned, _, rank = down.shape
    view = down.reshape(owned, CHIPS, CORES, BLOCK, rank)
    shape = (owned, GROUP, 1, BLOCK, rank)
    own = pl.BlockSpec(shape, lambda i, core: (0, i, core[0], 0, 0))
    other = pl.BlockSpec(shape, lambda i, core: (0, i, 1 - core[0], 0, 0))
    return view, own, other


def returned_body(core_ref, grads_ref, own_down_ref, other_down_ref, own_ref, other_ref):
    grads = grads_ref[...]
    for down_ref, out_ref in ((other_down_ref, other_ref), (own_down_ref, own_ref)):
        for index in range(GROUP):
            part = lax.dot_general(grads, lanes(down_ref, index, 0), NT, preferred_element_type=F32)
            out_ref[index] = part.astype(BF16)


def returned_of(core, code_grads, down):
    rows = code_grads.shape[0]
    view, own, other = halves(down)
    out = pl.BlockSpec((GROUP, rows, BLOCK), lambda i, core: (i, 0, 0))
    return kernel(
        returned_body,
        "returned",
        (CHIPS // GROUP,),
        1,
        [whole(code_grads.shape), own, other],
        [(out, (CHIPS, rows, BLOCK), BF16)] * 2,
        10**9,
    )(core, code_grads, view, view)


def forward_codes_body(core_ref, own_x_ref, other_x_ref, own_down_ref, other_down_ref, scale_ref, codes_ref, code_sum):
    step = pl.program_id(0)

    @pl.when(step == 0)
    def _():
        code_sum[...] = jnp.zeros_like(code_sum)

    for x_ref, down_ref in ((own_x_ref, own_down_ref), (other_x_ref, other_down_ref)):
        x = jnp.concatenate([x_ref[s] for s in range(GROUP)], axis=1)
        matrix = jnp.concatenate([lanes(down_ref, s, 0) for s in range(GROUP)], axis=0)
        code_sum[...] += jnp.dot(x, matrix, preferred_element_type=F32)

    @pl.when(step == pl.num_programs(0) - 1)
    def _():
        codes_ref[...] = (code_sum[...] * scale_ref[...]).astype(BF16)


def forward_codes_of(core, own_windows, other_windows, down, scale):
    rows = own_windows.shape[1]
    view, own, other = halves(down)
    x = pl.BlockSpec((GROUP, rows, BLOCK), lambda i, core: (i, 0, 0))
    shape = scale.shape
    return kernel(
        forward_codes_body,
        "forward_codes",
        (CHIPS // GROUP,),
        1,
        [x, x, own, other, whole(shape)],
        [(whole(shape), shape, BF16)],
        10**9,
        [pltpu.VMEM(shape, F32)],
    )(core, own_windows, other_windows, view, view, scale)[0]


def adapter_body(codes_ref, up_ref, out_ref):
    up = up_ref[...].reshape(-1, up_ref.shape[2])
    part = jnp.dot(codes_ref[...], up, preferred_element_type=F32).astype(BF16)
    for index in range(out_ref.shape[0]):
        out_ref[index] = part[:, index * BLOCK : (index + 1) * BLOCK]


def adapter_rows_of(codes, up, devices):
    rows = codes.shape[0]
    owned, rank, _ = up.shape
    group = GROUP
    out = pl.BlockSpec((group, rows, BLOCK), lambda i: (i, 0, 0))
    return kernel(
        adapter_body,
        "adapter_rows",
        (devices // group,),
        0,
        [whole(codes.shape), pl.BlockSpec((owned, rank, group * BLOCK), lambda i: (0, 0, i))],
        [(out, (devices, rows, BLOCK), BF16)],
        10**9,
    )(codes, up)[0]


def gradients_body(windows_ref, codes_ref, grads_ref, down_ref, up_ref):
    owned, _, rank = down_ref.shape
    for s in range(GROUP):
        span = slice(s * BLOCK, (s + 1) * BLOCK)
        stash, grad = windows_ref[s, :, :BLOCK], windows_ref[s, :, BLOCK:]
        down = lax.dot_general(stash, grads_ref[...], TN, preferred_element_type=F32).astype(BF16)
        up = lax.dot_general(codes_ref[...], grad, TN, preferred_element_type=F32).astype(BF16)
        for slot in range(owned):
            own = slice(slot * rank, (slot + 1) * rank)
            down_ref[slot, span] = down[:, own]
            up_ref[slot, :, span] = up[own]


def gradients_of(windows, back_codes, code_grads, owned):
    devices, rows, _ = windows.shape
    rank = back_codes.shape[1] // owned
    width = devices * BLOCK
    return kernel(
        gradients_body,
        "gradients",
        (devices // GROUP,),
        0,
        [
            pl.BlockSpec((GROUP, rows, 2 * BLOCK), lambda i: (i, 0, 0)),
            whole(back_codes.shape),
            whole(code_grads.shape),
        ],
        [
            (pl.BlockSpec((owned, GROUP * BLOCK, rank), lambda i: (0, i, 0)), (owned, width, rank), BF16),
            (pl.BlockSpec((owned, rank, GROUP * BLOCK), lambda i: (0, 0, i)), (owned, rank, width), BF16),
        ],
        2 * 10**9,
    )(windows, back_codes, code_grads)


PAIR = 2


def forward_body(window, order_ref, info_ref, *rest):
    pieces, rest = rest[:13], rest[13:]
    own_w, other_w, rest = rest[:PAIR], rest[PAIR : 2 * PAIR], rest[2 * PAIR :]
    own_ref, other_ref, own_x_ref, other_x_ref, wide_ref = rest
    step = pl.program_id(0)
    tokens = own_ref.shape[0]
    core = order_ref[CHIPS]
    chip = order_ref[CHIPS + 1]
    adapters = info_ref.shape[0] // 5
    owned = own_x_ref.shape[1] // window

    @pl.when(step == 0)
    def _():
        own_ref[...] = jnp.zeros_like(own_ref)
        other_ref[...] = jnp.zeros_like(other_ref)

    def take(*blocks):
        own_sum, other_sum = own_ref[...], other_ref[...]
        for index, (x_ref, at) in enumerate(blocks):
            x = x_ref[...] if at is None else x_ref[at]
            own_sum += jnp.dot(x, own_w[index][0, 0], preferred_element_type=F32)
            other_sum += jnp.dot(x, other_w[index][0], preferred_element_type=F32)
            wide_ref[:tokens] = x.astype(F32)
            at = order_ref[PAIR * step + index]
            for whose, out_ref in ((core, own_x_ref), (1 - core, other_x_ref)):
                for slot in range(owned):
                    place_of = (chip * CORES + whose) * owned + slot
                    rows = slot_rows(wide_ref, info_ref[place_of], info_ref[adapters + place_of], window)
                    out_ref[at, slot * window : (slot + 1) * window] = rows
        own_ref[...] = own_sum
        other_ref[...] = other_sum

    own, far, near = pieces[0:9:3], pieces[1:9:3], pieces[2:9:3]
    pairs = []
    for line in range(3):
        pairs += [((own[line], None), (far[line], None)), ((near[line], 0), (near[line], 1))]
    pairs += [((pieces[9], None), (pieces[10], None)), ((pieces[11], None), (pieces[12], None))]
    for index, pair in enumerate(pairs):
        pl.when(step == index)(functools.partial(take, *pair))


def forward_product(order, info, pieces, weight, other_weight, window, rows):
    tokens = pieces[0].shape[0]
    product = (whole((tokens, BLOCK)), (tokens, BLOCK), F32)
    windows = (whole((CHIPS, rows, BLOCK)), (CHIPS, rows, BLOCK), BF16)

    def own(index):
        shape = (1, 1, BLOCK, BLOCK)
        return pl.BlockSpec(shape, lambda k, order, info: (order[PAIR * k + index], order[CHIPS], 0, 0))

    def other(index):
        return pl.BlockSpec((1, BLOCK, BLOCK), lambda k, order, info: (order[PAIR * k + index], 0, 0))

    return kernel(
        functools.partial(forward_body, window),
        "forward_product",
        (CHIPS // PAIR,),
        2,
        [whole(piece.shape) for piece in pieces]
        + [own(index) for index in range(PAIR)]
        + [other(index) for index in range(PAIR)],
        [product, product, windows, windows],
        9 * 10**9,
        [pltpu.VMEM((tokens + window + SUBLANES, BLOCK), F32)],
    )(order, info, *pieces, *[weight] * PAIR, *[other_weight] * PAIR)


def backward_body(takes, order_ref, grad_ref, own_w_ref, other_w_ref, spread_ref, own_ret_ref, other_ret_ref, *rest):
    received, out_ref = rest[:-1], rest[-1]
    step = pl.program_id(0)
    matrix = jnp.concatenate([own_w_ref[0, 0], other_w_ref[0]], axis=1)
    returned = jnp.concatenate([own_ret_ref[0], other_ret_ref[0]], axis=0)
    tile = 2 * BLOCK
    for low in range(0, grad_ref.shape[0], tile):
        span = slice(low, low + tile)
        total = lax.dot_general(grad_ref[span], matrix, NT, preferred_element_type=F32)
        total += jnp.dot(spread_ref[span], returned, preferred_element_type=F32)
        for ref, (first, last) in zip(received, takes):
            inside = (step >= first) & (step < last)
            total += jnp.where(inside, ref[0, span].astype(F32), 0.0)
        out_ref[0, span] = total.astype(BF16)


def backward_product(order, base, blocks, grads, weight, other_weight, spread, returned, received=(), takes=()):
    tokens = grads.shape[0]
    core_at = CHIPS

    def taken(bounds):
        first, last = bounds
        return pl.BlockSpec((1, tokens, BLOCK), lambda j, order: (jnp.clip(j - first, 0, last - first - 1), 0, 0))

    rows = pl.BlockSpec((1,) + returned[0].shape[1:], lambda j, order: (order[base + j], 0, 0))
    out = pl.BlockSpec((1, tokens, BLOCK), lambda j, order: (j, 0, 0))
    return kernel(
        functools.partial(backward_body, takes),
        "backward_product",
        (blocks,),
        1,
        [
            whole(grads.shape),
            pl.BlockSpec((1, 1, BLOCK, BLOCK), lambda j, order: (order[base + j], order[core_at], 0, 0)),
            pl.BlockSpec((1, BLOCK, BLOCK), lambda j, order: (order[base + j], 0, 0)),
            whole(spread.shape),
            rows,
            rows,
        ]
        + [taken(bounds) for bounds in takes],
        [(out, (blocks, tokens, BLOCK), BF16)],
        blocks * 34 * 10**7,
    )(order, grads, weight, other_weight, spread, *returned, *received)[0]


def add_rounded(*values):
    total = values[0].astype(F32)
    for value in values[1:]:
        total = total + value.astype(F32)
    return total.astype(BF16)


def shards(
    forward_inputs,
    backward_inputs,
    backward_cotangents,
    frozen_weight,
    adapter_down_weight,
    adapter_up_weight,
    forward_counts,
    backward_counts,
    ranks,
    adapter_slot,
):
    tokens = forward_inputs.shape[1]
    adapters = adapter_slot.shape[0]
    owned = adapter_down_weight.shape[1]
    rank = adapter_down_weight.shape[3]
    window = 2 * tokens // adapters
    rows = owned * window
    devices = CHIPS * CORES
    half = tokens // 2
    device = lax.axis_index("tp")
    core = device % CORES
    chip = device // CORES
    chip_z, chip_x = chip // SIDE, chip % SIDE

    layer_in = forward_inputs[0]
    stash = backward_inputs[0]
    cotangent = backward_cotangents[0]
    weight = frozen_weight[0].reshape(CHIPS, CORES, BLOCK, BLOCK)
    down = adapter_down_weight[0]
    up = adapter_up_weight[0]

    below, above = send(layer_in, FIRST_UP), send(layer_in, FIRST_DOWN)
    own_below, own_above = send(layer_in, SECOND_UP), send(layer_in, SECOND_DOWN)
    far_low, far_high = send(below[:half], FIRST_UP), send(above[half:], FIRST_DOWN)
    own_far = send(own_below, SECOND_UP)
    near = jnp.stack([below, above])
    near_below, near_above = send(near, SECOND_UP), send(near, SECOND_DOWN)
    far = jnp.concatenate([far_low, far_high])
    far_below, far_above = send(far, SECOND_UP), send(far, SECOND_DOWN)
    below_far, above_far = send(near_below[0], SECOND_UP), send(near_above[1], SECOND_DOWN)
    far_far = send(far_above, SECOND_DOWN)
    pieces = (layer_in, far, near, own_below, far_below, near_below, own_above, far_above, near_above)
    pieces += (own_far, far_far, below_far, above_far)

    for_other = lax.dynamic_index_in_dim(weight, 1 - core, axis=1, keepdims=False)
    other_weight = send(for_other, OTHER_CORE)
    other_cotangent = send(cotangent, OTHER_CORE)

    info = slots(forward_counts, backward_counts, ranks, adapter_slot)
    windows = windows_of(info, stash, cotangent, adapters, window, rows)
    windows = lax.all_to_all(windows, "tp", split_axis=0, concat_axis=0, tiled=True)

    starts = info.reshape(5, adapters)
    offsets = jnp.arange(window, dtype=jnp.int32)
    token_ids = jnp.arange(tokens, dtype=jnp.int32)

    def tokens_of(start, length):
        token = jnp.where(offsets[None, :] < length[:, None], start[:, None] + offsets[None, :], -1)
        return token.reshape(-1)

    def of_chip(token):
        mine = lax.dynamic_slice_in_dim(token, device * rows, rows)
        other = lax.dynamic_slice_in_dim(token, (device ^ 1) * rows, rows)
        return jnp.concatenate([mine, other])

    fwd_token = tokens_of(starts[0], starts[1])
    bwd_token = tokens_of(starts[2], starts[3])
    own_rank = lax.dynamic_slice_in_dim(starts[4], device * owned, owned)
    column = jnp.arange(owned * rank, dtype=jnp.int32)
    row = jnp.arange(rows, dtype=jnp.int32)
    factor = jnp.repeat(8.0 / jnp.sqrt(own_rank.astype(F32)), rank)
    live = column % rank < jnp.repeat(own_rank, rank)
    mine = row[:, None] // window == column[None, :] // rank
    scale = jnp.where(mine & live[None, :], factor[None, :], 0.0)
    spread = (token_ids[:, None] == of_chip(bwd_token)[None, :]).astype(BF16)
    put = (token_ids[:, None] == fwd_token[None, :]).astype(BF16)
    core_index = core.astype(jnp.int32).reshape(1)

    def chips(pairs):
        second, first = (jnp.array(list(offsets), jnp.int32) for offsets in zip(*pairs))
        z = jnp.where(core == 0, chip_z + second, chip_z + first) % SIDE
        x = jnp.where(core == 0, chip_x + first, chip_x + second) % SIDE
        return jnp.concatenate([z * SIDE + x, core.reshape(1), chip.reshape(1)]).astype(jnp.int32)

    order = chips([(s, f) for s in (2, 1, 3, 0) for f in (2, 1, 3, 0)])
    arrivals = chips([(s, f) for s in (0, 3, 1, 2) for f in (0, 2, 3, 1)])
    grads = jnp.concatenate([cotangent, other_cotangent], axis=1)

    ready = (windows, scale, spread, grads, order, arrivals)
    windows, scale, spread, grads, order, arrivals = lax.optimization_barrier(ready)
    back_codes, code_grads = codes_of(windows, down, up, scale)
    own_returned, for_other = returned_of(core_index, code_grads, down)
    returned = (own_returned, send(for_other, OTHER_CORE))

    def partial_sums(base, blocks, received=(), takes=(), grads=grads):
        return backward_product(order, base, blocks, grads, weight, other_weight, spread, returned, received, takes)

    far_up = send(partial_sums(0, 2), SECOND_UP)
    far_down = send(partial_sums(2, 2), SECOND_DOWN)
    own_out, for_other_out, own_x, for_other_x = forward_product(
        arrivals, info, pieces, weight, other_weight, window, rows
    )
    other_x = send(for_other_x, OTHER_CORE)
    other_out = send(for_other_out, OTHER_CORE)

    later_grads, _ = lax.optimization_barrier((grads, own_out))
    near_up = send(partial_sums(4, 4, (far_up,), ((0, 2),), later_grads), SECOND_UP)
    near_down = send(partial_sums(8, 4, (far_down,), ((2, 4),), later_grads), SECOND_DOWN)

    codes = forward_codes_of(core_index, own_x, other_x, down, scale)
    adapter_out = adapter_rows_of(codes, up, devices)
    later_grads, _ = lax.optimization_barrier((grads, adapter_out))
    sums = partial_sums(12, 4, (near_up, near_down), ((0, 4), (0, 4)), later_grads)
    far_up = send(sums[0, :half], FIRST_UP)
    far_down = send(sums[0, half:], FIRST_DOWN)
    near_up = jnp.concatenate([add_rounded(sums[1, :half], far_up), sums[1, half:]])
    near_down = jnp.concatenate([sums[2, :half], add_rounded(sums[2, half:], far_down)])
    near_up = send(near_up, FIRST_UP)
    near_down = send(near_down, FIRST_DOWN)
    back_out = add_rounded(cotangent, sums[3], near_up, near_down)
    next_bwd = shifted(back_out, "section", -1)[None]

    adapter_out = lax.all_to_all(adapter_out, "tp", split_axis=0, concat_axis=0, tiled=True)
    adapter_rows = jnp.dot(put, adapter_out.reshape(devices * rows, BLOCK), preferred_element_type=F32)
    layer_out = (layer_in.astype(F32) + (own_out + other_out) + adapter_rows).astype(BF16)
    next_fwd = shifted(layer_out, "section", 1)[None]

    grad_down, grad_up = gradients_of(windows, back_codes, code_grads, owned)
    return (next_fwd, next_bwd, grad_down[None], grad_up[None])


def solution(mesh):
    placed = (
        P("section", None, "tp"),
        P("section", None, "tp"),
        P("section", None, "tp"),
        P("section", None, "tp"),
        P("section", "tp", None, None),
        P("section", "tp", None, None),
        P("section", None),
        P("section", None),
        P(),
        P(),
    )
    return jax.shard_map(
        shards,
        mesh=mesh,
        in_specs=placed,
        out_specs=(
            P("section", None, "tp"),
            P("section", None, "tp"),
            P("section", "tp", None, None),
            P("section", "tp", None, None),
        ),
        check_vma=False,
    )
```

time: 262 us -> 199 us (0.76)
  matrix products: 28.8 us -> 2.77 us
  waiting for transfers between devices: 87.1 us -> 62.1 us
  starting transfers between devices: 33.1 us -> 50.9 us
  between operations: 14.5 us -> 1.1 us
  local copies, waits for them, and re-layouts: 38.2 us -> 24.9 us
  other arithmetic: 15.3 us -> 9.04 us
  Pallas kernels: 43.8 us -> 46.9 us
    all_to_all x1, waiting for transfers between devices: 32.7 us -> 0.01 us  [shards(): lax.all_to_all(windows, 'tp', split_axis=0, concat_axis=0, tiled=True)]
    dot_general x6 -> x0, matrix products: 26 us -> none  [the longest x1 6.05 us: shards(): jnp.einsum('kmr,kmd->krd', back_codes, grad_rows, preferred_element_type=...]
    ppermute x13 -> x27, starting transfers between devices: 13.3 us -> 34.7 us  [send(): return lax.ppermute(value, 'tp', pairs)]
    ppermute x13 -> x27, waiting for transfers between devices: 48.3 us -> 61.6 us  [send(): return lax.ppermute(value, 'tp', pairs)]
    reshape x5 -> x0, local copies, waits for them, and re-layouts: 11 us -> none  [the longest x2 6.72 us: shards(): windows.reshape(devices, owned, window, 2, BLOCK).transpose(3, 1, 2, 0, 4)]
    unnamed x37 -> x53, local copies, waits for them, and re-layouts: 10.2 us -> 17.9 us
    another operation x5 -> x0, local copies, waits for them, and re-layouts: 7.31 us -> none
    ppermute x2, waiting for transfers between devices: 5.39 us -> 0.44 us  [shifted(): return lax.ppermute(value, axis, pairs)]
  transfers between devices with their start and end apart: 18 -> 31, of which waited for: 8 -> 10; matrix products, arithmetic and copies ran while one was open for 26% -> 10% of each run, Pallas kernels for 11% -> 24%
where the time goes in v2:
time: 199 us; the launch traced here: 198 us
  waiting for transfers between devices  62.1 us (31%)
  starting transfers between devices  50.9 us (26%)
  Pallas kernels  46.9 us (24%)
  local copies, waits for them, and re-layouts  24.9 us (13%)
  other arithmetic  9.04 us (5%)
  matrix products  2.77 us (1%)
    ppermute x27, waiting for transfers between devices, send(): return lax.ppermute(value, 'tp', pairs)  61.6 us
    ppermute x27, starting transfers between devices, send(): return lax.ppermute(value, 'tp', pairs)  34.7 us
    unnamed x53, local copies, waits for them, and re-layouts  17.9 us
    pallas_call x5, Pallas kernels, backward_product(): kernel(functools.partial(backward_body, takes), 'backward_product', (bloc...  15.9 us
    pallas_call x1, Pallas kernels, forward_product(): kernel(functools.partial(forward_body, window), 'forward_product', (CHIPS...  10.7 us
    all_to_all x1, starting transfers between devices, shards(): lax.all_to_all(windows, 'tp', split_axis=0, concat_axis=0, tiled=True)  6.76 us
    pallas_call x1, Pallas kernels, gradients_of(): kernel(gradients_body, 'gradients', (devices // GROUP,), 0, [pl.BlockSpec...  6.54 us
    ppermute x2, starting transfers between devices, shifted(): return lax.ppermute(value, axis, pairs)  4.72 us
  transfers between devices with their start and end apart: 31, of which 10 were waited for; matrix products, arithmetic and copies ran while one was open for 10% of the time, Pallas kernels for 24%

profile of v2, /device:TPU:0, one launch (start us, length us, event | category | flops | bytes accessed | tf_op | source)
XLA Modules:
  0.0 197.6 jit_solution(5212218660433634872)
XLA Ops:
  0.6 1.6 collective-permute-start.1
  2.3 1.7 collective-permute-start.3
  4.5 1.7 slots.1.info_ref
  9.0 3.2 %windows.1 = bf16[32,64,512]{2,1,0:T(8,128)(2,1)} custom-call(s32[320]{0:T(512)S(1)} %copy-done.15, bf16[1024,256]{1,0:T(8,128)(2,1)S(1)} %bitcast.72, bf16[1024,256]{1,0:T(8,128)(2,1)S(1)} %bitcast.71), custom_call_target="tpu_custom_call" | custom-call | flops 2000000000 | bytes 4194304 | tf_op jit(solution)/shard_map/windows/pallas_call | solution.py:132
  12.2 6.8 %all-to-all-start = ((bf16[32,64,512]{2,1,0:T(8,128)(2,1)}), bf16[32,64,512]{2,1,0:T(8,128)(2,1)}, u32[]{:S(2)}, u32[]{:S(2)}) async-start(bf16[32,64,512]{2,1,0:T(8,128)(2,1)} %windows.1), calls=%async_computation | async-start | bytes 4194304 | tf_op jit(solution)/shard_map/all_to_all | solution.py:491
  19.0 3.1 %dynamic-slice_bitcast_fusion = bf16[16,256,256]{2,1,0:T(8,128)(2,1)} fusion(bf16[16,2,256,256]{3,2,1,0:T(8,128)(2,1)} %bitcast.54, s32[]{:T(128)S(6)} %select_n.143), kind=kLoop, calls=%fused_computation.3 | loop fusion | bytes 4194308 | tf_op jit(solution)/shard_map/jit(dynamic_index_in_dim)/squeeze | solution.py:485
  24.8 1.7 collective-permute-start.7
  26.5 1.6 collective-permute-start.10
  28.1 1.7 collective-permute-start.2
  29.9 1.6 collective-permute-start.4
  31.6 19.7 %collective-permute-done.2 = bf16[512,256]{1,0:T(8,128)(2,1)S(1)} collective-permute-done((bf16[512,256]{1,0:T(8,128)(2,1)S(1)}, bf16[512,256]{1,0:T(8,128)(2,1)S(1)}, u32[]{:S(2)}, u32[]{:S(2)}) %collective-permute-start.2) | collective-permute-done | bytes 262176 | tf_op jit(solution)/shard_map/ppermute | solution.py:42
  51.3 1.5 collective-permute-start.5
  54.8 1.8 collective-permute-start.8
  57.3 2.2 %copy-done.2 = bf16[1,2,8192,128]{3,2,1,0:T(8,128)(2,1)S(1)} copy-done((bf16[1,2,8192,128]{3,2,1,0:T(8,128)(2,1)S(1)}, bf16[1,2,8192,128]{3,2,1,0:T(8,128)(2,1)}, u32[]{:S(2)}) %copy-start.2) | copy-done | bytes 4194328
  59.5 2.2 %copy-done.3 = bf16[1,2,128,8192]{3,2,1,0:T(8,128)(2,1)S(1)} copy-done((bf16[1,2,128,8192]{3,2,1,0:T(8,128)(2,1)S(1)}, bf16[1,2,128,8192]{3,2,1,0:T(8,128)(2,1)}, u32[]{:S(2)}) %copy-start.3) | copy-done | bytes 4194328
  61.7 4.2 %codes.1 = (bf16[64,256]{1,0:T(8,128)(2,1)S(1)}, bf16[64,256]{1,0:T(8,128)(2,1)S(1)}) custom-call(bf16[32,64,512]{2,1,0:T(8,128)(2,1)} %all-to-all-done.windows_ref, bf16[2,8192,128]{2,1,0:T(8,128)(2,1)S(1)} %bitcast.62, bf16[2,128,8192]{2,1,0:T(8,128)(2,1)S(1)} %bitcast.67, f32[64,256]{1,0:T(8,128)S(1)} %and_select_fusion.scale_ref), custom_call_target="tpu_custom_call" | custom-call | flops 2000000000 | bytes 131072 | tf_op jit(solution)/shard_map/codes/pallas_call | solution.py:177
  65.9 1.6 collective-permute-start.9
  67.5 1.8 returned.1
  73.5 1.8 collective-permute-done.9.rest_7_
  75.3 2.7 %collective-permute-start.12 = (bf16[1024,256]{1,0:T(8,128)(2,1)S(1)}, bf16[1024,256]{1,0:T(8,128)(2,1)S(1)}, u32[]{:S(2)}, u32[]{:S(2)}) collective-permute-start(bf16[1024,256]{1,0:T(8,128)(2,1)S(1)} %collective-permute-done.9.rest_7_), channel_id=1, source_target_pairs={{0,24},{1,7},{2,26},{3,1},{4,28},{5,3},{6,30},{7,5},{8,0},{9,15},{... | collective-permute-start | bytes 1572872 | tf_op jit(solution)/shard_map/ppermute | solution.py:42
  78.1 3.2 %collective-permute-start.14 = (bf16[1024,256]{1,0:T(8,128)(2,1)S(1)}, bf16[1024,256]{1,0:T(8,128)(2,1)S(1)}, u32[]{:S(2)}, u32[]{:S(2)}) collective-permute-start(bf16[1024,256]{1,0:T(8,128)(2,1)S(1)} %slice_bitcast_fusion.1), channel_id=1, source_target_pairs={{0,24},{1,7},{2,26},{3,1},{4,28},{5,3},{6,30},{7,5},{8,0},{9,15},{... | collective-permute-start | bytes 1572872 | tf_op jit(solution)/shard_map/ppermute | solution.py:42
  81.3 1.7 backward_product.5
  83.1 1.7 backward_product.7
  84.8 2.1 %collective-permute-done.6.rest_4_ = bf16[1024,256]{1,0:T(8,128)(2,1)S(1)} collective-permute-done((bf16[1024,256]{1,0:T(8,128)(2,1)}, bf16[1024,256]{1,0:T(8,128)(2,1)S(1)}, u32[]{:S(2)}, u32[]{:S(2)}) %collective-permute-start.6) | collective-permute-done | bytes 524320 | tf_op jit(solution)/shard_map/ppermute | solution.py:42
  86.9 1.4 collective-permute-start.22
  88.3 4.2 %collective-permute-done.13.rest_11_ = bf16[1024,256]{1,0:T(8,128)(2,1)S(1)} collective-permute-done((bf16[1024,256]{1,0:T(8,128)(2,1)S(1)}, bf16[1024,256]{1,0:T(8,128)(2,1)S(1)}, u32[]{:S(2)}, u32[]{:S(2)}) %collective-permute-start.13) | collective-permute-done | bytes 524320 | tf_op jit(solution)/shard_map/ppermute | solution.py:42
  92.5 10.7 %forward_product.1 = (f32[1024,256]{1,0:T(8,128)S(1)}, f32[1024,256]{1,0:T(8,128)S(1)}, bf16[16,64,256]{2,1,0:T(8,128)(2,1)S(1)}, bf16[16,64,256]{2,1,0:T(8,128)(2,1)S(1)}) custom-call(s32[18]{0:T(128)S(1)} %get-tuple-element.22.order_ref, s32[320]{0:T(512)S(1)} %copy-done.16, bf16[1024,256]{1,0:T(8,128)(2,1)} %bitcast.rest_0_, ...), custom_call_target="tpu_custom_call" | custom-call | flops 8999999488 | bytes 4194304 | tf_op jit(solution)/shard_map/forward_product/pallas_call | solution.py:374
  104.2 3.8 %backward_product.6 = bf16[4,1024,256]{2,1,0:T(8,128)(2,1)} custom-call(s32[18]{0:T(128)S(1)} %get-tuple-element.28.order_ref, bf16[1024,512]{1,0:T(8,128)(2,1)S(1)} %pad_maximum_fusion.grad_ref, bf16[16,2,256,256]{3,2,1,0:T(8,128)(2,1)S(1)} %bitcast.59, bf16[16,256,256]{2,1,0:T(8,128)(2,1)S(1)} %collective-permute-done.15.rest_15_.rest_16_.other_w_ref, ...), custom_call_target="tpu_custom_call" | custom-call | flops 1360000000 | bytes 4194304 | tf_op jit(solution)/shard_map/backward_product/pallas_call | solution.py:414
  108.1 3.8 %backward_product.8 = bf16[4,1024,256]{2,1,0:T(8,128)(2,1)} custom-call(s32[18]{0:T(128)S(1)} %get-tuple-element.28.order_ref, bf16[1024,512]{1,0:T(8,128)(2,1)S(1)} %pad_maximum_fusion.grad_ref, bf16[16,2,256,256]{3,2,1,0:T(8,128)(2,1)S(1)} %bitcast.60, bf16[16,256,256]{2,1,0:T(8,128)(2,1)S(1)} %collective-permute-done.15.rest_15_.rest_16_.other_w_ref, ...), custom_call_target="tpu_custom_call" | custom-call | flops 1360000000 | bytes 4194304 | tf_op jit(solution)/shard_map/backward_product/pallas_call | solution.py:414
  111.9 3.2 %collective-permute-start.23 = (bf16[4,1024,256]{2,1,0:T(8,128)(2,1)}, bf16[4,1024,256]{2,1,0:T(8,128)(2,1)}, u32[]{:S(2)}, u32[]{:S(2)}) collective-permute-start(bf16[4,1024,256]{2,1,0:T(8,128)(2,1)} %backward_product.8), channel_id=1, source_target_pairs={{0,24},{1,7},{2,26},{3,1},{4,28},{5,3},{6,30},{7,5},{8,0},{9,15},{... | collective-permute-start | bytes 6291464 | tf_op jit(solution)/shard_map/ppermute | solution.py:42
  115.2 1.9 collective-permute-done.17.other_x_ref
  117.1 1.3 forward_codes.1.codes_ref
  119.3 1.5 adapter_rows.1
  121.7 4.7 %all-to-all-start.1 = ((bf16[32,64,256]{2,1,0:T(8,128)(2,1)}), bf16[32,64,256]{2,1,0:T(8,128)(2,1)}, u32[]{:S(2)}, u32[]{:S(2)}) async-start(bf16[32,64,256]{2,1,0:T(8,128)(2,1)} %copy-done.10), calls=%async_computation.1 | async-start | bytes 2097152 | tf_op jit(solution)/shard_map/all_to_all | solution.py:563
  126.4 15.8 %collective-permute-done.21.rest_0_ = bf16[4,1024,256]{2,1,0:T(8,128)(2,1)} collective-permute-done((bf16[4,1024,256]{2,1,0:T(8,128)(2,1)}, bf16[4,1024,256]{2,1,0:T(8,128)(2,1)}, u32[]{:S(2)}, u32[]{:S(2)}) %collective-permute-start.21) | collective-permute-done | bytes 2097184 | tf_op jit(solution)/shard_map/ppermute | solution.py:42
  142.2 7.4 %collective-permute-done.23.rest_1_ = bf16[4,1024,256]{2,1,0:T(8,128)(2,1)} collective-permute-done((bf16[4,1024,256]{2,1,0:T(8,128)(2,1)}, bf16[4,1024,256]{2,1,0:T(8,128)(2,1)}, u32[]{:S(2)}, u32[]{:S(2)}) %collective-permute-start.23) | collective-permute-done | bytes 2097184 | tf_op jit(solution)/shard_map/ppermute | solution.py:42
  149.6 2.2 %copy-done.1 = bf16[1,8192,256]{2,1,0:T(8,128)(2,1)S(1)} copy-done((bf16[1,8192,256]{2,1,0:T(8,128)(2,1)S(1)}, bf16[1,8192,256]{2,1,0:T(8,128)(2,1)}, u32[]{:S(2)}) %copy-start.1) | copy-done | bytes 4194328
  153.9 4.8 %backward_product.9 = bf16[4,1024,256]{2,1,0:T(8,128)(2,1)S(1)} custom-call(s32[18]{0:T(128)S(1)} %get-tuple-element.28.order_ref, bf16[1024,512]{1,0:T(8,128)(2,1)S(1)} %pad_maximum_fusion.grad_ref, bf16[16,2,256,256]{3,2,1,0:T(8,128)(2,1)S(1)} %bitcast.61, bf16[16,256,256]{2,1,0:T(8,128)(2,1)S(1)} %collective-permute-done.15.rest_15_.rest_16_.other_w_ref, ...), custom_call_target="tpu_custom_call" | custom-call | flops 1360000000 | bytes 4194304 | tf_op jit(solution)/shard_map/backward_product/pallas_call | solution.py:414
  160.5 2.9 %collective-permute-start.26 = (bf16[512,256]{1,0:T(8,128)(2,1)S(1)}, bf16[512,256]{1,0:T(8,128)(2,1)S(1)}, u32[]{:S(2)}, u32[]{:S(2)}) collective-permute-start(bf16[512,256]{1,0:T(8,128)(2,1)S(1)} %get-tuple-element.45), channel_id=1, source_target_pairs={{0,6},{1,25},{2,0},{3,27},{4,2},{5,29},{6,4},{7,31},{8,14},{9,1},{... | collective-permute-start | bytes 786440 | tf_op jit(solution)/shard_map/ppermute | solution.py:42
  163.6 4.2 %collective-permute-done.24 = bf16[512,256]{1,0:T(8,128)(2,1)S(1)} collective-permute-done((bf16[512,256]{1,0:T(8,128)(2,1)S(1)}, bf16[512,256]{1,0:T(8,128)(2,1)S(1)}, u32[]{:S(2)}, u32[]{:S(2)}) %collective-permute-start.24) | collective-permute-done | bytes 262176 | tf_op jit(solution)/shard_map/ppermute | solution.py:42
  169.8 3.2 %collective-permute-start.27 = (bf16[1024,256]{1,0:T(8,128)(2,1)}, bf16[1024,256]{1,0:T(8,128)(2,1)S(1)}, u32[]{:S(2)}, u32[]{:S(2)}) collective-permute-start(bf16[1024,256]{1,0:T(8,128)(2,1)} %pad_maximum_fusion.3), channel_id=1, source_target_pairs={{0,6},{1,25},{2,0},{3,27},{4,2},{5,29},{6,4},{7,31},{8,14},{9,1},{... | collective-permute-start | bytes 1572872 | tf_op jit(solution)/shard_map/ppermute | solution.py:42
  173.8 2.8 %fusion = f32[1024,256]{1,0:T(8,128)S(1)} fusion(bf16[2048,256]{1,0:T(8,128)(2,1)} %bitcast.17, s32[2048]{0:T(1024)S(1)} %select_n.145), kind=kOutput, calls=%fused_computation.1 | convolution fusion | flops 1075838976 | bytes 2105344 | tf_op jit(solution)/shard_map/dot_general | solution.py:564
  176.6 1.8 add_convert_fusion
  178.4 1.6 collective-permute-start.18
  180.0 4.5 %collective-permute-done.25 = bf16[1024,256]{1,0:T(8,128)(2,1)} collective-permute-done((bf16[1024,256]{1,0:T(8,128)(2,1)}, bf16[1024,256]{1,0:T(8,128)(2,1)}, u32[]{:S(2)}, u32[]{:S(2)}) %collective-permute-start.25) | collective-permute-done | bytes 524320 | tf_op jit(solution)/shard_map/ppermute | solution.py:42
  184.5 1.5 fusion.4
  186.0 3.1 %collective-permute-start.28 = (bf16[1024,256]{1,0:T(8,128)(2,1)S(1)}, bf16[1024,256]{1,0:T(8,128)(2,1)S(1)}, u32[]{:S(2)}, u32[]{:S(2)}) collective-permute-start(bf16[1024,256]{1,0:T(8,128)(2,1)S(1)} %fusion.4), channel_id=1, source_target_pairs={{0,96},{32,0},{64,32},{96,64},{1,97},{33,1},{65,33},{97,65},{2,98}... | collective-permute-start | bytes 1572872 | tf_op jit(solution)/shard_map/ppermute | solution.py:48
  189.1 6.5 %gradients.1 = (bf16[2,8192,128]{2,1,0:T(8,128)(2,1)}, bf16[2,128,8192]{2,1,0:T(8,128)(2,1)}) custom-call(bf16[32,64,512]{2,1,0:T(8,128)(2,1)} %all-to-all-done.windows_ref, bf16[64,256]{1,0:T(8,128)(2,1)S(1)} %get-tuple-element.37.codes_ref, bf16[64,256]{1,0:T(8,128)(2,1)S(1)} %get-tuple-element.33.grads_ref), custom_call_target="tpu_custom_call" | custom-call | flops 2000000000 | bytes 16777216 | tf_op jit(solution)/shard_map/gradients/pallas_call | solution.py:300
  (112 shorter events, 24.7 us)
Async XLA Ops:
  0.6 23.1 %collective-permute-start.1 = (bf16[1024,256]{1,0:T(8,128)(2,1)}, bf16[1024,256]{1,0:T(8,128)(2,1)S(1)}, u32[]{:S(2)}, u32[]{:S(2)}) collective-permute-start(bf16[1024,256]{1,0:T(8,128)(2,1)} %bitcast.rest_0_), channel_id=1, source_target_pairs={{0,2},{1,9},{2,4},{3,11},{4,6},{5,13},{6,0},{7,15},{8,10},{9,17},{... | collective-permute-start | bytes 1572872 | tf_op jit(solution)/shard_map/ppermute | solution.py:42
  2.3 21.4 %collective-permute-start.3 = (bf16[1024,256]{1,0:T(8,128)(2,1)}, bf16[1024,256]{1,0:T(8,128)(2,1)S(1)}, u32[]{:S(2)}, u32[]{:S(2)}) collective-permute-start(bf16[1024,256]{1,0:T(8,128)(2,1)} %bitcast.rest_0_), channel_id=1, source_target_pairs={{0,6},{1,25},{2,0},{3,27},{4,2},{5,29},{6,4},{7,31},{8,14},{9,1},{... | collective-permute-start | bytes 1572872 | tf_op jit(solution)/shard_map/ppermute | solution.py:42
  3.9 26.0 %collective-permute-start = (bf16[1024,256]{1,0:T(8,128)(2,1)}, bf16[1024,256]{1,0:T(8,128)(2,1)}, u32[]{:S(2)}, u32[]{:S(2)}) collective-permute-start(bf16[1024,256]{1,0:T(8,128)(2,1)} %bitcast.69), channel_id=1, source_target_pairs={{0,1},{1,0},{2,3},{3,2},{4,5},{5,4},{6,7},{7,6},{8,9},{9,8},{10,11... | collective-permute-start | bytes 1572872 | tf_op jit(solution)/shard_map/ppermute | solution.py:42
  12.2 45.1 %all-to-all-start = ((bf16[32,64,512]{2,1,0:T(8,128)(2,1)}), bf16[32,64,512]{2,1,0:T(8,128)(2,1)}, u32[]{:S(2)}, u32[]{:S(2)}) async-start(bf16[32,64,512]{2,1,0:T(8,128)(2,1)} %windows.1), calls=%async_computation | async-start | bytes 4194304 | tf_op jit(solution)/shard_map/all_to_all | solution.py:491
  19.0 3.4 %copy-start.16 = (s32[320]{0:T(512)S(1)}, s32[320]{0:T(512)}, u32[]{:S(2)}) copy-start(s32[320]{0:T(512)} %slots.1.info_ref) | copy-start | bytes 3844
  22.1 4.3 %copy-start.23 = (s32[16]{0:T(128)S(1)}, s32[16]{0:T(128)}, u32[]{:S(2)}) copy-start(s32[16]{0:T(128)} %constant.138.clone) | copy-start | bytes 196
  22.1 4.3 %copy-start.24 = (s32[16]{0:T(128)S(1)}, s32[16]{0:T(128)}, u32[]{:S(2)}) copy-start(s32[16]{0:T(128)} %constant.139.clone) | copy-start | bytes 196
  22.1 7.8 %copy-start.21 = (s32[16]{0:T(128)S(1)}, s32[16]{0:T(128)}, u32[]{:S(2)}) copy-start(s32[16]{0:T(128)} %constant.140.clone) | copy-start | bytes 196
  22.1 7.8 %copy-start.22 = (s32[16]{0:T(128)S(1)}, s32[16]{0:T(128)}, u32[]{:S(2)}) copy-start(s32[16]{0:T(128)} %constant.141.clone) | copy-start | bytes 196
  22.1 56.0 %collective-permute-start.15 = (bf16[16,256,256]{2,1,0:T(8,128)(2,1)}, bf16[16,256,256]{2,1,0:T(8,128)(2,1)S(1)}, u32[]{:S(2)}, u32[]{:S(2)}) collective-permute-start(bf16[16,256,256]{2,1,0:T(8,128)(2,1)} %dynamic-slice_bitcast_fusion), channel_id=1, source_target_pairs={{0,1},{1,0},{2,3},{3,2},{4,5},{5,4},{6,7},{7,6},{8,9},{9,8},{10,11... | collective-permute-start | bytes 6291464 | tf_op jit(solution)/shard_map/ppermute | solution.py:42
  24.8 44.5 %collective-permute-start.7 = (bf16[2,1024,256]{2,1,0:T(8,128)(2,1)}, bf16[2,1024,256]{2,1,0:T(8,128)(2,1)}, u32[]{:S(2)}, u32[]{:S(2)}) collective-permute-start(bf16[2,1024,256]{2,1,0:T(8,128)(2,1)} %pad_maximum_fusion.1.rest_2_), channel_id=1, source_target_pairs={{0,8},{1,3},{2,10},{3,5},{4,12},{5,7},{6,14},{7,1},{8,16},{9,11},{... | collective-permute-start | bytes 3145736 | tf_op jit(solution)/shard_map/ppermute | solution.py:42
  26.5 45.1 %collective-permute-start.10 = (bf16[2,1024,256]{2,1,0:T(8,128)(2,1)}, bf16[2,1024,256]{2,1,0:T(8,128)(2,1)}, u32[]{:S(2)}, u32[]{:S(2)}) collective-permute-start(bf16[2,1024,256]{2,1,0:T(8,128)(2,1)} %pad_maximum_fusion.1.rest_2_), channel_id=1, source_target_pairs={{0,24},{1,7},{2,26},{3,1},{4,28},{5,3},{6,30},{7,5},{8,0},{9,15},{... | collective-permute-start | bytes 3145736 | tf_op jit(solution)/shard_map/ppermute | solution.py:42
  28.1 23.2 %collective-permute-start.2 = (bf16[512,256]{1,0:T(8,128)(2,1)S(1)}, bf16[512,256]{1,0:T(8,128)(2,1)S(1)}, u32[]{:S(2)}, u32[]{:S(2)}) collective-permute-start(bf16[512,256]{1,0:T(8,128)(2,1)S(1)} %slice.69), channel_id=1, source_target_pairs={{0,2},{1,9},{2,4},{3,11},{4,6},{5,13},{6,0},{7,15},{8,10},{9,17},{... | collective-permute-start | bytes 786440 | tf_op jit(solution)/shard_map/ppermute | solution.py:42
  29.9 24.9 %collective-permute-start.4 = (bf16[512,256]{1,0:T(8,128)(2,1)S(1)}, bf16[512,256]{1,0:T(8,128)(2,1)S(1)}, u32[]{:S(2)}, u32[]{:S(2)}) collective-permute-start(bf16[512,256]{1,0:T(8,128)(2,1)S(1)} %slice.70), channel_id=1, source_target_pairs={{0,6},{1,25},{2,0},{3,27},{4,2},{5,29},{6,4},{7,31},{8,14},{9,1},{... | collective-permute-start | bytes 786440 | tf_op jit(solution)/shard_map/ppermute | solution.py:42
  51.3 14.5 %collective-permute-start.5 = (bf16[1024,256]{1,0:T(8,128)(2,1)}, bf16[1024,256]{1,0:T(8,128)(2,1)}, u32[]{:S(2)}, u32[]{:S(2)}) collective-permute-start(bf16[1024,256]{1,0:T(8,128)(2,1)} %bitcast.rest_0_), channel_id=1, source_target_pairs={{0,8},{1,3},{2,10},{3,5},{4,12},{5,7},{6,14},{7,1},{8,16},{9,11},{... | collective-permute-start | bytes 1572872 | tf_op jit(solution)/shard_map/ppermute | solution.py:42
  54.8 15.8 %collective-permute-start.8 = (bf16[1024,256]{1,0:T(8,128)(2,1)}, bf16[1024,256]{1,0:T(8,128)(2,1)}, u32[]{:S(2)}, u32[]{:S(2)}) collective-permute-start(bf16[1024,256]{1,0:T(8,128)(2,1)} %bitcast.rest_0_), channel_id=1, source_target_pairs={{0,24},{1,7},{2,26},{3,1},{4,28},{5,3},{6,30},{7,5},{8,0},{9,15},{... | collective-permute-start | bytes 1572872 | tf_op jit(solution)/shard_map/ppermute | solution.py:42
  57.3 2.2 %copy-start.2 = (bf16[1,2,8192,128]{3,2,1,0:T(8,128)(2,1)S(1)}, bf16[1,2,8192,128]{3,2,1,0:T(8,128)(2,1)}, u32[]{:S(2)}) copy-start(bf16[1,2,8192,128]{3,2,1,0:T(8,128)(2,1)} %param.18) | copy-start | bytes 12582916
  59.5 2.2 %copy-start.3 = (bf16[1,2,128,8192]{3,2,1,0:T(8,128)(2,1)S(1)}, bf16[1,2,128,8192]{3,2,1,0:T(8,128)(2,1)}, u32[]{:S(2)}) copy-start(bf16[1,2,128,8192]{3,2,1,0:T(8,128)(2,1)} %param.19) | copy-start | bytes 12582916
  65.9 9.5 %collective-permute-start.9 = (bf16[1024,256]{1,0:T(8,128)(2,1)}, bf16[1024,256]{1,0:T(8,128)(2,1)S(1)}, u32[]{:S(2)}, u32[]{:S(2)}) collective-permute-start(bf16[1024,256]{1,0:T(8,128)(2,1)} %constant_dynamic-update-slice_fusion.rest_1_), channel_id=1, source_target_pairs={{0,24},{1,7},{2,26},{3,1},{4,28},{5,3},{6,30},{7,5},{8,0},{9,15},{... | collective-permute-start | bytes 1572872 | tf_op jit(solution)/shard_map/ppermute | solution.py:42
  67.5 13.9 %copy-start = (bf16[1,8192,256]{2,1,0:T(8,128)(2,1)S(1)}, bf16[1,8192,256]{2,1,0:T(8,128)(2,1)}, u32[]{:S(2)}) copy-start(bf16[1,8192,256]{2,1,0:T(8,128)(2,1)} %param.17) | copy-start | bytes 12582916
  69.3 38.8 %copy-start.5 = (bf16[16,64,256]{2,1,0:T(8,128)(2,1)}, bf16[16,64,256]{2,1,0:T(8,128)(2,1)S(1)}, u32[]{:S(2)}) copy-start(bf16[16,64,256]{2,1,0:T(8,128)(2,1)S(1)} %get-tuple-element.34.own_ret_ref) | copy-start | bytes 1572868
  69.3 8.8 %collective-permute-start.19 = (bf16[16,64,256]{2,1,0:T(8,128)(2,1)S(1)}, bf16[16,64,256]{2,1,0:T(8,128)(2,1)S(1)}, u32[]{:S(2)}, u32[]{:S(2)}) collective-permute-start(bf16[16,64,256]{2,1,0:T(8,128)(2,1)S(1)} %get-tuple-element.35), channel_id=1, source_target_pairs={{0,1},{1,0},{2,3},{3,2},{4,5},{5,4},{6,7},{7,6},{8,9},{9,8},{10,11... | collective-permute-start | bytes 1572872 | tf_op jit(solution)/shard_map/ppermute | solution.py:42
  70.6 12.4 %collective-permute-start.11 = (bf16[1024,256]{1,0:T(8,128)(2,1)}, bf16[1024,256]{1,0:T(8,128)(2,1)S(1)}, u32[]{:S(2)}, u32[]{:S(2)}) collective-permute-start(bf16[1024,256]{1,0:T(8,128)(2,1)} %collective-permute-done.5.rest_3_), channel_id=1, source_target_pairs={{0,8},{1,3},{2,10},{3,5},{4,12},{5,7},{6,14},{7,1},{8,16},{9,11},{... | collective-permute-start | bytes 1572872 | tf_op jit(solution)/shard_map/ppermute | solution.py:42
  71.6 15.3 %collective-permute-start.6 = (bf16[1024,256]{1,0:T(8,128)(2,1)}, bf16[1024,256]{1,0:T(8,128)(2,1)S(1)}, u32[]{:S(2)}, u32[]{:S(2)}) collective-permute-start(bf16[1024,256]{1,0:T(8,128)(2,1)} %constant_dynamic-update-slice_fusion.rest_1_), channel_id=1, source_target_pairs={{0,8},{1,3},{2,10},{3,5},{4,12},{5,7},{6,14},{7,1},{8,16},{9,11},{... | collective-permute-start | bytes 1572872 | tf_op jit(solution)/shard_map/ppermute | solution.py:42
  75.3 12.9 %collective-permute-start.12 = (bf16[1024,256]{1,0:T(8,128)(2,1)S(1)}, bf16[1024,256]{1,0:T(8,128)(2,1)S(1)}, u32[]{:S(2)}, u32[]{:S(2)}) collective-permute-start(bf16[1024,256]{1,0:T(8,128)(2,1)S(1)} %collective-permute-done.9.rest_7_), channel_id=1, source_target_pairs={{0,24},{1,7},{2,26},{3,1},{4,28},{5,3},{6,30},{7,5},{8,0},{9,15},{... | collective-permute-start | bytes 1572872 | tf_op jit(solution)/shard_map/ppermute | solution.py:42
  78.1 14.4 %collective-permute-start.13 = (bf16[1024,256]{1,0:T(8,128)(2,1)S(1)}, bf16[1024,256]{1,0:T(8,128)(2,1)S(1)}, u32[]{:S(2)}, u32[]{:S(2)}) collective-permute-start(bf16[1024,256]{1,0:T(8,128)(2,1)S(1)} %slice_bitcast_fusion.2), channel_id=1, source_target_pairs={{0,8},{1,3},{2,10},{3,5},{4,12},{5,7},{6,14},{7,1},{8,16},{9,11},{... | collective-permute-start | bytes 1572872 | tf_op jit(solution)/shard_map/ppermute | solution.py:42
  78.1 30.0 %copy-start.7 = (bf16[16,64,256]{2,1,0:T(8,128)(2,1)}, bf16[16,64,256]{2,1,0:T(8,128)(2,1)S(1)}, u32[]{:S(2)}) copy-start(bf16[16,64,256]{2,1,0:T(8,128)(2,1)S(1)} %collective-permute-done.19.other_ret_ref) | copy-start | bytes 1572868
  78.1 14.4 %collective-permute-start.14 = (bf16[1024,256]{1,0:T(8,128)(2,1)S(1)}, bf16[1024,256]{1,0:T(8,128)(2,1)S(1)}, u32[]{:S(2)}, u32[]{:S(2)}) collective-permute-start(bf16[1024,256]{1,0:T(8,128)(2,1)S(1)} %slice_bitcast_fusion.1), channel_id=1, source_target_pairs={{0,24},{1,7},{2,26},{3,1},{4,28},{5,3},{6,30},{7,5},{8,0},{9,15},{... | collective-permute-start | bytes 1572872 | tf_op jit(solution)/shard_map/ppermute | solution.py:42
  83.0 21.2 %collective-permute-start.20 = (bf16[2,1024,256]{2,1,0:T(8,128)(2,1)S(1)}, bf16[2,1024,256]{2,1,0:T(8,128)(2,1)S(1)}, u32[]{:S(2)}, u32[]{:S(2)}) collective-permute-start(bf16[2,1024,256]{2,1,0:T(8,128)(2,1)S(1)} %backward_product.5), channel_id=1, source_target_pairs={{0,8},{1,3},{2,10},{3,5},{4,12},{5,7},{6,14},{7,1},{8,16},{9,11},{... | collective-permute-start | bytes 3145736 | tf_op jit(solution)/shard_map/ppermute | solution.py:42
  86.9 21.2 %collective-permute-start.22 = (bf16[2,1024,256]{2,1,0:T(8,128)(2,1)S(1)}, bf16[2,1024,256]{2,1,0:T(8,128)(2,1)S(1)}, u32[]{:S(2)}, u32[]{:S(2)}) collective-permute-start(bf16[2,1024,256]{2,1,0:T(8,128)(2,1)S(1)} %backward_product.7), channel_id=1, source_target_pairs={{0,24},{1,7},{2,26},{3,1},{4,28},{5,3},{6,30},{7,5},{8,0},{9,15},{... | collective-permute-start | bytes 3145736 | tf_op jit(solution)/shard_map/ppermute | solution.py:42
  104.2 3.8 %copy-start.17 = (f32[1024,256]{1,0:T(8,128)}, f32[1024,256]{1,0:T(8,128)S(1)}, u32[]{:S(2)}) copy-start(f32[1024,256]{1,0:T(8,128)S(1)} %get-tuple-element.24) | copy-start | bytes 3145732
  108.1 34.2 %collective-permute-start.21 = (bf16[4,1024,256]{2,1,0:T(8,128)(2,1)}, bf16[4,1024,256]{2,1,0:T(8,128)(2,1)}, u32[]{:S(2)}, u32[]{:S(2)}) collective-permute-start(bf16[4,1024,256]{2,1,0:T(8,128)(2,1)} %backward_product.6), channel_id=1, source_target_pairs={{0,8},{1,3},{2,10},{3,5},{4,12},{5,7},{6,14},{7,1},{8,16},{9,11},{... | collective-permute-start | bytes 6291464 | tf_op jit(solution)/shard_map/ppermute | solution.py:42
  111.9 37.7 %collective-permute-start.23 = (bf16[4,1024,256]{2,1,0:T(8,128)(2,1)}, bf16[4,1024,256]{2,1,0:T(8,128)(2,1)}, u32[]{:S(2)}, u32[]{:S(2)}) collective-permute-start(bf16[4,1024,256]{2,1,0:T(8,128)(2,1)} %backward_product.8), channel_id=1, source_target_pairs={{0,24},{1,7},{2,26},{3,1},{4,28},{5,3},{6,30},{7,5},{8,0},{9,15},{... | collective-permute-start | bytes 6291464 | tf_op jit(solution)/shard_map/ppermute | solution.py:42
  115.2 1.9 collective-permute-start.17
  117.1 2.2 %copy-start.4 = (bf16[1,2,128,8192]{3,2,1,0:T(8,128)(2,1)S(1)}, bf16[1,2,128,8192]{3,2,1,0:T(8,128)(2,1)}, u32[]{:S(2)}) copy-start(bf16[1,2,128,8192]{3,2,1,0:T(8,128)(2,1)} %param.19) | copy-start | bytes 12582916
  121.7 52.1 %all-to-all-start.1 = ((bf16[32,64,256]{2,1,0:T(8,128)(2,1)}), bf16[32,64,256]{2,1,0:T(8,128)(2,1)}, u32[]{:S(2)}, u32[]{:S(2)}) async-start(bf16[32,64,256]{2,1,0:T(8,128)(2,1)} %copy-done.10), calls=%async_computation.1 | async-start | bytes 2097152 | tf_op jit(solution)/shard_map/all_to_all | solution.py:563
  149.6 2.2 %copy-start.1 = (bf16[1,8192,256]{2,1,0:T(8,128)(2,1)S(1)}, bf16[1,8192,256]{2,1,0:T(8,128)(2,1)}, u32[]{:S(2)}) copy-start(bf16[1,8192,256]{2,1,0:T(8,128)(2,1)} %param.17) | copy-start | bytes 12582916
  160.0 3.4 %copy-start.18 = (f32[1024,256]{1,0:T(8,128)S(1)}, f32[1024,256]{1,0:T(8,128)}, u32[]{:S(2)}) copy-start(f32[1024,256]{1,0:T(8,128)} %copy-done.17) | copy-start | bytes 3145732
  160.0 3.4 %copy-start.20 = (s32[64]{0:T(128)S(1)}, s32[64]{0:T(128)}, u32[]{:S(2)}) copy-start(s32[64]{0:T(128)} %get-tuple-element.51) | copy-start | bytes 772
  160.1 7.7 %collective-permute-start.24 = (bf16[512,256]{1,0:T(8,128)(2,1)S(1)}, bf16[512,256]{1,0:T(8,128)(2,1)S(1)}, u32[]{:S(2)}, u32[]{:S(2)}) collective-permute-start(bf16[512,256]{1,0:T(8,128)(2,1)S(1)} %get-tuple-element.44), channel_id=1, source_target_pairs={{0,2},{1,9},{2,4},{3,11},{4,6},{5,13},{6,0},{7,15},{8,10},{9,17},{... | collective-permute-start | bytes 786440 | tf_op jit(solution)/shard_map/ppermute | solution.py:42
  160.5 7.3 %collective-permute-start.26 = (bf16[512,256]{1,0:T(8,128)(2,1)S(1)}, bf16[512,256]{1,0:T(8,128)(2,1)S(1)}, u32[]{:S(2)}, u32[]{:S(2)}) collective-permute-start(bf16[512,256]{1,0:T(8,128)(2,1)S(1)} %get-tuple-element.45), channel_id=1, source_target_pairs={{0,6},{1,25},{2,0},{3,27},{4,2},{5,29},{6,4},{7,31},{8,14},{9,1},{... | collective-permute-start | bytes 786440 | tf_op jit(solution)/shard_map/ppermute | solution.py:42
  163.4 13.2 %collective-permute-start.16 = (f32[1024,256]{1,0:T(8,128)S(1)}, f32[1024,256]{1,0:T(8,128)}, u32[]{:S(2)}, u32[]{:S(2)}) collective-permute-start(f32[1024,256]{1,0:T(8,128)S(1)} %copy-done.18), channel_id=1, source_target_pairs={{0,1},{1,0},{2,3},{3,2},{4,5},{5,4},{6,7},{7,6},{8,9},{9,8},{10,11... | collective-permute-start | bytes 3145736 | tf_op jit(solution)/shard_map/ppermute | solution.py:42
  169.8 10.3 %collective-permute-start.27 = (bf16[1024,256]{1,0:T(8,128)(2,1)}, bf16[1024,256]{1,0:T(8,128)(2,1)S(1)}, u32[]{:S(2)}, u32[]{:S(2)}) collective-permute-start(bf16[1024,256]{1,0:T(8,128)(2,1)} %pad_maximum_fusion.3), channel_id=1, source_target_pairs={{0,6},{1,25},{2,0},{3,27},{4,2},{5,29},{6,4},{7,31},{8,14},{9,1},{... | collective-permute-start | bytes 1572872 | tf_op jit(solution)/shard_map/ppermute | solution.py:42
  173.8 10.7 %collective-permute-start.25 = (bf16[1024,256]{1,0:T(8,128)(2,1)}, bf16[1024,256]{1,0:T(8,128)(2,1)}, u32[]{:S(2)}, u32[]{:S(2)}) collective-permute-start(bf16[1024,256]{1,0:T(8,128)(2,1)} %pad_maximum_fusion.2), channel_id=1, source_target_pairs={{0,2},{1,9},{2,4},{3,11},{4,6},{5,13},{6,0},{7,15},{8,10},{9,17},{... | collective-permute-start | bytes 1572872 | tf_op jit(solution)/shard_map/ppermute | solution.py:42
  173.8 2.8 %copy-start.14 = (f32[1024,256]{1,0:T(8,128)S(1)}, f32[1024,256]{1,0:T(8,128)}, u32[]{:S(2)}) copy-start(f32[1024,256]{1,0:T(8,128)} %copy-done.13) | copy-start | bytes 3145732
  176.6 7.9 %copy-start.12 = (bf16[1,1024,256]{2,1,0:T(8,128)(2,1)S(1)}, bf16[1,1024,256]{2,1,0:T(8,128)(2,1)}, u32[]{:S(2)}) copy-start(bf16[1,1024,256]{2,1,0:T(8,128)(2,1)} %param.16) | copy-start | bytes 1572868
  178.4 17.2 %collective-permute-start.18 = (bf16[1024,256]{1,0:T(8,128)(2,1)S(1)}, bf16[1024,256]{1,0:T(8,128)(2,1)S(1)}, u32[]{:S(2)}, u32[]{:S(2)}) collective-permute-start(bf16[1024,256]{1,0:T(8,128)(2,1)S(1)} %add_convert_fusion), channel_id=1, source_target_pairs={{0,32},{32,64},{64,96},{96,0},{1,33},{33,65},{65,97},{97,1},{2,34}... | collective-permute-start | bytes 1572872 | tf_op jit(solution)/shard_map/ppermute | solution.py:48
  186.0 10.1 %collective-permute-start.28 = (bf16[1024,256]{1,0:T(8,128)(2,1)S(1)}, bf16[1024,256]{1,0:T(8,128)(2,1)S(1)}, u32[]{:S(2)}, u32[]{:S(2)}) collective-permute-start(bf16[1024,256]{1,0:T(8,128)(2,1)S(1)} %fusion.4), channel_id=1, source_target_pairs={{0,96},{32,0},{64,32},{96,64},{1,97},{33,1},{65,33},{97,65},{2,98}... | collective-permute-start | bytes 1572872 | tf_op jit(solution)/shard_map/ppermute | solution.py:48
  (8 other events, 8.1 us)

commit v3 on v2

--- a/solution.py
+++ b/solution.py
@@ -106,10 +106,10 @@
     return jnp.where(held, rows, 0.0).astype(BF16)
 
 
-def windows_body(adapters, window, each, info_ref, stash_ref, cotangent_ref, out_ref, wide_ref):
+def windows_body(adapters, window, each, info_ref, stash_ref, cotangent_ref, stash_out_ref, cotangent_out_ref, wide_ref):
     tokens = stash_ref.shape[0]
     step = pl.program_id(0)
-    owned = out_ref.shape[1] // window
+    owned = stash_out_ref.shape[1] // window
 
     @pl.when(step == 0)
     def _():
@@ -120,7 +120,8 @@
         slot = step * each + index
         rows = slot_rows(wide_ref, info_ref[2 * adapters + slot], info_ref[3 * adapters + slot], window)
         low = index % owned * window
-        out_ref[index // owned, low : low + window] = rows
+        stash_out_ref[index // owned, low : low + window] = rows[:, :BLOCK]
+        cotangent_out_ref[index // owned, low : low + window] = rows[:, BLOCK:]
 
 
 def windows_of(info, stash, cotangent, adapters, window, rows):
@@ -128,17 +129,17 @@
     tokens = stash.shape[0]
     each = 16
     owners = each * window // rows
-    out = pl.BlockSpec((owners, rows, 2 * BLOCK), lambda i, info: (i, 0, 0))
+    out = pl.BlockSpec((owners, rows, BLOCK), lambda i, info: (i, 0, 0))
     return kernel(
         functools.partial(windows_body, adapters, window, each),
         "windows",
         (adapters // each,),
         1,
         [whole(stash.shape), whole(cotangent.shape)],
-        [(out, (devices, rows, 2 * BLOCK), BF16)],
+        [(out, (devices, rows, BLOCK), BF16)] * 2,
         2 * 10**9,
         [pltpu.VMEM((tokens + window + SUBLANES, 2 * BLOCK), F32)],
-    )(info, stash, cotangent)[0]
+    )(info, stash, cotangent)
 
 
 NT = (((1,), (1,)), ((), ()))
@@ -150,45 +151,75 @@
     return jnp.concatenate([ref[(slot,) + index] for slot in range(ref.shape[0])], axis=1)
 
 
-def codes_body(windows_ref, down_ref, up_ref, scale_ref, codes_ref, grads_ref, code_sum, grad_sum):
+def code_grads_body(windows_ref, up_ref, scale_ref, grads_ref, grad_sum):
     step = pl.program_id(0)
 
     @pl.when(step == 0)
     def _():
+        grad_sum[...] = jnp.zeros_like(grad_sum)
+
+    grad = jnp.concatenate([windows_ref[s] for s in range(GROUP)], axis=1)
+    up = up_ref[...].reshape(-1, up_ref.shape[2])
+    grad_sum[...] += lax.dot_general(grad, up, NT, preferred_element_type=F32)
+
+    @pl.when(step == pl.num_programs(0) - 1)
+    def _():
+        grads_ref[...] = (grad_sum[...] * scale_ref[...]).astype(BF16)
+
+
+def code_grads_of(windows, up, scale):
+    devices, rows, _ = windows.shape
+    owned, rank, _ = up.shape
+    shape = scale.shape
+    return kernel(
+        code_grads_body,
+        "code_grads",
+        (devices // GROUP,),
+        0,
+        [
+            pl.BlockSpec((GROUP, rows, BLOCK), lambda i: (i, 0, 0)),
+            pl.BlockSpec((owned, rank, GROUP * BLOCK), lambda i: (0, 0, i)),
+            whole(shape),
+        ],
+        [(whole(shape), shape, BF16)],
+        10**9,
+        [pltpu.VMEM(shape, F32)],
+    )(windows, up, scale)[0]
+
+
+def back_codes_body(windows_ref, down_ref, scale_ref, codes_ref, code_sum):
+    step = pl.program_id(0)
+
+    @pl.when(step == 0)
+    def _():
         code_sum[...] = jnp.zeros_like(code_sum)
-        grad_sum[...] = jnp.zeros_like(grad_sum)
-
-    stash = jnp.concatenate([windows_ref[s, :, :BLOCK] for s in range(GROUP)], axis=1)
-    grad = jnp.concatenate([windows_ref[s, :, BLOCK:] for s in range(GROUP)], axis=1)
-    up = up_ref[...].reshape(-1, up_ref.shape[2])
+
+    stash = jnp.concatenate([windows_ref[s] for s in range(GROUP)], axis=1)
     code_sum[...] += jnp.dot(stash, lanes(down_ref), preferred_element_type=F32)
-    grad_sum[...] += lax.dot_general(grad, up, NT, preferred_element_type=F32)
 
     @pl.when(step == pl.num_programs(0) - 1)
     def _():
         codes_ref[...] = (code_sum[...] * scale_ref[...]).astype(BF16)
-        grads_ref[...] = (grad_sum[...] * scale_ref[...]).astype(BF16)
-
-
-def codes_of(windows, down, up, scale):
+
+
+def back_codes_of(windows, down, scale):
     devices, rows, _ = windows.shape
     owned, _, rank = down.shape
     shape = scale.shape
     return kernel(
-        codes_body,
-        "codes",
+        back_codes_body,
+        "back_codes",
         (devices // GROUP,),
         0,
         [
-            pl.BlockSpec((GROUP, rows, 2 * BLOCK), lambda i: (i, 0, 0)),
+            pl.BlockSpec((GROUP, rows, BLOCK), lambda i: (i, 0, 0)),
             pl.BlockSpec((owned, GROUP * BLOCK, rank), lambda i: (0, i, 0)),
-            pl.BlockSpec((owned, rank, GROUP * BLOCK), lambda i: (0, 0, i)),
             whole(shape),
         ],
-        [(whole(shape), shape, BF16)] * 2,
-        2 * 10**9,
-        [pltpu.VMEM(shape, F32)] * 2,
-    )(windows, down, up, scale)
+        [(whole(shape), shape, BF16)],
+        10**9,
+        [pltpu.VMEM(shape, F32)],
+    )(windows, down, scale)[0]
 
 
 def halves(down):
@@ -267,34 +298,65 @@
 def adapter_rows_of(codes, up, devices):
     rows = codes.shape[0]
     owned, rank, _ = up.shape
-    group = GROUP
-    out = pl.BlockSpec((group, rows, BLOCK), lambda i: (i, 0, 0))
+    out = pl.BlockSpec((GROUP, rows, BLOCK), lambda i: (i, 0, 0))
     return kernel(
         adapter_body,
         "adapter_rows",
-        (devices // group,),
+        (devices // GROUP,),
         0,
-        [whole(codes.shape), pl.BlockSpec((owned, rank, group * BLOCK), lambda i: (0, 0, i))],
+        [whole(codes.shape), pl.BlockSpec((owned, rank, GROUP * BLOCK), lambda i: (0, 0, i))],
         [(out, (devices, rows, BLOCK), BF16)],
         10**9,
     )(codes, up)[0]
 
 
-def gradients_body(windows_ref, codes_ref, grads_ref, down_ref, up_ref):
+def forward_sum_body(window, info_ref, x_ref, own_ref, other_ref, adapter_ref, out_ref, wide_ref):
+    tokens = x_ref.shape[0]
+    wide_ref[:tokens] = x_ref[...].astype(F32) + (own_ref[...] + other_ref[...])
+    devices, rows, _ = adapter_ref.shape
+    owned = rows // window
+    spare = jnp.zeros((SUBLANES, BLOCK), F32)
+    for slot in range(devices * owned):
+        start = info_ref[slot]
+        past = lax.rem(start, SUBLANES)
+        low = slot % owned * window
+        added = adapter_ref[slot // owned, low : low + window].astype(F32)
+        added = pltpu.roll(jnp.concatenate([added, spare]), past, 0)
+        span = pl.ds(pl.multiple_of(start - past, SUBLANES), window + SUBLANES)
+        wide_ref[span, :] += added
+    out_ref[...] = wide_ref[:tokens].astype(BF16)
+
+
+def forward_sum(info, layer_in, own_out, other_out, arrived, window):
+    devices, rows, _ = arrived.shape
+    shape = layer_in.shape
+    adapter = pl.BlockSpec((devices, rows, BLOCK), lambda i, info: (0, 0, 0))
+    return kernel(
+        functools.partial(forward_sum_body, window),
+        "forward_sum",
+        (1,),
+        1,
+        [whole(shape), whole(shape), whole(shape), adapter],
+        [(whole(shape), shape, BF16)],
+        10**8,
+        [pltpu.VMEM((shape[0] + window + SUBLANES, BLOCK), F32)],
+    )(info, layer_in, own_out, other_out, arrived)[0]
+
+
+def gradients_body(stash_ref, grad_ref, codes_ref, grads_ref, down_ref, up_ref):
     owned, _, rank = down_ref.shape
     for s in range(GROUP):
         span = slice(s * BLOCK, (s + 1) * BLOCK)
-        stash, grad = windows_ref[s, :, :BLOCK], windows_ref[s, :, BLOCK:]
-        down = lax.dot_general(stash, grads_ref[...], TN, preferred_element_type=F32).astype(BF16)
-        up = lax.dot_general(codes_ref[...], grad, TN, preferred_element_type=F32).astype(BF16)
+        down = lax.dot_general(stash_ref[s], grads_ref[...], TN, preferred_element_type=F32).astype(BF16)
+        up = lax.dot_general(codes_ref[...], grad_ref[s], TN, preferred_element_type=F32).astype(BF16)
         for slot in range(owned):
             own = slice(slot * rank, (slot + 1) * rank)
             down_ref[slot, span] = down[:, own]
             up_ref[slot, :, span] = up[own]
 
 
-def gradients_of(windows, back_codes, code_grads, owned):
-    devices, rows, _ = windows.shape
+def gradients_of(stash_windows, grad_windows, back_codes, code_grads, owned):
+    devices, rows, _ = grad_windows.shape
     rank = back_codes.shape[1] // owned
     width = devices * BLOCK
     return kernel(
@@ -303,7 +365,8 @@
         (devices // GROUP,),
         0,
         [
-            pl.BlockSpec((GROUP, rows, 2 * BLOCK), lambda i: (i, 0, 0)),
+            pl.BlockSpec((GROUP, rows, BLOCK), lambda i: (i, 0, 0)),
+            pl.BlockSpec((GROUP, rows, BLOCK), lambda i: (i, 0, 0)),
             whole(back_codes.shape),
             whole(code_grads.shape),
         ],
@@ -312,14 +375,14 @@
             (pl.BlockSpec((owned, rank, GROUP * BLOCK), lambda i: (0, 0, i)), (owned, rank, width), BF16),
         ],
         2 * 10**9,
-    )(windows, back_codes, code_grads)
+    )(stash_windows, grad_windows, back_codes, code_grads)
 
 
 PAIR = 2
 
 
 def forward_body(window, order_ref, info_ref, *rest):
-    pieces, rest = rest[:13], rest[13:]
+    pieces, rest = rest[:12], rest[12:]
     own_w, other_w, rest = rest[:PAIR], rest[PAIR : 2 * PAIR], rest[2 * PAIR :]
     own_ref, other_ref, own_x_ref, other_x_ref, wide_ref = rest
     step = pl.program_id(0)
@@ -350,11 +413,10 @@
         own_ref[...] = own_sum
         other_ref[...] = other_sum
 
-    own, far, near = pieces[0:9:3], pieces[1:9:3], pieces[2:9:3]
+    own, far, near = pieces[0::3], pieces[1::3], pieces[2::3]
     pairs = []
-    for line in range(3):
+    for line in range(SIDE):
         pairs += [((own[line], None), (far[line], None)), ((near[line], 0), (near[line], 1))]
-    pairs += [((pieces[9], None), (pieces[10], None)), ((pieces[11], None), (pieces[12], None))]
     for index, pair in enumerate(pairs):
         pl.when(step == index)(functools.partial(take, *pair))
 
@@ -385,56 +447,59 @@
     )(order, info, *pieces, *[weight] * PAIR, *[other_weight] * PAIR)
 
 
-def backward_body(takes, order_ref, grad_ref, own_w_ref, other_w_ref, spread_ref, own_ret_ref, other_ret_ref, *rest):
-    received, out_ref = rest[:-1], rest[-1]
+def backward_body(sizes, order_ref, grad_ref, own_w_ref, other_w_ref, spread_ref, own_ret_ref, other_ret_ref, *outs):
     step = pl.program_id(0)
     matrix = jnp.concatenate([own_w_ref[0, 0], other_w_ref[0]], axis=1)
     returned = jnp.concatenate([own_ret_ref[0], other_ret_ref[0]], axis=0)
-    tile = 2 * BLOCK
-    for low in range(0, grad_ref.shape[0], tile):
-        span = slice(low, low + tile)
-        total = lax.dot_general(grad_ref[span], matrix, NT, preferred_element_type=F32)
-        total += jnp.dot(spread_ref[span], returned, preferred_element_type=F32)
-        for ref, (first, last) in zip(received, takes):
-            inside = (step >= first) & (step < last)
-            total += jnp.where(inside, ref[0, span].astype(F32), 0.0)
-        out_ref[0, span] = total.astype(BF16)
-
-
-def backward_product(order, base, blocks, grads, weight, other_weight, spread, returned, received=(), takes=()):
+    total = lax.dot_general(grad_ref[...], matrix, NT, preferred_element_type=F32)
+    total += jnp.dot(spread_ref[...], returned, preferred_element_type=F32)
+    total = total.astype(BF16)
+    low = 0
+    for out_ref, size in zip(outs, sizes):
+
+        @pl.when((step >= low) & (step < low + size))
+        def _(out_ref=out_ref):
+            out_ref[0] = total
+
+        low += size
+
+
+def backward_product(order, base, sizes, grads, weight, other_weight, spread, returned):
     tokens = grads.shape[0]
-    core_at = CHIPS
-
-    def taken(bounds):
-        first, last = bounds
-        return pl.BlockSpec((1, tokens, BLOCK), lambda j, order: (jnp.clip(j - first, 0, last - first - 1), 0, 0))
+    blocks = sum(sizes)
+
+    def out(index):
+        low, size = sum(sizes[:index]), sizes[index]
+        return pl.BlockSpec((1, tokens, BLOCK), lambda j, order: (jnp.clip(j - low, 0, size - 1), 0, 0))
 
     rows = pl.BlockSpec((1,) + returned[0].shape[1:], lambda j, order: (order[base + j], 0, 0))
-    out = pl.BlockSpec((1, tokens, BLOCK), lambda j, order: (j, 0, 0))
-    return kernel(
-        functools.partial(backward_body, takes),
+    return kernel(
+        functools.partial(backward_body, sizes),
         "backward_product",
         (blocks,),
         1,
         [
             whole(grads.shape),
-            pl.BlockSpec((1, 1, BLOCK, BLOCK), lambda j, order: (order[base + j], order[core_at], 0, 0)),
+            pl.BlockSpec((1, 1, BLOCK, BLOCK), lambda j, order: (order[base + j], order[CHIPS], 0, 0)),
             pl.BlockSpec((1, BLOCK, BLOCK), lambda j, order: (order[base + j], 0, 0)),
             whole(spread.shape),
             rows,
             rows,
-        ]
-        + [taken(bounds) for bounds in takes],
-        [(out, (blocks, tokens, BLOCK), BF16)],
+        ],
+        [(out(index), (size, tokens, BLOCK), BF16) for index, size in enumerate(sizes)],
         blocks * 34 * 10**7,
-    )(order, grads, weight, other_weight, spread, *returned, *received)[0]
-
-
-def add_rounded(*values):
+    )(order, grads, weight, other_weight, spread, *returned)
+
+
+def total_of(*values):
     total = values[0].astype(F32)
     for value in values[1:]:
         total = total + value.astype(F32)
-    return total.astype(BF16)
+    return total
+
+
+def add_rounded(*values):
+    return total_of(*values).astype(BF16)
 
 
 def shards(
@@ -456,7 +521,6 @@
     window = 2 * tokens // adapters
     rows = owned * window
     devices = CHIPS * CORES
-    half = tokens // 2
     device = lax.axis_index("tp")
     core = device % CORES
     chip = device // CORES
@@ -471,24 +535,26 @@
 
     below, above = send(layer_in, FIRST_UP), send(layer_in, FIRST_DOWN)
     own_below, own_above = send(layer_in, SECOND_UP), send(layer_in, SECOND_DOWN)
-    far_low, far_high = send(below[:half], FIRST_UP), send(above[half:], FIRST_DOWN)
-    own_far = send(own_below, SECOND_UP)
+    far = send(below, FIRST_UP)
     near = jnp.stack([below, above])
     near_below, near_above = send(near, SECOND_UP), send(near, SECOND_DOWN)
-    far = jnp.concatenate([far_low, far_high])
     far_below, far_above = send(far, SECOND_UP), send(far, SECOND_DOWN)
-    below_far, above_far = send(near_below[0], SECOND_UP), send(near_above[1], SECOND_DOWN)
+    own_far = send(own_above, SECOND_DOWN)
+    near_far = send(near_below, SECOND_UP)
     far_far = send(far_above, SECOND_DOWN)
     pieces = (layer_in, far, near, own_below, far_below, near_below, own_above, far_above, near_above)
-    pieces += (own_far, far_far, below_far, above_far)
+    pieces += (own_far, far_far, near_far)
 
     for_other = lax.dynamic_index_in_dim(weight, 1 - core, axis=1, keepdims=False)
     other_weight = send(for_other, OTHER_CORE)
     other_cotangent = send(cotangent, OTHER_CORE)
 
     info = slots(forward_counts, backward_counts, ranks, adapter_slot)
-    windows = windows_of(info, stash, cotangent, adapters, window, rows)
-    windows = lax.all_to_all(windows, "tp", split_axis=0, concat_axis=0, tiled=True)
+    stash_windows, grad_windows = windows_of(info, stash, cotangent, adapters, window, rows)
+    grad_windows = lax.all_to_all(grad_windows, "tp", split_axis=0, concat_axis=0, tiled=True)
+
+    stash_windows, other_weight = lax.optimization_barrier((stash_windows, other_weight))
+    stash_windows = lax.all_to_all(stash_windows, "tp", split_axis=0, concat_axis=0, tiled=True)
 
     starts = info.reshape(5, adapters)
     offsets = jnp.arange(window, dtype=jnp.int32)
@@ -503,7 +569,6 @@
         other = lax.dynamic_slice_in_dim(token, (device ^ 1) * rows, rows)
         return jnp.concatenate([mine, other])
 
-    fwd_token = tokens_of(starts[0], starts[1])
     bwd_token = tokens_of(starts[2], starts[3])
     own_rank = lax.dynamic_slice_in_dim(starts[4], device * owned, owned)
     column = jnp.arange(owned * rank, dtype=jnp.int32)
@@ -513,7 +578,6 @@
     mine = row[:, None] // window == column[None, :] // rank
     scale = jnp.where(mine & live[None, :], factor[None, :], 0.0)
     spread = (token_ids[:, None] == of_chip(bwd_token)[None, :]).astype(BF16)
-    put = (token_ids[:, None] == fwd_token[None, :]).astype(BF16)
     core_index = core.astype(jnp.int32).reshape(1)
 
     def chips(pairs):
@@ -522,50 +586,55 @@
         x = jnp.where(core == 0, chip_x + first, chip_x + second) % SIDE
         return jnp.concatenate([z * SIDE + x, core.reshape(1), chip.reshape(1)]).astype(jnp.int32)
 
-    order = chips([(s, f) for s in (2, 1, 3, 0) for f in (2, 1, 3, 0)])
+    far_blocks = [(2, 2), (2, 1), (2, 3), (2, 0)]
+    direct_blocks = [(1, 3), (1, 0), (3, 2), (3, 1)]
+    rest_blocks = [(1, 2), (1, 1), (3, 3), (3, 0), (0, 2), (0, 1), (0, 3), (0, 0)]
+    order = chips(far_blocks + direct_blocks + rest_blocks)
     arrivals = chips([(s, f) for s in (0, 3, 1, 2) for f in (0, 2, 3, 1)])
     grads = jnp.concatenate([cotangent, other_cotangent], axis=1)
 
-    ready = (windows, scale, spread, grads, order, arrivals)
-    windows, scale, spread, grads, order, arrivals = lax.optimization_barrier(ready)
-    back_codes, code_grads = codes_of(windows, down, up, scale)
+    ready = (grad_windows, scale, spread, grads, order, arrivals)
+    grad_windows, scale, spread, grads, order, arrivals = lax.optimization_barrier(ready)
+    code_grads = code_grads_of(grad_windows, up, scale)
     own_returned, for_other = returned_of(core_index, code_grads, down)
     returned = (own_returned, send(for_other, OTHER_CORE))
 
-    def partial_sums(base, blocks, received=(), takes=(), grads=grads):
-        return backward_product(order, base, blocks, grads, weight, other_weight, spread, returned, received, takes)
-
-    far_up = send(partial_sums(0, 2), SECOND_UP)
-    far_down = send(partial_sums(2, 2), SECOND_DOWN)
+    def partial_sums(order, base, sizes):
+        return backward_product(order, base, sizes, grads, weight, other_weight, spread, returned)
+
+    far_up, far_down = partial_sums(order, 0, (2, 2))
+    order, far_up, far_down = lax.optimization_barrier((order, far_up, far_down))
+    far_up, far_down = send(far_up, SECOND_UP), send(far_down, SECOND_DOWN)
+    near_up_b, near_down_a = partial_sums(order, 4, (2, 2))
+    order, near_up_b, near_down_a = lax.optimization_barrier((order, near_up_b, near_down_a))
+    near_up_b, near_down_a = send(near_up_b, SECOND_UP), send(near_down_a, SECOND_DOWN)
+    near_up_a, near_down_b, sums_a, sums_b = partial_sums(order, 8, (2, 2, 2, 2))
+    near_up_a = send(add_rounded(near_up_a, far_up), SECOND_UP)
+    near_down_b = send(add_rounded(near_down_b, far_down), SECOND_DOWN)
+
+    info_later, _ = lax.optimization_barrier((info, sums_a))
     own_out, for_other_out, own_x, for_other_x = forward_product(
-        arrivals, info, pieces, weight, other_weight, window, rows
+        arrivals, info_later, pieces, weight, other_weight, window, rows
     )
     other_x = send(for_other_x, OTHER_CORE)
     other_out = send(for_other_out, OTHER_CORE)
-
-    later_grads, _ = lax.optimization_barrier((grads, own_out))
-    near_up = send(partial_sums(4, 4, (far_up,), ((0, 2),), later_grads), SECOND_UP)
-    near_down = send(partial_sums(8, 4, (far_down,), ((2, 4),), later_grads), SECOND_DOWN)
-
     codes = forward_codes_of(core_index, own_x, other_x, down, scale)
-    adapter_out = adapter_rows_of(codes, up, devices)
-    later_grads, _ = lax.optimization_barrier((grads, adapter_out))
-    sums = partial_sums(12, 4, (near_up, near_down), ((0, 4), (0, 4)), later_grads)
-    far_up = send(sums[0, :half], FIRST_UP)
-    far_down = send(sums[0, half:], FIRST_DOWN)
-    near_up = jnp.concatenate([add_rounded(sums[1, :half], far_up), sums[1, half:]])
-    near_down = jnp.concatenate([sums[2, :half], add_rounded(sums[2, half:], far_down)])
-    near_up = send(near_up, FIRST_UP)
-    near_down = send(near_down, FIRST_DOWN)
-    back_out = add_rounded(cotangent, sums[3], near_up, near_down)
+    leaving = adapter_rows_of(codes, up, devices)
+    arrived = lax.all_to_all(leaving, "tp", split_axis=0, concat_axis=0, tiled=True)
+
+    sums_a, sums_b, _ = lax.optimization_barrier((sums_a, sums_b, leaving))
+    far_sum = send(add_rounded(sums_a[0], near_up_a[0], near_down_a[0]), FIRST_UP)
+    down_sum = send(add_rounded(sums_b[0], near_up_b[0], near_down_b[0]), FIRST_DOWN)
+    up_sum = send(add_rounded(sums_a[1], near_up_a[1], near_down_a[1], far_sum), FIRST_UP)
+    own_sum = total_of(cotangent, sums_b[1], near_up_b[1], near_down_b[1])
+    back_out = add_rounded(own_sum, up_sum, down_sum)
     next_bwd = shifted(back_out, "section", -1)[None]
 
-    adapter_out = lax.all_to_all(adapter_out, "tp", split_axis=0, concat_axis=0, tiled=True)
-    adapter_rows = jnp.dot(put, adapter_out.reshape(devices * rows, BLOCK), preferred_element_type=F32)
-    layer_out = (layer_in.astype(F32) + (own_out + other_out) + adapter_rows).astype(BF16)
+    layer_out = forward_sum(info, layer_in, own_out, other_out, arrived, window)
     next_fwd = shifted(layer_out, "section", 1)[None]
 
-    grad_down, grad_up = gradients_of(windows, back_codes, code_grads, owned)
+    back_codes = back_codes_of(stash_windows, down, scale)
+    grad_down, grad_up = gradients_of(stash_windows, grad_windows, back_codes, code_grads, owned)
     return (next_fwd, next_bwd, grad_down[None], grad_up[None])
 
 

time: 199 us -> 178 us (0.89)
  waiting for transfers between devices: 62.1 us -> 49.8 us
  local copies, waits for them, and re-layouts: 24.9 us -> 15.5 us
  other arithmetic: 9.04 us -> 13.5 us
  starting transfers between devices: 50.9 us -> 46.9 us
  matrix products: 2.77 us -> 0 us
  Pallas kernels: 46.9 us -> 49.2 us
    ppermute x27 -> x26, waiting for transfers between devices: 61.6 us -> 34.7 us  [send(): return lax.ppermute(value, 'tp', pairs)]
    all_to_all x2 -> x3, waiting for transfers between devices: 0.01 us -> 15.1 us  [the longest x1 8.78 us: shards(): lax.all_to_all(grad_windows, 'tp', split_axis=0, concat_axis=0, tiled=True)]
    ppermute x27 -> x26, starting transfers between devices: 34.7 us -> 24.3 us  [send(): return lax.ppermute(value, 'tp', pairs)]
    all_to_all x2 -> x3, starting transfers between devices: 11.4 us -> 19.3 us  [the longest x1 7.78 us: shards(): lax.all_to_all(grad_windows, 'tp', split_axis=0, concat_axis=0, tiled=True)]
    convert_element_type x3 -> x6, other arithmetic: 4.39 us -> 10.4 us  [add_rounded(): return total_of(*values).astype(BF16)]
    unnamed x53 -> x48, local copies, waits for them, and re-layouts: 17.9 us -> 12.1 us
    dot_general x1 -> x0, matrix products: 2.77 us -> none  [shards(): jnp.dot(put, adapter_out.reshape(devices * rows, BLOCK), preferred_elemen...]
    pallas_call x7, Pallas kernels: 21.5 us -> 24 us  [the longest x3 12.9 us: backward_product(): kernel(functools.partial(backward_body, sizes), 'backward_product', (bloc...]
  transfers between devices with their start and end apart: 31 -> 31, of which waited for: 10 -> 9; matrix products, arithmetic and copies ran while one was open for 10% -> 10% of each run, Pallas kernels for 24% -> 28%
where the time goes in v3:
time: 178 us; the launch traced here: 176 us
  waiting for transfers between devices  49.8 us (28%)
  Pallas kernels  49.2 us (28%)
  starting transfers between devices  46.9 us (26%)
  local copies, waits for them, and re-layouts  15.5 us (9%)
  other arithmetic  13.5 us (8%)
    ppermute x26, waiting for transfers between devices, send(): return lax.ppermute(value, 'tp', pairs)  34.7 us
    ppermute x26, starting transfers between devices, send(): return lax.ppermute(value, 'tp', pairs)  24.3 us
    pallas_call x3, Pallas kernels, backward_product(): kernel(functools.partial(backward_body, sizes), 'backward_product', (bloc...  12.9 us
    unnamed x48, local copies, waits for them, and re-layouts  12.1 us
    pallas_call x1, Pallas kernels, forward_product(): kernel(functools.partial(forward_body, window), 'forward_product', (CHIPS...  10.9 us
    convert_element_type x6, other arithmetic, add_rounded(): return total_of(*values).astype(BF16)  10.4 us
    all_to_all x1, waiting for transfers between devices, shards(): lax.all_to_all(grad_windows, 'tp', split_axis=0, concat_axis=0, tiled=True)  8.78 us
    all_to_all x1, starting transfers between devices, shards(): lax.all_to_all(grad_windows, 'tp', split_axis=0, concat_axis=0, tiled=True)  7.78 us
  transfers between devices with their start and end apart: 31, of which 9 were waited for; matrix products, arithmetic and copies ran while one was open for 10% of the time, Pallas kernels for 28%

profile of v3, /device:TPU:0, one launch (start us, length us, event | category | flops | bytes accessed | tf_op | source)
XLA Modules:
  0.0 175.8 jit_solution(13812708630505949819)
XLA Ops:
  0.6 2.9 %collective-permute-start.5 = (bf16[1024,256]{1,0:T(8,128)(2,1)}, bf16[1024,256]{1,0:T(8,128)(2,1)S(1)}, u32[]{:S(2)}, u32[]{:S(2)}) collective-permute-start(bf16[1024,256]{1,0:T(8,128)(2,1)} %bitcast.61), channel_id=1, source_target_pairs={{0,6},{1,25},{2,0},{3,27},{4,2},{5,29},{6,4},{7,31},{8,14},{9,1},{... | collective-permute-start | bytes 1572872 | tf_op jit(solution)/shard_map/ppermute | solution.py:42
  4.4 1.7 slots.1.info_ref
  6.1 1.0 copy-done.4
  7.8 1.0 copy-done.16
  8.9 3.3 %windows.1 = (bf16[32,64,256]{2,1,0:T(8,128)(2,1)}, bf16[32,64,256]{2,1,0:T(8,128)(2,1)}) custom-call(s32[320]{0:T(512)S(1)} %copy-done.14, bf16[1024,256]{1,0:T(8,128)(2,1)S(1)} %bitcast.67, bf16[1024,256]{1,0:T(8,128)(2,1)S(1)} %bitcast.60), custom_call_target="tpu_custom_call" | custom-call | flops 2000000000 | bytes 4194304 | tf_op jit(solution)/shard_map/windows/pallas_call | solution.py:133
  12.2 7.8 %all-to-all-start = ((bf16[32,64,256]{2,1,0:T(8,128)(2,1)}), bf16[32,64,256]{2,1,0:T(8,128)(2,1)}, u32[]{:S(2)}, u32[]{:S(2)}) async-start(bf16[32,64,256]{2,1,0:T(8,128)(2,1)} %get-tuple-element.39), calls=%async_computation | async-start | bytes 2097152 | tf_op jit(solution)/shard_map/all_to_all | solution.py:554
  20.0 3.1 %dynamic-slice_bitcast_fusion = bf16[16,256,256]{2,1,0:T(8,128)(2,1)} fusion(bf16[16,2,256,256]{3,2,1,0:T(8,128)(2,1)} %bitcast.50, s32[]{:T(128)S(6)} %select_n.133), kind=kLoop, calls=%fused_computation.2 | loop fusion | bytes 4194308 | tf_op jit(solution)/shard_map/jit(dynamic_index_in_dim)/squeeze | solution.py:548
  24.4 1.1 pad_maximum_fusion.1.rest_2_
  25.5 1.7 collective-permute-start.8
  27.2 1.3 pad_maximum_fusion.grad_ref
  28.5 8.8 %all-to-all-done.windows_ref.grad_ref = bf16[32,64,256]{2,1,0:T(8,128)(2,1)} async-done(((bf16[32,64,256]{2,1,0:T(8,128)(2,1)}), bf16[32,64,256]{2,1,0:T(8,128)(2,1)}, u32[]{:S(2)}, u32[]{:S(2)}) %all-to-all-start) | async-done | bytes 1048608 | tf_op jit(solution)/shard_map/all_to_all | solution.py:554
  37.3 2.2 %copy-done.3 = bf16[1,2,128,8192]{3,2,1,0:T(8,128)(2,1)S(1)} copy-done((bf16[1,2,128,8192]{3,2,1,0:T(8,128)(2,1)S(1)}, bf16[1,2,128,8192]{3,2,1,0:T(8,128)(2,1)}, u32[]{:S(2)}) %copy-start.3) | copy-done | bytes 4194328
  39.5 3.5 %code_grads.1.grads_ref = bf16[64,256]{1,0:T(8,128)(2,1)S(1)} custom-call(bf16[32,64,256]{2,1,0:T(8,128)(2,1)} %all-to-all-done.windows_ref.grad_ref, bf16[2,128,8192]{2,1,0:T(8,128)(2,1)S(1)} %bitcast.56, f32[64,256]{1,0:T(8,128)S(1)} %and_select_fusion.scale_ref), custom_call_target="tpu_custom_call" | custom-call | flops 1000000000 | bytes 65536 | tf_op jit(solution)/shard_map/code_grads/pallas_call | solution.py:174
  43.0 1.8 %returned.1 = (bf16[16,64,256]{2,1,0:T(8,128)(2,1)S(1)}, bf16[16,64,256]{2,1,0:T(8,128)(2,1)S(1)}) custom-call(s32[1]{0:T(128)} %bitcast.7.core_ref, bf16[64,256]{1,0:T(8,128)(2,1)S(1)} %code_grads.1.grads_ref, bf16[2,16,2,256,128]{4,3,2,1,0:T(8,128)(2,1)S(1)} %bitcast.45, bf16[2,16,2,256,128]{4,3,2,1,0:T(8,128)(2,1)S(1)} %bitcast.46), custom_call_target="tpu_custom_call" | custom-call | flops 1000000000 | bytes 2097152 | tf_op jit(solution)/shard_map/returned/pallas_call | solution.py:246
  47.8 3.0 %backward_product.3 = (bf16[2,1024,256]{2,1,0:T(8,128)(2,1)S(1)}, bf16[2,1024,256]{2,1,0:T(8,128)(2,1)S(1)}) custom-call(s32[18]{0:T(128)S(1)} %add_add_fusion.order_ref, bf16[1024,512]{1,0:T(8,128)(2,1)S(1)} %pad_maximum_fusion.grad_ref, bf16[16,2,256,256]{3,2,1,0:T(8,128)(2,1)S(1)} %bitcast.51, ...), custom_call_target="tpu_custom_call" | custom-call | flops 1360000000 | bytes 4194304 | tf_op jit(solution)/shard_map/backward_product/pallas_call | solution.py:476
  51.5 3.0 %collective-permute-done.9.rest_6_ = bf16[1024,256]{1,0:T(8,128)(2,1)S(1)} collective-permute-done((bf16[1024,256]{1,0:T(8,128)(2,1)S(1)}, bf16[1024,256]{1,0:T(8,128)(2,1)S(1)}, u32[]{:S(2)}, u32[]{:S(2)}) %collective-permute-start.9) | collective-permute-done | bytes 524320 | tf_op jit(solution)/shard_map/ppermute | solution.py:42
  54.5 2.0 %collective-permute-start.12 = (bf16[1024,256]{1,0:T(8,128)(2,1)S(1)}, bf16[1024,256]{1,0:T(8,128)(2,1)S(1)}, u32[]{:S(2)}, u32[]{:S(2)}) collective-permute-start(bf16[1024,256]{1,0:T(8,128)(2,1)S(1)} %collective-permute-done.9.rest_6_), channel_id=1, source_target_pairs={{0,24},{1,7},{2,26},{3,1},{4,28},{5,3},{6,30},{7,5},{8,0},{9,15},{... | collective-permute-start | bytes 1572872 | tf_op jit(solution)/shard_map/ppermute | solution.py:42
  56.5 5.6 %collective-permute-done.4.rest_1_ = bf16[1024,256]{1,0:T(8,128)(2,1)S(1)} collective-permute-done((bf16[1024,256]{1,0:T(8,128)(2,1)S(1)}, bf16[1024,256]{1,0:T(8,128)(2,1)S(1)}, u32[]{:S(2)}, u32[]{:S(2)}) %collective-permute-start.4) | collective-permute-done | bytes 524320 | tf_op jit(solution)/shard_map/ppermute | solution.py:42
  62.1 1.3 collective-permute-start.11
  64.2 4.3 %backward_product.4 = (bf16[2,1024,256]{2,1,0:T(8,128)(2,1)}, bf16[2,1024,256]{2,1,0:T(8,128)(2,1)}) custom-call(s32[18]{0:T(128)S(1)} %add_add_fusion.order_ref, bf16[1024,512]{1,0:T(8,128)(2,1)S(1)} %pad_maximum_fusion.grad_ref, bf16[16,2,256,256]{3,2,1,0:T(8,128)(2,1)S(1)} %bitcast.52, ...), custom_call_target="tpu_custom_call" | custom-call | flops 1360000000 | bytes 4194304 | tf_op jit(solution)/shard_map/backward_product/pallas_call | solution.py:476
  68.5 2.0 %collective-permute-start.7 = (bf16[1024,256]{1,0:T(8,128)(2,1)S(1)}, bf16[1024,256]{1,0:T(8,128)(2,1)S(1)}, u32[]{:S(2)}, u32[]{:S(2)}) collective-permute-start(bf16[1024,256]{1,0:T(8,128)(2,1)S(1)} %collective-permute-done.4.rest_1_), channel_id=1, source_target_pairs={{0,8},{1,3},{2,10},{3,5},{4,12},{5,7},{6,14},{7,1},{8,16},{9,11},{... | collective-permute-start | bytes 1572872 | tf_op jit(solution)/shard_map/ppermute | solution.py:42
  71.3 1.2 collective-permute-start.13
  72.5 5.6 %backward_product.5 = (bf16[2,1024,256]{2,1,0:T(8,128)(2,1)S(1)}, bf16[2,1024,256]{2,1,0:T(8,128)(2,1)S(1)}, bf16[2,1024,256]{2,1,0:T(8,128)(2,1)S(1)}, bf16[2,1024,256]{2,1,0:T(8,128)(2,1)S(1)}) custom-call(s32[18]{0:T(128)S(1)} %add_add_fusion.order_ref, bf16[1024,512]{1,0:T(8,128)(2,1)S(1)} %pad_maximum_fusion.grad_ref, ...), custom_call_target="tpu_custom_call" | custom-call | flops 2720000000 | bytes 8388608 | tf_op jit(solution)/shard_map/backward_product/pallas_call | solution.py:476
  79.6 1.3 add_convert_fusion
  80.9 8.8 %collective-permute-done.7.rest_4_ = bf16[1024,256]{1,0:T(8,128)(2,1)S(1)} collective-permute-done((bf16[1024,256]{1,0:T(8,128)(2,1)S(1)}, bf16[1024,256]{1,0:T(8,128)(2,1)S(1)}, u32[]{:S(2)}, u32[]{:S(2)}) %collective-permute-start.7) | collective-permute-done | bytes 524320 | tf_op jit(solution)/shard_map/ppermute | solution.py:42
  89.7 3.2 %collective-permute-start.23 = (bf16[2,1024,256]{2,1,0:T(8,128)(2,1)}, bf16[2,1024,256]{2,1,0:T(8,128)(2,1)}, u32[]{:S(2)}, u32[]{:S(2)}) collective-permute-start(bf16[2,1024,256]{2,1,0:T(8,128)(2,1)} %get-tuple-element.70), channel_id=1, source_target_pairs={{0,24},{1,7},{2,26},{3,1},{4,28},{5,3},{6,30},{7,5},{8,0},{9,15},{... | collective-permute-start | bytes 3145736 | tf_op jit(solution)/shard_map/ppermute | solution.py:42
  93.0 10.9 %forward_product.1 = (f32[1024,256]{1,0:T(8,128)S(1)}, f32[1024,256]{1,0:T(8,128)}, bf16[16,64,256]{2,1,0:T(8,128)(2,1)S(1)}, bf16[16,64,256]{2,1,0:T(8,128)(2,1)S(1)}) custom-call(s32[18]{0:T(128)S(1)} %add_add_fusion.1.order_ref, s32[320]{0:T(512)S(1)} %copy-done.15, bf16[1024,256]{1,0:T(8,128)(2,1)S(1)} %bitcast.65, ...), custom_call_target="tpu_custom_call" | custom-call | flops 8999999488 | bytes 4194304 | tf_op jit(solution)/shard_map/forward_product/pallas_call | solution.py:436
  103.9 1.3 add_convert_fusion.1
  105.2 3.2 %collective-permute-start.20 = (bf16[2,1024,256]{2,1,0:T(8,128)(2,1)}, bf16[2,1024,256]{2,1,0:T(8,128)(2,1)}, u32[]{:S(2)}, u32[]{:S(2)}) collective-permute-start(bf16[2,1024,256]{2,1,0:T(8,128)(2,1)} %add_convert_fusion.1), channel_id=1, source_target_pairs={{0,24},{1,7},{2,26},{3,1},{4,28},{5,3},{6,30},{7,5},{8,0},{9,15},{... | collective-permute-start | bytes 3145736 | tf_op jit(solution)/shard_map/ppermute | solution.py:42
  108.4 1.3 forward_codes.1.codes_ref
  109.8 2.5 %adapter_rows.1 = bf16[32,64,256]{2,1,0:T(8,128)(2,1)} custom-call(bf16[64,256]{1,0:T(8,128)(2,1)S(1)} %forward_codes.1.codes_ref, bf16[2,128,8192]{2,1,0:T(8,128)(2,1)S(1)} %bitcast.57), custom_call_target="tpu_custom_call" | custom-call | flops 1000000000 | bytes 2097152 | tf_op jit(solution)/shard_map/adapter_rows/pallas_call | solution.py:302
  112.3 4.1 %all-to-all-start.1 = ((bf16[32,64,256]{2,1,0:T(8,128)(2,1)}), bf16[32,64,256]{2,1,0:T(8,128)(2,1)S(1)}, u32[]{:S(2)}, u32[]{:S(2)}) async-start(bf16[32,64,256]{2,1,0:T(8,128)(2,1)} %adapter_rows.1), calls=%async_computation.1 | async-start | bytes 2097152 | tf_op jit(solution)/shard_map/all_to_all | solution.py:623
  117.3 1.4 fusion.4
  119.6 12.6 %collective-permute-done.20 = bf16[2,1024,256]{2,1,0:T(8,128)(2,1)} collective-permute-done((bf16[2,1024,256]{2,1,0:T(8,128)(2,1)}, bf16[2,1024,256]{2,1,0:T(8,128)(2,1)}, u32[]{:S(2)}, u32[]{:S(2)}) %collective-permute-start.20) | collective-permute-done | bytes 1048608 | tf_op jit(solution)/shard_map/ppermute | solution.py:42
  132.2 2.2 %fusion.5 = bf16[1024,256]{1,0:T(8,128)(2,1)} fusion(bf16[2,1024,256]{2,1,0:T(8,128)(2,1)} %collective-permute-done.20, bf16[2,1024,256]{2,1,0:T(8,128)(2,1)} %collective-permute-done.18, bf16[2,1024,256]{2,1,0:T(8,128)(2,1)S(1)} %copy-done.7), kind=kLoop, calls=%fused_computation.16 | loop fusion | flops 1572864 | bytes 2097152 | tf_op jit(solution)/shard_map/convert_element_type | solution.py:502
  134.4 2.9 %collective-permute-done.24 = bf16[1024,256]{1,0:T(8,128)(2,1)S(1)} collective-permute-done((bf16[1024,256]{1,0:T(8,128)(2,1)S(1)}, bf16[1024,256]{1,0:T(8,128)(2,1)S(1)}, u32[]{:S(2)}, u32[]{:S(2)}) %collective-permute-start.24) | collective-permute-done | bytes 524320 | tf_op jit(solution)/shard_map/ppermute | solution.py:42
  137.2 2.3 %fusion.3 = bf16[1024,256]{1,0:T(8,128)(2,1)} fusion(bf16[1024,256]{1,0:T(8,128)(2,1)S(1)} %collective-permute-done.24, bf16[2,1024,256]{2,1,0:T(8,128)(2,1)} %collective-permute-done.23, bf16[2,1024,256]{2,1,0:T(8,128)(2,1)} %collective-permute-done.22, bf16[2,1024,256]{2,1,0:T(8,128)(2,1)S(1)} %copy-done.9), kind=kLoop, calls=%fused_computation.12 | loop fusion | flops 2097152 | bytes 2621440 | tf_op jit(solution)/shard_map/convert_element_type | solution.py:502
  139.5 7.4 %all-to-all-start.2 = ((bf16[32,64,256]{2,1,0:T(8,128)(2,1)}), bf16[32,64,256]{2,1,0:T(8,128)(2,1)S(1)}, u32[]{:S(2)}, u32[]{:S(2)}) async-start(bf16[32,64,256]{2,1,0:T(8,128)(2,1)} %get-tuple-element.71), calls=%async_computation.2 | async-start | bytes 2097152 | tf_op jit(solution)/shard_map/all_to_all | solution.py:557
  146.9 1.2 copy-done.11
  148.2 1.0 copy-done.13
  149.2 3.5 %forward_sum.1 = bf16[1024,256]{1,0:T(8,128)(2,1)} custom-call(s32[320]{0:T(512)S(1)} %copy-done.15, bf16[1024,256]{1,0:T(8,128)(2,1)S(1)} %bitcast.66, f32[1024,256]{1,0:T(8,128)S(1)} %copy-done.11, f32[1024,256]{1,0:T(8,128)} %collective-permute-done.15.other_ref, bf16[32,64,256]{2,1,0:T(8,128)(2,1)S(1)} %all-to-all-done.1.adapter_ref), custom_call_target="tpu_custom_call" | custom-call | flops 100000000 | bytes 1048576 | tf_op jit(solution)/shard_map/forward_sum/pallas_call | solution.py:334
  152.7 1.6 collective-permute-start.17
  154.3 1.9 %fusion.2 = bf16[1024,256]{1,0:T(8,128)(2,1)S(1)} fusion(bf16[1024,256]{1,0:T(8,128)(2,1)} %collective-permute-done.26, bf16[1024,256]{1,0:T(8,128)(2,1)} %collective-permute-done.25, bf16[2,1024,256]{2,1,0:T(8,128)(2,1)} %collective-permute-done.20, bf16[2,1024,256]{2,1,0:T(8,128)(2,1)} %collective-permute-done.18, bf16[2,1024,256]{2,1,0:T(8,128)(2,1)S(1)} %copy-done.7, ...), kind=kLoop, calls=%fused_computation.8 | loop fusion | flops 3145728 | bytes 3670016 | tf_op jit(solution)/shard_map/convert_element_type | solution.py:502
  156.2 1.7 collective-permute-start.27
  157.9 6.3 %all-to-all-done.2.windows_ref.stash_ref = bf16[32,64,256]{2,1,0:T(8,128)(2,1)S(1)} async-done(((bf16[32,64,256]{2,1,0:T(8,128)(2,1)}), bf16[32,64,256]{2,1,0:T(8,128)(2,1)S(1)}, u32[]{:S(2)}, u32[]{:S(2)}) %all-to-all-start.2) | async-done | bytes 1048608 | tf_op jit(solution)/shard_map/all_to_all | solution.py:557
  164.3 2.2 %copy-done.1 = bf16[1,2,8192,128]{3,2,1,0:T(8,128)(2,1)S(1)} copy-done((bf16[1,2,8192,128]{3,2,1,0:T(8,128)(2,1)S(1)}, bf16[1,2,8192,128]{3,2,1,0:T(8,128)(2,1)}, u32[]{:S(2)}) %copy-start.1) | copy-done | bytes 4194328
  166.4 1.6 back_codes.1.codes_ref
  168.0 6.2 %gradients.1 = (bf16[2,8192,128]{2,1,0:T(8,128)(2,1)}, bf16[2,128,8192]{2,1,0:T(8,128)(2,1)}) custom-call(bf16[32,64,256]{2,1,0:T(8,128)(2,1)S(1)} %all-to-all-done.2.windows_ref.stash_ref, bf16[32,64,256]{2,1,0:T(8,128)(2,1)} %all-to-all-done.windows_ref.grad_ref, bf16[64,256]{1,0:T(8,128)(2,1)S(1)} %back_codes.1.codes_ref, ...), custom_call_target="tpu_custom_call" | custom-call | flops 2000000000 | bytes 16777216 | tf_op jit(solution)/shard_map/gradients/pallas_call | solution.py:362
  (99 shorter events, 12.9 us)
Async XLA Ops:
  0.6 23.7 %collective-permute-start.5 = (bf16[1024,256]{1,0:T(8,128)(2,1)}, bf16[1024,256]{1,0:T(8,128)(2,1)S(1)}, u32[]{:S(2)}, u32[]{:S(2)}) collective-permute-start(bf16[1024,256]{1,0:T(8,128)(2,1)} %bitcast.61), channel_id=1, source_target_pairs={{0,6},{1,25},{2,0},{3,27},{4,2},{5,29},{6,4},{7,31},{8,14},{9,1},{... | collective-permute-start | bytes 1572872 | tf_op jit(solution)/shard_map/ppermute | solution.py:42
  3.5 20.8 %collective-permute-start.3 = (bf16[1024,256]{1,0:T(8,128)(2,1)}, bf16[1024,256]{1,0:T(8,128)(2,1)S(1)}, u32[]{:S(2)}, u32[]{:S(2)}) collective-permute-start(bf16[1024,256]{1,0:T(8,128)(2,1)} %bitcast.62), channel_id=1, source_target_pairs={{0,2},{1,9},{2,4},{3,11},{4,6},{5,13},{6,0},{7,15},{8,10},{9,17},{... | collective-permute-start | bytes 1572872 | tf_op jit(solution)/shard_map/ppermute | solution.py:42
  3.5 23.7 %collective-permute-start = (bf16[1024,256]{1,0:T(8,128)(2,1)}, bf16[1024,256]{1,0:T(8,128)(2,1)}, u32[]{:S(2)}, u32[]{:S(2)}) collective-permute-start(bf16[1024,256]{1,0:T(8,128)(2,1)} %bitcast.58), channel_id=1, source_target_pairs={{0,1},{1,0},{2,3},{3,2},{4,5},{5,4},{6,7},{7,6},{8,9},{9,8},{10,11... | collective-permute-start | bytes 1572872 | tf_op jit(solution)/shard_map/ppermute | solution.py:42
  12.2 25.1 %all-to-all-start = ((bf16[32,64,256]{2,1,0:T(8,128)(2,1)}), bf16[32,64,256]{2,1,0:T(8,128)(2,1)}, u32[]{:S(2)}, u32[]{:S(2)}) async-start(bf16[32,64,256]{2,1,0:T(8,128)(2,1)} %get-tuple-element.39), calls=%async_computation | async-start | bytes 2097152 | tf_op jit(solution)/shard_map/all_to_all | solution.py:554
  20.0 3.4 %copy-start.15 = (s32[320]{0:T(512)S(1)}, s32[320]{0:T(512)}, u32[]{:S(2)}) copy-start(s32[320]{0:T(512)} %slots.1.info_ref) | copy-start | bytes 3844
  20.0 4.0 %copy-start.19 = (s32[16]{0:T(128)S(1)}, s32[16]{0:T(128)}, u32[]{:S(2)}) copy-start(s32[16]{0:T(128)} %constant.141.clone) | copy-start | bytes 196
  20.0 4.0 %copy-start.20 = (s32[16]{0:T(128)S(1)}, s32[16]{0:T(128)}, u32[]{:S(2)}) copy-start(s32[16]{0:T(128)} %constant.140.clone) | copy-start | bytes 196
  20.0 4.0 %copy-start.21 = (s32[16]{0:T(128)S(1)}, s32[16]{0:T(128)}, u32[]{:S(2)}) copy-start(s32[16]{0:T(128)} %constant.139.clone) | copy-start | bytes 196
  20.0 4.0 %copy-start.22 = (s32[16]{0:T(128)S(1)}, s32[16]{0:T(128)}, u32[]{:S(2)}) copy-start(s32[16]{0:T(128)} %constant.138.clone) | copy-start | bytes 196
  23.1 23.7 %collective-permute-start.1 = (bf16[16,256,256]{2,1,0:T(8,128)(2,1)}, bf16[16,256,256]{2,1,0:T(8,128)(2,1)S(1)}, u32[]{:S(2)}, u32[]{:S(2)}) collective-permute-start(bf16[16,256,256]{2,1,0:T(8,128)(2,1)} %dynamic-slice_bitcast_fusion), channel_id=1, source_target_pairs={{0,1},{1,0},{2,3},{3,2},{4,5},{5,4},{6,7},{7,6},{8,9},{9,8},{10,11... | collective-permute-start | bytes 6291464 | tf_op jit(solution)/shard_map/ppermute | solution.py:42
  24.4 2.8 %copy-start.17 = (bf16[1024,256]{1,0:T(8,128)(2,1)}, bf16[1024,256]{1,0:T(8,128)(2,1)S(1)}, u32[]{:S(2)}) copy-start(bf16[1024,256]{1,0:T(8,128)(2,1)S(1)} %collective-permute-done.3) | copy-start | bytes 1572868
  25.5 37.9 %collective-permute-start.8 = (bf16[2,1024,256]{2,1,0:T(8,128)(2,1)}, bf16[2,1024,256]{2,1,0:T(8,128)(2,1)}, u32[]{:S(2)}, u32[]{:S(2)}) collective-permute-start(bf16[2,1024,256]{2,1,0:T(8,128)(2,1)} %pad_maximum_fusion.1.rest_2_), channel_id=1, source_target_pairs={{0,8},{1,3},{2,10},{3,5},{4,12},{5,7},{6,14},{7,1},{8,16},{9,11},{... | collective-permute-start | bytes 3145736 | tf_op jit(solution)/shard_map/ppermute | solution.py:42
  37.3 2.2 %copy-start.3 = (bf16[1,2,128,8192]{3,2,1,0:T(8,128)(2,1)S(1)}, bf16[1,2,128,8192]{3,2,1,0:T(8,128)(2,1)}, u32[]{:S(2)}) copy-start(bf16[1,2,128,8192]{3,2,1,0:T(8,128)(2,1)} %param.19) | copy-start | bytes 12582916
  39.5 3.5 %copy-start = (bf16[1,2,8192,128]{3,2,1,0:T(8,128)(2,1)S(1)}, bf16[1,2,8192,128]{3,2,1,0:T(8,128)(2,1)}, u32[]{:S(2)}) copy-start(bf16[1,2,8192,128]{3,2,1,0:T(8,128)(2,1)} %param.18) | copy-start | bytes 12582916
  43.0 2.3 %copy-start.12 = (bf16[1,1024,256]{2,1,0:T(8,128)(2,1)S(1)}, bf16[1,1024,256]{2,1,0:T(8,128)(2,1)}, u32[]{:S(2)}) copy-start(bf16[1,1024,256]{2,1,0:T(8,128)(2,1)} %param.14) | copy-start | bytes 1572868
  43.0 3.1 %copy-start.18 = (bf16[1024,256]{1,0:T(8,128)(2,1)S(1)}, bf16[1024,256]{1,0:T(8,128)(2,1)}, u32[]{:S(2)}) copy-start(bf16[1024,256]{1,0:T(8,128)(2,1)} %copy-done.17) | copy-start | bytes 1572868
  43.0 4.8 %copy-start.2 = (bf16[1,8192,256]{2,1,0:T(8,128)(2,1)S(1)}, bf16[1,8192,256]{2,1,0:T(8,128)(2,1)}, u32[]{:S(2)}) copy-start(bf16[1,8192,256]{2,1,0:T(8,128)(2,1)} %param.17) | copy-start | bytes 12582916
  44.9 2.9 %collective-permute-start.2 = (bf16[16,64,256]{2,1,0:T(8,128)(2,1)S(1)}, bf16[16,64,256]{2,1,0:T(8,128)(2,1)S(1)}, u32[]{:S(2)}, u32[]{:S(2)}) collective-permute-start(bf16[16,64,256]{2,1,0:T(8,128)(2,1)S(1)} %get-tuple-element.49), channel_id=1, source_target_pairs={{0,1},{1,0},{2,3},{3,2},{4,5},{5,4},{6,7},{7,6},{8,9},{9,8},{10,11... | collective-permute-start | bytes 1572872 | tf_op jit(solution)/shard_map/ppermute | solution.py:42
  45.3 9.2 %collective-permute-start.9 = (bf16[1024,256]{1,0:T(8,128)(2,1)S(1)}, bf16[1024,256]{1,0:T(8,128)(2,1)S(1)}, u32[]{:S(2)}, u32[]{:S(2)}) collective-permute-start(bf16[1024,256]{1,0:T(8,128)(2,1)S(1)} %bitcast.63), channel_id=1, source_target_pairs={{0,24},{1,7},{2,26},{3,1},{4,28},{5,3},{6,30},{7,5},{8,0},{9,15},{... | collective-permute-start | bytes 1572872 | tf_op jit(solution)/shard_map/ppermute | solution.py:42
  46.1 16.0 %collective-permute-start.4 = (bf16[1024,256]{1,0:T(8,128)(2,1)S(1)}, bf16[1024,256]{1,0:T(8,128)(2,1)S(1)}, u32[]{:S(2)}, u32[]{:S(2)}) collective-permute-start(bf16[1024,256]{1,0:T(8,128)(2,1)S(1)} %copy-done.18), channel_id=1, source_target_pairs={{0,2},{1,9},{2,4},{3,11},{4,6},{5,13},{6,0},{7,15},{8,10},{9,17},{... | collective-permute-start | bytes 1572872 | tf_op jit(solution)/shard_map/ppermute | solution.py:42
  46.9 15.2 %collective-permute-start.6 = (bf16[1024,256]{1,0:T(8,128)(2,1)S(1)}, bf16[1024,256]{1,0:T(8,128)(2,1)S(1)}, u32[]{:S(2)}, u32[]{:S(2)}) collective-permute-start(bf16[1024,256]{1,0:T(8,128)(2,1)S(1)} %bitcast.64), channel_id=1, source_target_pairs={{0,8},{1,3},{2,10},{3,5},{4,12},{5,7},{6,14},{7,1},{8,16},{9,11},{... | collective-permute-start | bytes 1572872 | tf_op jit(solution)/shard_map/ppermute | solution.py:42
  50.8 28.2 %collective-permute-start.21 = (bf16[2,1024,256]{2,1,0:T(8,128)(2,1)S(1)}, bf16[2,1024,256]{2,1,0:T(8,128)(2,1)S(1)}, u32[]{:S(2)}, u32[]{:S(2)}) collective-permute-start(bf16[2,1024,256]{2,1,0:T(8,128)(2,1)S(1)} %get-tuple-element.69), channel_id=1, source_target_pairs={{0,8},{1,3},{2,10},{3,5},{4,12},{5,7},{6,14},{7,1},{8,16},{9,11},{... | collective-permute-start | bytes 3145736 | tf_op jit(solution)/shard_map/ppermute | solution.py:42
  54.5 14.0 %collective-permute-start.12 = (bf16[1024,256]{1,0:T(8,128)(2,1)S(1)}, bf16[1024,256]{1,0:T(8,128)(2,1)S(1)}, u32[]{:S(2)}, u32[]{:S(2)}) collective-permute-start(bf16[1024,256]{1,0:T(8,128)(2,1)S(1)} %collective-permute-done.9.rest_6_), channel_id=1, source_target_pairs={{0,24},{1,7},{2,26},{3,1},{4,28},{5,3},{6,30},{7,5},{8,0},{9,15},{... | collective-permute-start | bytes 1572872 | tf_op jit(solution)/shard_map/ppermute | solution.py:42
  62.1 9.2 %collective-permute-start.10 = (bf16[1024,256]{1,0:T(8,128)(2,1)S(1)}, bf16[1024,256]{1,0:T(8,128)(2,1)S(1)}, u32[]{:S(2)}, u32[]{:S(2)}) collective-permute-start(bf16[1024,256]{1,0:T(8,128)(2,1)S(1)} %collective-permute-done.4.rest_1_), channel_id=1, source_target_pairs={{0,24},{1,7},{2,26},{3,1},{4,28},{5,3},{6,30},{7,5},{8,0},{9,15},{... | collective-permute-start | bytes 1572872 | tf_op jit(solution)/shard_map/ppermute | solution.py:42
  62.1 27.6 %collective-permute-start.11 = (bf16[2,1024,256]{2,1,0:T(8,128)(2,1)}, bf16[2,1024,256]{2,1,0:T(8,128)(2,1)S(1)}, u32[]{:S(2)}, u32[]{:S(2)}) collective-permute-start(bf16[2,1024,256]{2,1,0:T(8,128)(2,1)} %pad_maximum_fusion.1.rest_2_), channel_id=1, source_target_pairs={{0,24},{1,7},{2,26},{3,1},{4,28},{5,3},{6,30},{7,5},{8,0},{9,15},{... | collective-permute-start | bytes 3145736 | tf_op jit(solution)/shard_map/ppermute | solution.py:42
  63.4 29.5 %collective-permute-start.14 = (bf16[2,1024,256]{2,1,0:T(8,128)(2,1)}, bf16[2,1024,256]{2,1,0:T(8,128)(2,1)S(1)}, u32[]{:S(2)}, u32[]{:S(2)}) collective-permute-start(bf16[2,1024,256]{2,1,0:T(8,128)(2,1)} %collective-permute-done.8.rest_5_), channel_id=1, source_target_pairs={{0,8},{1,3},{2,10},{3,5},{4,12},{5,7},{6,14},{7,1},{8,16},{9,11},{... | collective-permute-start | bytes 3145736 | tf_op jit(solution)/shard_map/ppermute | solution.py:42
  68.5 21.3 %collective-permute-start.7 = (bf16[1024,256]{1,0:T(8,128)(2,1)S(1)}, bf16[1024,256]{1,0:T(8,128)(2,1)S(1)}, u32[]{:S(2)}, u32[]{:S(2)}) collective-permute-start(bf16[1024,256]{1,0:T(8,128)(2,1)S(1)} %collective-permute-done.4.rest_1_), channel_id=1, source_target_pairs={{0,8},{1,3},{2,10},{3,5},{4,12},{5,7},{6,14},{7,1},{8,16},{9,11},{... | collective-permute-start | bytes 1572872 | tf_op jit(solution)/shard_map/ppermute | solution.py:42
  71.3 21.7 %collective-permute-start.13 = (bf16[1024,256]{1,0:T(8,128)(2,1)S(1)}, bf16[1024,256]{1,0:T(8,128)(2,1)S(1)}, u32[]{:S(2)}, u32[]{:S(2)}) collective-permute-start(bf16[1024,256]{1,0:T(8,128)(2,1)S(1)} %collective-permute-done.10.rest_7_), channel_id=1, source_target_pairs={{0,24},{1,7},{2,26},{3,1},{4,28},{5,3},{6,30},{7,5},{8,0},{9,15},{... | collective-permute-start | bytes 1572872 | tf_op jit(solution)/shard_map/ppermute | solution.py:42
  79.1 1.8 %copy-start.8 = (bf16[2,1024,256]{2,1,0:T(8,128)(2,1)}, bf16[2,1024,256]{2,1,0:T(8,128)(2,1)S(1)}, u32[]{:S(2)}) copy-start(bf16[2,1024,256]{2,1,0:T(8,128)(2,1)S(1)} %get-tuple-element.67) | copy-start | bytes 3145732
  79.1 24.8 %collective-permute-start.19 = (bf16[2,1024,256]{2,1,0:T(8,128)(2,1)S(1)}, bf16[2,1024,256]{2,1,0:T(8,128)(2,1)S(1)}, u32[]{:S(2)}, u32[]{:S(2)}) collective-permute-start(bf16[2,1024,256]{2,1,0:T(8,128)(2,1)S(1)} %get-tuple-element.66), channel_id=1, source_target_pairs={{0,24},{1,7},{2,26},{3,1},{4,28},{5,3},{6,30},{7,5},{8,0},{9,15},{... | collective-permute-start | bytes 3145736 | tf_op jit(solution)/shard_map/ppermute | solution.py:42
  89.7 29.8 %collective-permute-start.18 = (bf16[2,1024,256]{2,1,0:T(8,128)(2,1)}, bf16[2,1024,256]{2,1,0:T(8,128)(2,1)}, u32[]{:S(2)}, u32[]{:S(2)}) collective-permute-start(bf16[2,1024,256]{2,1,0:T(8,128)(2,1)} %get-tuple-element.64), channel_id=1, source_target_pairs={{0,8},{1,3},{2,10},{3,5},{4,12},{5,7},{6,14},{7,1},{8,16},{9,11},{... | collective-permute-start | bytes 3145736 | tf_op jit(solution)/shard_map/ppermute | solution.py:42
  89.7 26.6 %collective-permute-start.23 = (bf16[2,1024,256]{2,1,0:T(8,128)(2,1)}, bf16[2,1024,256]{2,1,0:T(8,128)(2,1)}, u32[]{:S(2)}, u32[]{:S(2)}) collective-permute-start(bf16[2,1024,256]{2,1,0:T(8,128)(2,1)} %get-tuple-element.70), channel_id=1, source_target_pairs={{0,24},{1,7},{2,26},{3,1},{4,28},{5,3},{6,30},{7,5},{8,0},{9,15},{... | collective-permute-start | bytes 3145736 | tf_op jit(solution)/shard_map/ppermute | solution.py:42
  93.0 24.3 %collective-permute-start.22 = (bf16[2,1024,256]{2,1,0:T(8,128)(2,1)}, bf16[2,1024,256]{2,1,0:T(8,128)(2,1)}, u32[]{:S(2)}, u32[]{:S(2)}) collective-permute-start(bf16[2,1024,256]{2,1,0:T(8,128)(2,1)} %add_convert_fusion), channel_id=1, source_target_pairs={{0,8},{1,3},{2,10},{3,5},{4,12},{5,7},{6,14},{7,1},{8,16},{9,11},{... | collective-permute-start | bytes 3145736 | tf_op jit(solution)/shard_map/ppermute | solution.py:42
  103.9 5.9 %copy-start.10 = (f32[1024,256]{1,0:T(8,128)}, f32[1024,256]{1,0:T(8,128)S(1)}, u32[]{:S(2)}) copy-start(f32[1024,256]{1,0:T(8,128)S(1)} %get-tuple-element.58.own_ref) | copy-start | bytes 3145732
  103.9 4.5 %collective-permute-start.16 = (bf16[16,64,256]{2,1,0:T(8,128)(2,1)S(1)}, bf16[16,64,256]{2,1,0:T(8,128)(2,1)S(1)}, u32[]{:S(2)}, u32[]{:S(2)}) collective-permute-start(bf16[16,64,256]{2,1,0:T(8,128)(2,1)S(1)} %get-tuple-element.61), channel_id=1, source_target_pairs={{0,1},{1,0},{2,3},{3,2},{4,5},{5,4},{6,7},{7,6},{8,9},{9,8},{10,11... | collective-permute-start | bytes 1572872 | tf_op jit(solution)/shard_map/ppermute | solution.py:42
  105.2 27.0 %collective-permute-start.20 = (bf16[2,1024,256]{2,1,0:T(8,128)(2,1)}, bf16[2,1024,256]{2,1,0:T(8,128)(2,1)}, u32[]{:S(2)}, u32[]{:S(2)}) collective-permute-start(bf16[2,1024,256]{2,1,0:T(8,128)(2,1)} %add_convert_fusion.1), channel_id=1, source_target_pairs={{0,24},{1,7},{2,26},{3,1},{4,28},{5,3},{6,30},{7,5},{8,0},{9,15},{... | collective-permute-start | bytes 3145736 | tf_op jit(solution)/shard_map/ppermute | solution.py:42
  112.3 5.0 %copy-start.9 = (bf16[2,1024,256]{2,1,0:T(8,128)(2,1)S(1)}, bf16[2,1024,256]{2,1,0:T(8,128)(2,1)}, u32[]{:S(2)}) copy-start(bf16[2,1024,256]{2,1,0:T(8,128)(2,1)} %copy-done.8) | copy-start | bytes 3145732
  112.3 19.9 %copy-start.7 = (bf16[2,1024,256]{2,1,0:T(8,128)(2,1)S(1)}, bf16[2,1024,256]{2,1,0:T(8,128)(2,1)}, u32[]{:S(2)}) copy-start(bf16[2,1024,256]{2,1,0:T(8,128)(2,1)} %copy-done.6) | copy-start | bytes 3145732
  112.3 27.2 %all-to-all-start.1 = ((bf16[32,64,256]{2,1,0:T(8,128)(2,1)}), bf16[32,64,256]{2,1,0:T(8,128)(2,1)S(1)}, u32[]{:S(2)}, u32[]{:S(2)}) async-start(bf16[32,64,256]{2,1,0:T(8,128)(2,1)} %adapter_rows.1), calls=%async_computation.1 | async-start | bytes 2097152 | tf_op jit(solution)/shard_map/all_to_all | solution.py:623
  118.7 18.6 %collective-permute-start.24 = (bf16[1024,256]{1,0:T(8,128)(2,1)S(1)}, bf16[1024,256]{1,0:T(8,128)(2,1)S(1)}, u32[]{:S(2)}, u32[]{:S(2)}) collective-permute-start(bf16[1024,256]{1,0:T(8,128)(2,1)S(1)} %fusion.4), channel_id=1, source_target_pairs={{0,2},{1,9},{2,4},{3,11},{4,6},{5,13},{6,0},{7,15},{8,10},{9,17},{... | collective-permute-start | bytes 1572872 | tf_op jit(solution)/shard_map/ppermute | solution.py:42
  119.5 27.4 %collective-permute-start.15 = (f32[1024,256]{1,0:T(8,128)}, f32[1024,256]{1,0:T(8,128)}, u32[]{:S(2)}, u32[]{:S(2)}) collective-permute-start(f32[1024,256]{1,0:T(8,128)} %get-tuple-element.59), channel_id=1, source_target_pairs={{0,1},{1,0},{2,3},{3,2},{4,5},{5,4},{6,7},{7,6},{8,9},{9,8},{10,11... | collective-permute-start | bytes 3145736 | tf_op jit(solution)/shard_map/ppermute | solution.py:42
  134.4 19.9 %collective-permute-start.26 = (bf16[1024,256]{1,0:T(8,128)(2,1)}, bf16[1024,256]{1,0:T(8,128)(2,1)}, u32[]{:S(2)}, u32[]{:S(2)}) collective-permute-start(bf16[1024,256]{1,0:T(8,128)(2,1)} %fusion.5), channel_id=1, source_target_pairs={{0,6},{1,25},{2,0},{3,27},{4,2},{5,29},{6,4},{7,31},{8,14},{9,1},{... | collective-permute-start | bytes 1572872 | tf_op jit(solution)/shard_map/ppermute | solution.py:42
  139.5 14.8 %collective-permute-start.25 = (bf16[1024,256]{1,0:T(8,128)(2,1)}, bf16[1024,256]{1,0:T(8,128)(2,1)}, u32[]{:S(2)}, u32[]{:S(2)}) collective-permute-start(bf16[1024,256]{1,0:T(8,128)(2,1)} %fusion.3), channel_id=1, source_target_pairs={{0,2},{1,9},{2,4},{3,11},{4,6},{5,13},{6,0},{7,15},{8,10},{9,17},{... | collective-permute-start | bytes 1572872 | tf_op jit(solution)/shard_map/ppermute | solution.py:42
  139.5 24.8 %all-to-all-start.2 = ((bf16[32,64,256]{2,1,0:T(8,128)(2,1)}), bf16[32,64,256]{2,1,0:T(8,128)(2,1)S(1)}, u32[]{:S(2)}, u32[]{:S(2)}) async-start(bf16[32,64,256]{2,1,0:T(8,128)(2,1)} %get-tuple-element.71), calls=%async_computation.2 | async-start | bytes 2097152 | tf_op jit(solution)/shard_map/all_to_all | solution.py:557
  149.2 5.1 %copy-start.5 = (bf16[1,1024,256]{2,1,0:T(8,128)(2,1)S(1)}, bf16[1,1024,256]{2,1,0:T(8,128)(2,1)}, u32[]{:S(2)}) copy-start(bf16[1,1024,256]{2,1,0:T(8,128)(2,1)} %param.16) | copy-start | bytes 1572868
  152.7 21.5 %collective-permute-start.17 = (bf16[1024,256]{1,0:T(8,128)(2,1)}, bf16[1024,256]{1,0:T(8,128)(2,1)S(1)}, u32[]{:S(2)}, u32[]{:S(2)}) collective-permute-start(bf16[1024,256]{1,0:T(8,128)(2,1)} %forward_sum.1), channel_id=1, source_target_pairs={{0,32},{32,64},{64,96},{96,0},{1,33},{33,65},{65,97},{97,1},{2,34}... | collective-permute-start | bytes 1572872 | tf_op jit(solution)/shard_map/ppermute | solution.py:48
  156.2 18.0 %collective-permute-start.27 = (bf16[1024,256]{1,0:T(8,128)(2,1)S(1)}, bf16[1024,256]{1,0:T(8,128)(2,1)S(1)}, u32[]{:S(2)}, u32[]{:S(2)}) collective-permute-start(bf16[1024,256]{1,0:T(8,128)(2,1)S(1)} %fusion.2), channel_id=1, source_target_pairs={{0,96},{32,0},{64,32},{96,64},{1,97},{33,1},{65,33},{97,65},{2,98}... | collective-permute-start | bytes 1572872 | tf_op jit(solution)/shard_map/ppermute | solution.py:48
  164.3 2.2 %copy-start.1 = (bf16[1,2,8192,128]{3,2,1,0:T(8,128)(2,1)S(1)}, bf16[1,2,8192,128]{3,2,1,0:T(8,128)(2,1)}, u32[]{:S(2)}) copy-start(bf16[1,2,8192,128]{3,2,1,0:T(8,128)(2,1)} %param.18) | copy-start | bytes 12582916
  (6 other events, 6.0 us)

commit v4 on v3

--- a/solution.py
+++ b/solution.py
@@ -52,7 +52,7 @@
     return pl.BlockSpec(shape, lambda *_: (0,) * len(shape))
 
 
-def kernel(body, name, grid, prefetched, in_specs, outs, flops, scratch=()):
+def kernel(body, name, grid, prefetched, in_specs, outs, flops, scratch=(), vmem=VMEM):
     out_shape = [jax.ShapeDtypeStruct(shape, dtype) for _, shape, dtype in outs]
     size = sum(2 * math.prod(shape) for _, shape, _ in outs)
     return pl.pallas_call(
@@ -65,7 +65,7 @@
             scratch_shapes=list(scratch),
         ),
         out_shape=out_shape,
-        compiler_params=pltpu.CompilerParams(vmem_limit_bytes=VMEM),
+        compiler_params=pltpu.CompilerParams(vmem_limit_bytes=vmem),
         cost_estimate=pl.CostEstimate(flops=flops, bytes_accessed=2 * size, transcendentals=0),
         name=name,
     )
@@ -106,27 +106,25 @@
     return jnp.where(held, rows, 0.0).astype(BF16)
 
 
-def windows_body(adapters, window, each, info_ref, stash_ref, cotangent_ref, stash_out_ref, cotangent_out_ref, wide_ref):
-    tokens = stash_ref.shape[0]
+def windows_body(adapters, window, each, info_ref, in_ref, out_ref, wide_ref):
+    tokens = in_ref.shape[0]
     step = pl.program_id(0)
-    owned = stash_out_ref.shape[1] // window
+    owned = out_ref.shape[1] // window
 
     @pl.when(step == 0)
     def _():
-        wide_ref[:tokens, :BLOCK] = stash_ref[...].astype(F32)
-        wide_ref[:tokens, BLOCK:] = cotangent_ref[...].astype(F32)
+        wide_ref[:tokens] = in_ref[...].astype(F32)
 
     for index in range(each):
         slot = step * each + index
         rows = slot_rows(wide_ref, info_ref[2 * adapters + slot], info_ref[3 * adapters + slot], window)
         low = index % owned * window
-        stash_out_ref[index // owned, low : low + window] = rows[:, :BLOCK]
-        cotangent_out_ref[index // owned, low : low + window] = rows[:, BLOCK:]
-
-
-def windows_of(info, stash, cotangent, adapters, window, rows):
+        out_ref[index // owned, low : low + window] = rows
+
+
+def windows_of(info, values, adapters, window, rows):
     devices = adapters * window // rows
-    tokens = stash.shape[0]
+    tokens = values.shape[0]
     each = 16
     owners = each * window // rows
     out = pl.BlockSpec((owners, rows, BLOCK), lambda i, info: (i, 0, 0))
@@ -135,11 +133,12 @@
         "windows",
         (adapters // each,),
         1,
-        [whole(stash.shape), whole(cotangent.shape)],
-        [(out, (devices, rows, BLOCK), BF16)] * 2,
+        [whole(values.shape)],
+        [(out, (devices, rows, BLOCK), BF16)],
         2 * 10**9,
-        [pltpu.VMEM((tokens + window + SUBLANES, 2 * BLOCK), F32)],
-    )(info, stash, cotangent)
+        [pltpu.VMEM((tokens + window + SUBLANES, BLOCK), F32)],
+        3 * VMEM,
+    )(info, values)[0]
 
 
 NT = (((1,), (1,)), ((), ()))
@@ -184,6 +183,7 @@
         [(whole(shape), shape, BF16)],
         10**9,
         [pltpu.VMEM(shape, F32)],
+        3 * VMEM,
     )(windows, up, scale)[0]
 
 
@@ -550,9 +550,10 @@
     other_cotangent = send(cotangent, OTHER_CORE)
 
     info = slots(forward_counts, backward_counts, ranks, adapter_slot)
-    stash_windows, grad_windows = windows_of(info, stash, cotangent, adapters, window, rows)
+    grad_windows = windows_of(info, cotangent, adapters, window, rows)
     grad_windows = lax.all_to_all(grad_windows, "tp", split_axis=0, concat_axis=0, tiled=True)
 
+    stash_windows = windows_of(info, stash, adapters, window, rows)
     stash_windows, other_weight = lax.optimization_barrier((stash_windows, other_weight))
     stash_windows = lax.all_to_all(stash_windows, "tp", split_axis=0, concat_axis=0, tiled=True)
 

time: 178 us -> 179 us (level)
  waiting for transfers between devices: 49.8 us -> 42.5 us
  starting transfers between devices: 46.9 us -> 49.5 us
  Pallas kernels: 49.2 us -> 51 us
    ppermute x26, waiting for transfers between devices: 34.7 us -> 29.1 us  [send(): return lax.ppermute(value, 'tp', pairs)]
    ppermute x26, starting transfers between devices: 24.3 us -> 27.3 us  [send(): return lax.ppermute(value, 'tp', pairs)]
    pallas_call x1 -> x2, Pallas kernels: 3.28 us -> 5.21 us  [windows_of(): kernel(functools.partial(windows_body, adapters, window, each), 'windows'...]
    unnamed x48 -> x54, local copies, waits for them, and re-layouts: 12.1 us -> 13.7 us
  transfers between devices with their start and end apart: 31 -> 31, of which waited for: 9 -> 9; matrix products, arithmetic and copies ran while one was open for 10% -> 11% of each run, Pallas kernels for 28% -> 29%
where the time goes in v4:
time: 179 us; the launch traced here: 176 us
  Pallas kernels  51 us (28%)
  starting transfers between devices  49.5 us (28%)
  waiting for transfers between devices  42.5 us (24%)
  local copies, waits for them, and re-layouts  17.1 us (10%)
  other arithmetic  15.2 us (8%)
    ppermute x26, waiting for transfers between devices, send(): return lax.ppermute(value, 'tp', pairs)  29.1 us
    ppermute x26, starting transfers between devices, send(): return lax.ppermute(value, 'tp', pairs)  27.3 us
    unnamed x54, local copies, waits for them, and re-layouts  13.7 us
    pallas_call x3, Pallas kernels, backward_product(): kernel(functools.partial(backward_body, sizes), 'backward_product', (bloc...  12.8 us
    convert_element_type x6, other arithmetic, add_rounded(): return total_of(*values).astype(BF16)  11.2 us
    pallas_call x1, Pallas kernels, forward_product(): kernel(functools.partial(forward_body, window), 'forward_product', (CHIPS...  10.8 us
    all_to_all x1, waiting for transfers between devices, shards(): lax.all_to_all(grad_windows, 'tp', split_axis=0, concat_axis=0, tiled=True)  7.82 us
    all_to_all x1, starting transfers between devices, shards(): lax.all_to_all(grad_windows, 'tp', split_axis=0, concat_axis=0, tiled=True)  7.79 us
  transfers between devices with their start and end apart: 31, of which 9 were waited for; matrix products, arithmetic and copies ran while one was open for 11% of the time, Pallas kernels for 29%

profile of v4, /device:TPU:0, one launch (start us, length us, event | category | flops | bytes accessed | tf_op | source)
XLA Modules:
  0.0 176.5 jit_solution(3300134054924765196)
XLA Ops:
  0.6 2.9 %collective-permute-start.5 = (bf16[1024,256]{1,0:T(8,128)(2,1)}, bf16[1024,256]{1,0:T(8,128)(2,1)S(1)}, u32[]{:S(2)}, u32[]{:S(2)}) collective-permute-start(bf16[1024,256]{1,0:T(8,128)(2,1)} %bitcast.61), channel_id=1, source_target_pairs={{0,6},{1,25},{2,0},{3,27},{4,2},{5,29},{6,4},{7,31},{8,14},{9,1},{... | collective-permute-start | bytes 1572872 | tf_op jit(solution)/shard_map/ppermute | solution.py:42
  4.4 1.7 slots.1.info_ref
  7.8 2.6 %windows.2 = bf16[32,64,256]{2,1,0:T(8,128)(2,1)} custom-call(s32[320]{0:T(512)S(1)} %copy-done.15, bf16[1024,256]{1,0:T(8,128)(2,1)S(1)} %bitcast.60), custom_call_target="tpu_custom_call" | custom-call | flops 2000000000 | bytes 2097152 | tf_op jit(solution)/shard_map/windows/pallas_call | solution.py:131
  10.5 7.8 %all-to-all-start = ((bf16[32,64,256]{2,1,0:T(8,128)(2,1)}), bf16[32,64,256]{2,1,0:T(8,128)(2,1)}, u32[]{:S(2)}, u32[]{:S(2)}) async-start(bf16[32,64,256]{2,1,0:T(8,128)(2,1)} %windows.2), calls=%async_computation | async-start | bytes 2097152 | tf_op jit(solution)/shard_map/all_to_all | solution.py:554
  18.3 3.1 %dynamic-slice_bitcast_fusion = bf16[16,256,256]{2,1,0:T(8,128)(2,1)} fusion(bf16[16,2,256,256]{3,2,1,0:T(8,128)(2,1)} %bitcast.50, s32[]{:T(128)S(6)} %select_n.133), kind=kLoop, calls=%fused_computation.2 | loop fusion | bytes 4194308 | tf_op jit(solution)/shard_map/jit(dynamic_index_in_dim)/squeeze | solution.py:548
  22.7 2.1 %pad_maximum_fusion.1.rest_2_ = bf16[2,1024,256]{2,1,0:T(8,128)(2,1)} fusion(bf16[1,1024,256]{2,1,0:T(8,128)(2,1)S(1)} %bitcast.69, bf16[1,1024,256]{2,1,0:T(8,128)(2,1)} %bitcast.13), kind=kLoop, calls=%fused_computation.4 | loop fusion | flops 524288 | bytes 2097152 | tf_op jit(solution)/shard_map/stack | solution.py:539
  24.8 1.7 collective-permute-start.8
  26.5 1.3 pad_maximum_fusion.grad_ref
  27.7 7.8 %all-to-all-done.windows_ref.grad_ref = bf16[32,64,256]{2,1,0:T(8,128)(2,1)} async-done(((bf16[32,64,256]{2,1,0:T(8,128)(2,1)}), bf16[32,64,256]{2,1,0:T(8,128)(2,1)}, u32[]{:S(2)}, u32[]{:S(2)}) %all-to-all-start) | async-done | bytes 1048608 | tf_op jit(solution)/shard_map/all_to_all | solution.py:554
  35.6 2.2 %copy-done.3 = bf16[1,2,128,8192]{3,2,1,0:T(8,128)(2,1)S(1)} copy-done((bf16[1,2,128,8192]{3,2,1,0:T(8,128)(2,1)S(1)}, bf16[1,2,128,8192]{3,2,1,0:T(8,128)(2,1)}, u32[]{:S(2)}) %copy-start.3) | copy-done | bytes 4194328
  37.7 3.5 %code_grads.1.grads_ref = bf16[64,256]{1,0:T(8,128)(2,1)S(1)} custom-call(bf16[32,64,256]{2,1,0:T(8,128)(2,1)} %all-to-all-done.windows_ref.grad_ref, bf16[2,128,8192]{2,1,0:T(8,128)(2,1)S(1)} %bitcast.56, f32[64,256]{1,0:T(8,128)S(1)} %and_select_fusion.scale_ref), custom_call_target="tpu_custom_call" | custom-call | flops 1000000000 | bytes 65536 | tf_op jit(solution)/shard_map/code_grads/pallas_call | solution.py:173
  41.3 1.9 %returned.1 = (bf16[16,64,256]{2,1,0:T(8,128)(2,1)S(1)}, bf16[16,64,256]{2,1,0:T(8,128)(2,1)S(1)}) custom-call(s32[1]{0:T(128)} %bitcast.6.core_ref, bf16[64,256]{1,0:T(8,128)(2,1)S(1)} %code_grads.1.grads_ref, bf16[2,16,2,256,128]{4,3,2,1,0:T(8,128)(2,1)S(1)} %bitcast.45, bf16[2,16,2,256,128]{4,3,2,1,0:T(8,128)(2,1)S(1)} %bitcast.46), custom_call_target="tpu_custom_call" | custom-call | flops 1000000000 | bytes 2097152 | tf_op jit(solution)/shard_map/returned/pallas_call | solution.py:246
  44.4 1.2 collective-permute-start.6
  46.1 2.6 %windows.3 = bf16[32,64,256]{2,1,0:T(8,128)(2,1)} custom-call(s32[320]{0:T(512)S(1)} %copy-done.16, bf16[1024,256]{1,0:T(8,128)(2,1)S(1)} %bitcast.67), custom_call_target="tpu_custom_call" | custom-call | flops 2000000000 | bytes 2097152 | tf_op jit(solution)/shard_map/windows/pallas_call | solution.py:131
  48.7 3.0 %backward_product.3 = (bf16[2,1024,256]{2,1,0:T(8,128)(2,1)S(1)}, bf16[2,1024,256]{2,1,0:T(8,128)(2,1)S(1)}) custom-call(s32[18]{0:T(128)S(1)} %add_add_fusion.order_ref, bf16[1024,512]{1,0:T(8,128)(2,1)S(1)} %pad_maximum_fusion.grad_ref, bf16[16,2,256,256]{3,2,1,0:T(8,128)(2,1)S(1)} %bitcast.51, ...), custom_call_target="tpu_custom_call" | custom-call | flops 1360000000 | bytes 4194304 | tf_op jit(solution)/shard_map/backward_product/pallas_call | solution.py:476
  52.7 2.3 %collective-permute-start.12 = (bf16[1024,256]{1,0:T(8,128)(2,1)S(1)}, bf16[1024,256]{1,0:T(8,128)(2,1)S(1)}, u32[]{:S(2)}, u32[]{:S(2)}) collective-permute-start(bf16[1024,256]{1,0:T(8,128)(2,1)S(1)} %collective-permute-done.9.rest_6_), channel_id=1, source_target_pairs={{0,24},{1,7},{2,26},{3,1},{4,28},{5,3},{6,30},{7,5},{8,0},{9,15},{... | collective-permute-start | bytes 1572872 | tf_op jit(solution)/shard_map/ppermute | solution.py:42
  55.0 6.9 %collective-permute-done.4.rest_1_ = bf16[1024,256]{1,0:T(8,128)(2,1)} collective-permute-done((bf16[1024,256]{1,0:T(8,128)(2,1)}, bf16[1024,256]{1,0:T(8,128)(2,1)}, u32[]{:S(2)}, u32[]{:S(2)}) %collective-permute-start.4) | collective-permute-done | bytes 524320 | tf_op jit(solution)/shard_map/ppermute | solution.py:42
  62.0 2.0 %collective-permute-start.10 = (bf16[1024,256]{1,0:T(8,128)(2,1)}, bf16[1024,256]{1,0:T(8,128)(2,1)S(1)}, u32[]{:S(2)}, u32[]{:S(2)}) collective-permute-start(bf16[1024,256]{1,0:T(8,128)(2,1)} %collective-permute-done.4.rest_1_), channel_id=1, source_target_pairs={{0,24},{1,7},{2,26},{3,1},{4,28},{5,3},{6,30},{7,5},{8,0},{9,15},{... | collective-permute-start | bytes 1572872 | tf_op jit(solution)/shard_map/ppermute | solution.py:42
  64.8 2.0 %collective-permute-start.14 = (bf16[2,1024,256]{2,1,0:T(8,128)(2,1)}, bf16[2,1024,256]{2,1,0:T(8,128)(2,1)S(1)}, u32[]{:S(2)}, u32[]{:S(2)}) collective-permute-start(bf16[2,1024,256]{2,1,0:T(8,128)(2,1)} %collective-permute-done.8.rest_5_), channel_id=1, source_target_pairs={{0,8},{1,3},{2,10},{3,5},{4,12},{5,7},{6,14},{7,1},{8,16},{9,11},{... | collective-permute-start | bytes 3145736 | tf_op jit(solution)/shard_map/ppermute | solution.py:42
  66.8 4.2 %backward_product.4 = (bf16[2,1024,256]{2,1,0:T(8,128)(2,1)}, bf16[2,1024,256]{2,1,0:T(8,128)(2,1)}) custom-call(s32[18]{0:T(128)S(1)} %add_add_fusion.order_ref, bf16[1024,512]{1,0:T(8,128)(2,1)S(1)} %pad_maximum_fusion.grad_ref, bf16[16,2,256,256]{3,2,1,0:T(8,128)(2,1)S(1)} %bitcast.52, ...), custom_call_target="tpu_custom_call" | custom-call | flops 1360000000 | bytes 4194304 | tf_op jit(solution)/shard_map/backward_product/pallas_call | solution.py:476
  71.4 3.2 %collective-permute-start.13 = (bf16[1024,256]{1,0:T(8,128)(2,1)S(1)}, bf16[1024,256]{1,0:T(8,128)(2,1)S(1)}, u32[]{:S(2)}, u32[]{:S(2)}) collective-permute-start(bf16[1024,256]{1,0:T(8,128)(2,1)S(1)} %collective-permute-done.10.rest_7_), channel_id=1, source_target_pairs={{0,24},{1,7},{2,26},{3,1},{4,28},{5,3},{6,30},{7,5},{8,0},{9,15},{... | collective-permute-start | bytes 1572872 | tf_op jit(solution)/shard_map/ppermute | solution.py:42
  74.6 5.6 %backward_product.5 = (bf16[2,1024,256]{2,1,0:T(8,128)(2,1)S(1)}, bf16[2,1024,256]{2,1,0:T(8,128)(2,1)S(1)}, bf16[2,1024,256]{2,1,0:T(8,128)(2,1)S(1)}, bf16[2,1024,256]{2,1,0:T(8,128)(2,1)S(1)}) custom-call(s32[18]{0:T(128)S(1)} %add_add_fusion.order_ref, bf16[1024,512]{1,0:T(8,128)(2,1)S(1)} %pad_maximum_fusion.grad_ref, ...), custom_call_target="tpu_custom_call" | custom-call | flops 2720000000 | bytes 8388608 | tf_op jit(solution)/shard_map/backward_product/pallas_call | solution.py:476
  81.3 1.3 add_convert_fusion
  82.6 5.9 %collective-permute-done.7.rest_4_ = bf16[1024,256]{1,0:T(8,128)(2,1)S(1)} collective-permute-done((bf16[1024,256]{1,0:T(8,128)(2,1)}, bf16[1024,256]{1,0:T(8,128)(2,1)S(1)}, u32[]{:S(2)}, u32[]{:S(2)}) %collective-permute-start.7) | collective-permute-done | bytes 524320 | tf_op jit(solution)/shard_map/ppermute | solution.py:42
  88.5 3.2 %collective-permute-start.23 = (bf16[2,1024,256]{2,1,0:T(8,128)(2,1)}, bf16[2,1024,256]{2,1,0:T(8,128)(2,1)}, u32[]{:S(2)}, u32[]{:S(2)}) collective-permute-start(bf16[2,1024,256]{2,1,0:T(8,128)(2,1)} %get-tuple-element.66), channel_id=1, source_target_pairs={{0,24},{1,7},{2,26},{3,1},{4,28},{5,3},{6,30},{7,5},{8,0},{9,15},{... | collective-permute-start | bytes 3145736 | tf_op jit(solution)/shard_map/ppermute | solution.py:42
  91.7 10.8 %forward_product.1 = (f32[1024,256]{1,0:T(8,128)S(1)}, f32[1024,256]{1,0:T(8,128)}, bf16[16,64,256]{2,1,0:T(8,128)(2,1)S(1)}, bf16[16,64,256]{2,1,0:T(8,128)(2,1)S(1)}) custom-call(s32[18]{0:T(128)S(1)} %add_add_fusion.1.order_ref, s32[320]{0:T(512)S(1)} %copy-done.16, bf16[1024,256]{1,0:T(8,128)(2,1)S(1)} %bitcast.65, ...), custom_call_target="tpu_custom_call" | custom-call | flops 8999999488 | bytes 4194304 | tf_op jit(solution)/shard_map/forward_product/pallas_call | solution.py:436
  102.6 1.3 add_convert_fusion.1
  103.9 3.2 %collective-permute-start.20 = (bf16[2,1024,256]{2,1,0:T(8,128)(2,1)}, bf16[2,1024,256]{2,1,0:T(8,128)(2,1)}, u32[]{:S(2)}, u32[]{:S(2)}) collective-permute-start(bf16[2,1024,256]{2,1,0:T(8,128)(2,1)} %add_convert_fusion.1), channel_id=1, source_target_pairs={{0,24},{1,7},{2,26},{3,1},{4,28},{5,3},{6,30},{7,5},{8,0},{9,15},{... | collective-permute-start | bytes 3145736 | tf_op jit(solution)/shard_map/ppermute | solution.py:42
  107.1 1.3 forward_codes.1.codes_ref
  109.3 2.5 %adapter_rows.1 = bf16[32,64,256]{2,1,0:T(8,128)(2,1)} custom-call(bf16[64,256]{1,0:T(8,128)(2,1)S(1)} %forward_codes.1.codes_ref, bf16[2,128,8192]{2,1,0:T(8,128)(2,1)S(1)} %bitcast.57), custom_call_target="tpu_custom_call" | custom-call | flops 1000000000 | bytes 2097152 | tf_op jit(solution)/shard_map/adapter_rows/pallas_call | solution.py:302
  111.9 4.1 %all-to-all-start.1 = ((bf16[32,64,256]{2,1,0:T(8,128)(2,1)}), bf16[32,64,256]{2,1,0:T(8,128)(2,1)S(1)}, u32[]{:S(2)}, u32[]{:S(2)}) async-start(bf16[32,64,256]{2,1,0:T(8,128)(2,1)} %adapter_rows.1), calls=%async_computation.1 | async-start | bytes 2097152 | tf_op jit(solution)/shard_map/all_to_all | solution.py:624
  116.0 1.4 fusion.4
  117.4 1.7 collective-permute-start.24
  119.1 13.8 %collective-permute-done.20 = bf16[2,1024,256]{2,1,0:T(8,128)(2,1)} collective-permute-done((bf16[2,1024,256]{2,1,0:T(8,128)(2,1)}, bf16[2,1024,256]{2,1,0:T(8,128)(2,1)}, u32[]{:S(2)}, u32[]{:S(2)}) %collective-permute-start.20) | collective-permute-done | bytes 1048608 | tf_op jit(solution)/shard_map/ppermute | solution.py:42
  132.9 2.2 %fusion.5 = bf16[1024,256]{1,0:T(8,128)(2,1)} fusion(bf16[2,1024,256]{2,1,0:T(8,128)(2,1)} %collective-permute-done.20, bf16[2,1024,256]{2,1,0:T(8,128)(2,1)} %collective-permute-done.18, bf16[2,1024,256]{2,1,0:T(8,128)(2,1)S(1)} %copy-done.8), kind=kLoop, calls=%fused_computation.16 | loop fusion | flops 1572864 | bytes 2097152 | tf_op jit(solution)/shard_map/convert_element_type | solution.py:502
  135.1 1.7 collective-permute-done.24
  136.8 2.3 %fusion.3 = bf16[1024,256]{1,0:T(8,128)(2,1)} fusion(bf16[1024,256]{1,0:T(8,128)(2,1)S(1)} %collective-permute-done.24, bf16[2,1024,256]{2,1,0:T(8,128)(2,1)} %collective-permute-done.23, bf16[2,1024,256]{2,1,0:T(8,128)(2,1)} %collective-permute-done.22, bf16[2,1024,256]{2,1,0:T(8,128)(2,1)S(1)} %copy-done.10), kind=kLoop, calls=%fused_computation.12 | loop fusion | flops 2097152 | bytes 2621440 | tf_op jit(solution)/shard_map/convert_element_type | solution.py:502
  139.4 7.1 %all-to-all-start.2 = ((bf16[32,64,256]{2,1,0:T(8,128)(2,1)}), bf16[32,64,256]{2,1,0:T(8,128)(2,1)S(1)}, u32[]{:S(2)}, u32[]{:S(2)}) async-start(bf16[32,64,256]{2,1,0:T(8,128)(2,1)} %windows.3), calls=%async_computation.2 | async-start | bytes 2097152 | tf_op jit(solution)/shard_map/all_to_all | solution.py:558
  146.5 1.2 copy-done.12
  148.8 3.5 %forward_sum.1 = bf16[1024,256]{1,0:T(8,128)(2,1)} custom-call(s32[320]{0:T(512)S(1)} %copy-done.16, bf16[1024,256]{1,0:T(8,128)(2,1)S(1)} %bitcast.66, f32[1024,256]{1,0:T(8,128)S(1)} %copy-done.12, f32[1024,256]{1,0:T(8,128)} %collective-permute-done.15.other_ref, bf16[32,64,256]{2,1,0:T(8,128)(2,1)S(1)} %all-to-all-done.1.adapter_ref), custom_call_target="tpu_custom_call" | custom-call | flops 100000000 | bytes 1048576 | tf_op jit(solution)/shard_map/forward_sum/pallas_call | solution.py:334
  152.2 1.6 collective-permute-start.17
  153.8 2.7 %fusion.2 = bf16[1024,256]{1,0:T(8,128)(2,1)} fusion(bf16[1024,256]{1,0:T(8,128)(2,1)} %collective-permute-done.26, bf16[1024,256]{1,0:T(8,128)(2,1)} %collective-permute-done.25, bf16[2,1024,256]{2,1,0:T(8,128)(2,1)} %collective-permute-done.20, bf16[2,1024,256]{2,1,0:T(8,128)(2,1)} %collective-permute-done.18, bf16[2,1024,256]{2,1,0:T(8,128)(2,1)S(1)} %copy-done.8, ...), kind=kLoop, calls=%fused_computation.8 | loop fusion | flops 3145728 | bytes 3670016 | tf_op jit(solution)/shard_map/convert_element_type | solution.py:502
  156.6 1.7 collective-permute-start.27
  158.2 5.6 %all-to-all-done.2.windows_ref.stash_ref = bf16[32,64,256]{2,1,0:T(8,128)(2,1)S(1)} async-done(((bf16[32,64,256]{2,1,0:T(8,128)(2,1)}), bf16[32,64,256]{2,1,0:T(8,128)(2,1)S(1)}, u32[]{:S(2)}, u32[]{:S(2)}) %all-to-all-start.2) | async-done | bytes 1048608 | tf_op jit(solution)/shard_map/all_to_all | solution.py:558
  163.8 2.2 %copy-done.1 = bf16[1,2,8192,128]{3,2,1,0:T(8,128)(2,1)S(1)} copy-done((bf16[1,2,8192,128]{3,2,1,0:T(8,128)(2,1)S(1)}, bf16[1,2,8192,128]{3,2,1,0:T(8,128)(2,1)}, u32[]{:S(2)}) %copy-start.1) | copy-done | bytes 4194328
  166.0 1.6 back_codes.1.codes_ref
  167.6 6.2 %gradients.1 = (bf16[2,8192,128]{2,1,0:T(8,128)(2,1)}, bf16[2,128,8192]{2,1,0:T(8,128)(2,1)}) custom-call(bf16[32,64,256]{2,1,0:T(8,128)(2,1)S(1)} %all-to-all-done.2.windows_ref.stash_ref, bf16[32,64,256]{2,1,0:T(8,128)(2,1)} %all-to-all-done.windows_ref.grad_ref, bf16[64,256]{1,0:T(8,128)(2,1)S(1)} %back_codes.1.codes_ref, ...), custom_call_target="tpu_custom_call" | custom-call | flops 2000000000 | bytes 16777216 | tf_op jit(solution)/shard_map/gradients/pallas_call | solution.py:362
  173.8 1.9 %copy.20 = bf16[1,1024,256]{2,1,0:T(8,128)(2,1)} copy(bf16[1,1024,256]{2,1,0:T(8,128)(2,1)} %bitcast.15) | data formatting | bytes 1048576
  (106 shorter events, 11.8 us)
Async XLA Ops:
  0.6 22.0 %collective-permute-start.5 = (bf16[1024,256]{1,0:T(8,128)(2,1)}, bf16[1024,256]{1,0:T(8,128)(2,1)S(1)}, u32[]{:S(2)}, u32[]{:S(2)}) collective-permute-start(bf16[1024,256]{1,0:T(8,128)(2,1)} %bitcast.61), channel_id=1, source_target_pairs={{0,6},{1,25},{2,0},{3,27},{4,2},{5,29},{6,4},{7,31},{8,14},{9,1},{... | collective-permute-start | bytes 1572872 | tf_op jit(solution)/shard_map/ppermute | solution.py:42
  3.5 19.1 %collective-permute-start.3 = (bf16[1024,256]{1,0:T(8,128)(2,1)}, bf16[1024,256]{1,0:T(8,128)(2,1)}, u32[]{:S(2)}, u32[]{:S(2)}) collective-permute-start(bf16[1024,256]{1,0:T(8,128)(2,1)} %bitcast.62), channel_id=1, source_target_pairs={{0,2},{1,9},{2,4},{3,11},{4,6},{5,13},{6,0},{7,15},{8,10},{9,17},{... | collective-permute-start | bytes 1572872 | tf_op jit(solution)/shard_map/ppermute | solution.py:42
  3.5 22.9 %collective-permute-start = (bf16[1024,256]{1,0:T(8,128)(2,1)}, bf16[1024,256]{1,0:T(8,128)(2,1)}, u32[]{:S(2)}, u32[]{:S(2)}) collective-permute-start(bf16[1024,256]{1,0:T(8,128)(2,1)} %bitcast.58), channel_id=1, source_target_pairs={{0,1},{1,0},{2,3},{3,2},{4,5},{5,4},{6,7},{7,6},{8,9},{9,8},{10,11... | collective-permute-start | bytes 1572872 | tf_op jit(solution)/shard_map/ppermute | solution.py:42
  10.5 25.1 %all-to-all-start = ((bf16[32,64,256]{2,1,0:T(8,128)(2,1)}), bf16[32,64,256]{2,1,0:T(8,128)(2,1)}, u32[]{:S(2)}, u32[]{:S(2)}) async-start(bf16[32,64,256]{2,1,0:T(8,128)(2,1)} %windows.2), calls=%async_computation | async-start | bytes 2097152 | tf_op jit(solution)/shard_map/all_to_all | solution.py:554
  18.3 3.4 %copy-start.16 = (s32[320]{0:T(512)S(1)}, s32[320]{0:T(512)}, u32[]{:S(2)}) copy-start(s32[320]{0:T(512)} %slots.1.info_ref) | copy-start | bytes 3844
  18.3 4.0 %copy-start.22 = (s32[16]{0:T(128)S(1)}, s32[16]{0:T(128)}, u32[]{:S(2)}) copy-start(s32[16]{0:T(128)} %constant.141.clone) | copy-start | bytes 196
  18.3 4.0 %copy-start.23 = (s32[16]{0:T(128)S(1)}, s32[16]{0:T(128)}, u32[]{:S(2)}) copy-start(s32[16]{0:T(128)} %constant.140.clone) | copy-start | bytes 196
  18.3 4.0 %copy-start.24 = (s32[16]{0:T(128)S(1)}, s32[16]{0:T(128)}, u32[]{:S(2)}) copy-start(s32[16]{0:T(128)} %constant.139.clone) | copy-start | bytes 196
  18.3 4.0 %copy-start.25 = (s32[16]{0:T(128)S(1)}, s32[16]{0:T(128)}, u32[]{:S(2)}) copy-start(s32[16]{0:T(128)} %constant.138.clone) | copy-start | bytes 196
  21.4 24.1 %collective-permute-start.1 = (bf16[16,256,256]{2,1,0:T(8,128)(2,1)}, bf16[16,256,256]{2,1,0:T(8,128)(2,1)S(1)}, u32[]{:S(2)}, u32[]{:S(2)}) collective-permute-start(bf16[16,256,256]{2,1,0:T(8,128)(2,1)} %dynamic-slice_bitcast_fusion), channel_id=1, source_target_pairs={{0,1},{1,0},{2,3},{3,2},{4,5},{5,4},{6,7},{7,6},{8,9},{9,8},{10,11... | collective-permute-start | bytes 6291464 | tf_op jit(solution)/shard_map/ppermute | solution.py:42
  24.8 40.0 %collective-permute-start.8 = (bf16[2,1024,256]{2,1,0:T(8,128)(2,1)}, bf16[2,1024,256]{2,1,0:T(8,128)(2,1)}, u32[]{:S(2)}, u32[]{:S(2)}) collective-permute-start(bf16[2,1024,256]{2,1,0:T(8,128)(2,1)} %pad_maximum_fusion.1.rest_2_), channel_id=1, source_target_pairs={{0,8},{1,3},{2,10},{3,5},{4,12},{5,7},{6,14},{7,1},{8,16},{9,11},{... | collective-permute-start | bytes 3145736 | tf_op jit(solution)/shard_map/ppermute | solution.py:42
  37.7 3.5 %copy-start = (bf16[1,2,8192,128]{3,2,1,0:T(8,128)(2,1)S(1)}, bf16[1,2,8192,128]{3,2,1,0:T(8,128)(2,1)}, u32[]{:S(2)}) copy-start(bf16[1,2,8192,128]{3,2,1,0:T(8,128)(2,1)} %param.18) | copy-start | bytes 12582916
  41.3 2.3 %copy-start.13 = (bf16[1,1024,256]{2,1,0:T(8,128)(2,1)S(1)}, bf16[1,1024,256]{2,1,0:T(8,128)(2,1)}, u32[]{:S(2)}) copy-start(bf16[1,1024,256]{2,1,0:T(8,128)(2,1)} %param.14) | copy-start | bytes 1572868
  41.3 4.8 %copy-start.17 = (bf16[1,1024,256]{2,1,0:T(8,128)(2,1)S(1)}, bf16[1,1024,256]{2,1,0:T(8,128)(2,1)}, u32[]{:S(2)}) copy-start(bf16[1,1024,256]{2,1,0:T(8,128)(2,1)} %param.15) | copy-start | bytes 1572868
  43.2 5.5 %collective-permute-start.2 = (bf16[16,64,256]{2,1,0:T(8,128)(2,1)S(1)}, bf16[16,64,256]{2,1,0:T(8,128)(2,1)S(1)}, u32[]{:S(2)}, u32[]{:S(2)}) collective-permute-start(bf16[16,64,256]{2,1,0:T(8,128)(2,1)S(1)} %get-tuple-element.45), channel_id=1, source_target_pairs={{0,1},{1,0},{2,3},{3,2},{4,5},{5,4},{6,7},{7,6},{8,9},{9,8},{10,11... | collective-permute-start | bytes 1572872 | tf_op jit(solution)/shard_map/ppermute | solution.py:42
  43.6 9.2 %collective-permute-start.9 = (bf16[1024,256]{1,0:T(8,128)(2,1)S(1)}, bf16[1024,256]{1,0:T(8,128)(2,1)S(1)}, u32[]{:S(2)}, u32[]{:S(2)}) collective-permute-start(bf16[1024,256]{1,0:T(8,128)(2,1)S(1)} %bitcast.63), channel_id=1, source_target_pairs={{0,24},{1,7},{2,26},{3,1},{4,28},{5,3},{6,30},{7,5},{8,0},{9,15},{... | collective-permute-start | bytes 1572872 | tf_op jit(solution)/shard_map/ppermute | solution.py:42
  44.4 19.6 %collective-permute-start.6 = (bf16[1024,256]{1,0:T(8,128)(2,1)S(1)}, bf16[1024,256]{1,0:T(8,128)(2,1)S(1)}, u32[]{:S(2)}, u32[]{:S(2)}) collective-permute-start(bf16[1024,256]{1,0:T(8,128)(2,1)S(1)} %bitcast.64), channel_id=1, source_target_pairs={{0,8},{1,3},{2,10},{3,5},{4,12},{5,7},{6,14},{7,1},{8,16},{9,11},{... | collective-permute-start | bytes 1572872 | tf_op jit(solution)/shard_map/ppermute | solution.py:42
  45.6 16.4 %collective-permute-start.4 = (bf16[1024,256]{1,0:T(8,128)(2,1)}, bf16[1024,256]{1,0:T(8,128)(2,1)}, u32[]{:S(2)}, u32[]{:S(2)}) collective-permute-start(bf16[1024,256]{1,0:T(8,128)(2,1)} %collective-permute-done.3), channel_id=1, source_target_pairs={{0,2},{1,9},{2,4},{3,11},{4,6},{5,13},{6,0},{7,15},{8,10},{9,17},{... | collective-permute-start | bytes 1572872 | tf_op jit(solution)/shard_map/ppermute | solution.py:42
  46.1 2.6 %copy-start.2 = (bf16[1,8192,256]{2,1,0:T(8,128)(2,1)S(1)}, bf16[1,8192,256]{2,1,0:T(8,128)(2,1)}, u32[]{:S(2)}) copy-start(bf16[1,8192,256]{2,1,0:T(8,128)(2,1)} %param.17) | copy-start | bytes 12582916
  51.7 29.4 %collective-permute-start.21 = (bf16[2,1024,256]{2,1,0:T(8,128)(2,1)S(1)}, bf16[2,1024,256]{2,1,0:T(8,128)(2,1)S(1)}, u32[]{:S(2)}, u32[]{:S(2)}) collective-permute-start(bf16[2,1024,256]{2,1,0:T(8,128)(2,1)S(1)} %get-tuple-element.65), channel_id=1, source_target_pairs={{0,8},{1,3},{2,10},{3,5},{4,12},{5,7},{6,14},{7,1},{8,16},{9,11},{... | collective-permute-start | bytes 3145736 | tf_op jit(solution)/shard_map/ppermute | solution.py:42
  52.7 18.3 %copy-start.18 = (bf16[1024,256]{1,0:T(8,128)(2,1)}, bf16[1024,256]{1,0:T(8,128)(2,1)S(1)}, u32[]{:S(2)}) copy-start(bf16[1024,256]{1,0:T(8,128)(2,1)S(1)} %collective-permute-done.9.rest_6_) | copy-start | bytes 1572868
  52.7 18.3 %collective-permute-start.12 = (bf16[1024,256]{1,0:T(8,128)(2,1)S(1)}, bf16[1024,256]{1,0:T(8,128)(2,1)S(1)}, u32[]{:S(2)}, u32[]{:S(2)}) collective-permute-start(bf16[1024,256]{1,0:T(8,128)(2,1)S(1)} %collective-permute-done.9.rest_6_), channel_id=1, source_target_pairs={{0,24},{1,7},{2,26},{3,1},{4,28},{5,3},{6,30},{7,5},{8,0},{9,15},{... | collective-permute-start | bytes 1572872 | tf_op jit(solution)/shard_map/ppermute | solution.py:42
  62.0 9.4 %collective-permute-start.10 = (bf16[1024,256]{1,0:T(8,128)(2,1)}, bf16[1024,256]{1,0:T(8,128)(2,1)S(1)}, u32[]{:S(2)}, u32[]{:S(2)}) collective-permute-start(bf16[1024,256]{1,0:T(8,128)(2,1)} %collective-permute-done.4.rest_1_), channel_id=1, source_target_pairs={{0,24},{1,7},{2,26},{3,1},{4,28},{5,3},{6,30},{7,5},{8,0},{9,15},{... | collective-permute-start | bytes 1572872 | tf_op jit(solution)/shard_map/ppermute | solution.py:42
  64.8 23.7 %collective-permute-start.11 = (bf16[2,1024,256]{2,1,0:T(8,128)(2,1)}, bf16[2,1024,256]{2,1,0:T(8,128)(2,1)S(1)}, u32[]{:S(2)}, u32[]{:S(2)}) collective-permute-start(bf16[2,1024,256]{2,1,0:T(8,128)(2,1)} %pad_maximum_fusion.1.rest_2_), channel_id=1, source_target_pairs={{0,24},{1,7},{2,26},{3,1},{4,28},{5,3},{6,30},{7,5},{8,0},{9,15},{... | collective-permute-start | bytes 3145736 | tf_op jit(solution)/shard_map/ppermute | solution.py:42
  64.8 26.9 %collective-permute-start.14 = (bf16[2,1024,256]{2,1,0:T(8,128)(2,1)}, bf16[2,1024,256]{2,1,0:T(8,128)(2,1)S(1)}, u32[]{:S(2)}, u32[]{:S(2)}) collective-permute-start(bf16[2,1024,256]{2,1,0:T(8,128)(2,1)} %collective-permute-done.8.rest_5_), channel_id=1, source_target_pairs={{0,8},{1,3},{2,10},{3,5},{4,12},{5,7},{6,14},{7,1},{8,16},{9,11},{... | collective-permute-start | bytes 3145736 | tf_op jit(solution)/shard_map/ppermute | solution.py:42
  71.1 17.4 %collective-permute-start.7 = (bf16[1024,256]{1,0:T(8,128)(2,1)}, bf16[1024,256]{1,0:T(8,128)(2,1)S(1)}, u32[]{:S(2)}, u32[]{:S(2)}) collective-permute-start(bf16[1024,256]{1,0:T(8,128)(2,1)} %collective-permute-done.4.rest_1_), channel_id=1, source_target_pairs={{0,8},{1,3},{2,10},{3,5},{4,12},{5,7},{6,14},{7,1},{8,16},{9,11},{... | collective-permute-start | bytes 1572872 | tf_op jit(solution)/shard_map/ppermute | solution.py:42
  71.4 20.3 %collective-permute-start.13 = (bf16[1024,256]{1,0:T(8,128)(2,1)S(1)}, bf16[1024,256]{1,0:T(8,128)(2,1)S(1)}, u32[]{:S(2)}, u32[]{:S(2)}) collective-permute-start(bf16[1024,256]{1,0:T(8,128)(2,1)S(1)} %collective-permute-done.10.rest_7_), channel_id=1, source_target_pairs={{0,24},{1,7},{2,26},{3,1},{4,28},{5,3},{6,30},{7,5},{8,0},{9,15},{... | collective-permute-start | bytes 1572872 | tf_op jit(solution)/shard_map/ppermute | solution.py:42
  81.2 21.4 %copy-start.9 = (bf16[2,1024,256]{2,1,0:T(8,128)(2,1)}, bf16[2,1024,256]{2,1,0:T(8,128)(2,1)S(1)}, u32[]{:S(2)}) copy-start(bf16[2,1024,256]{2,1,0:T(8,128)(2,1)S(1)} %get-tuple-element.63) | copy-start | bytes 3145732
  81.2 10.6 %copy-start.19 = (bf16[1024,256]{1,0:T(8,128)(2,1)S(1)}, bf16[1024,256]{1,0:T(8,128)(2,1)}, u32[]{:S(2)}) copy-start(bf16[1024,256]{1,0:T(8,128)(2,1)} %copy-done.18) | copy-start | bytes 1572868
  81.2 10.6 %copy-start.21 = (bf16[1024,256]{1,0:T(8,128)(2,1)S(1)}, bf16[1024,256]{1,0:T(8,128)(2,1)}, u32[]{:S(2)}) copy-start(bf16[1024,256]{1,0:T(8,128)(2,1)} %copy-done.20) | copy-start | bytes 1572868
  81.2 21.4 %collective-permute-start.19 = (bf16[2,1024,256]{2,1,0:T(8,128)(2,1)S(1)}, bf16[2,1024,256]{2,1,0:T(8,128)(2,1)S(1)}, u32[]{:S(2)}, u32[]{:S(2)}) collective-permute-start(bf16[2,1024,256]{2,1,0:T(8,128)(2,1)S(1)} %get-tuple-element.62), channel_id=1, source_target_pairs={{0,24},{1,7},{2,26},{3,1},{4,28},{5,3},{6,30},{7,5},{8,0},{9,15},{... | collective-permute-start | bytes 3145736 | tf_op jit(solution)/shard_map/ppermute | solution.py:42
  88.5 30.7 %collective-permute-start.18 = (bf16[2,1024,256]{2,1,0:T(8,128)(2,1)}, bf16[2,1024,256]{2,1,0:T(8,128)(2,1)}, u32[]{:S(2)}, u32[]{:S(2)}) collective-permute-start(bf16[2,1024,256]{2,1,0:T(8,128)(2,1)} %get-tuple-element.60), channel_id=1, source_target_pairs={{0,8},{1,3},{2,10},{3,5},{4,12},{5,7},{6,14},{7,1},{8,16},{9,11},{... | collective-permute-start | bytes 3145736 | tf_op jit(solution)/shard_map/ppermute | solution.py:42
  88.5 27.5 %collective-permute-start.23 = (bf16[2,1024,256]{2,1,0:T(8,128)(2,1)}, bf16[2,1024,256]{2,1,0:T(8,128)(2,1)}, u32[]{:S(2)}, u32[]{:S(2)}) collective-permute-start(bf16[2,1024,256]{2,1,0:T(8,128)(2,1)} %get-tuple-element.66), channel_id=1, source_target_pairs={{0,24},{1,7},{2,26},{3,1},{4,28},{5,3},{6,30},{7,5},{8,0},{9,15},{... | collective-permute-start | bytes 3145736 | tf_op jit(solution)/shard_map/ppermute | solution.py:42
  91.7 24.3 %collective-permute-start.22 = (bf16[2,1024,256]{2,1,0:T(8,128)(2,1)}, bf16[2,1024,256]{2,1,0:T(8,128)(2,1)}, u32[]{:S(2)}, u32[]{:S(2)}) collective-permute-start(bf16[2,1024,256]{2,1,0:T(8,128)(2,1)} %add_convert_fusion), channel_id=1, source_target_pairs={{0,8},{1,3},{2,10},{3,5},{4,12},{5,7},{6,14},{7,1},{8,16},{9,11},{... | collective-permute-start | bytes 3145736 | tf_op jit(solution)/shard_map/ppermute | solution.py:42
  102.6 5.9 %copy-start.11 = (f32[1024,256]{1,0:T(8,128)}, f32[1024,256]{1,0:T(8,128)S(1)}, u32[]{:S(2)}) copy-start(f32[1024,256]{1,0:T(8,128)S(1)} %get-tuple-element.54.own_ref) | copy-start | bytes 3145732
  102.6 4.5 %collective-permute-start.16 = (bf16[16,64,256]{2,1,0:T(8,128)(2,1)S(1)}, bf16[16,64,256]{2,1,0:T(8,128)(2,1)S(1)}, u32[]{:S(2)}, u32[]{:S(2)}) collective-permute-start(bf16[16,64,256]{2,1,0:T(8,128)(2,1)S(1)} %get-tuple-element.57), channel_id=1, source_target_pairs={{0,1},{1,0},{2,3},{3,2},{4,5},{5,4},{6,7},{7,6},{8,9},{9,8},{10,11... | collective-permute-start | bytes 1572872 | tf_op jit(solution)/shard_map/ppermute | solution.py:42
  103.9 29.0 %collective-permute-start.20 = (bf16[2,1024,256]{2,1,0:T(8,128)(2,1)}, bf16[2,1024,256]{2,1,0:T(8,128)(2,1)}, u32[]{:S(2)}, u32[]{:S(2)}) collective-permute-start(bf16[2,1024,256]{2,1,0:T(8,128)(2,1)} %add_convert_fusion.1), channel_id=1, source_target_pairs={{0,24},{1,7},{2,26},{3,1},{4,28},{5,3},{6,30},{7,5},{8,0},{9,15},{... | collective-permute-start | bytes 3145736 | tf_op jit(solution)/shard_map/ppermute | solution.py:42
  111.9 4.2 %copy-start.10 = (bf16[2,1024,256]{2,1,0:T(8,128)(2,1)S(1)}, bf16[2,1024,256]{2,1,0:T(8,128)(2,1)}, u32[]{:S(2)}) copy-start(bf16[2,1024,256]{2,1,0:T(8,128)(2,1)} %copy-done.9) | copy-start | bytes 3145732
  111.9 21.0 %copy-start.8 = (bf16[2,1024,256]{2,1,0:T(8,128)(2,1)S(1)}, bf16[2,1024,256]{2,1,0:T(8,128)(2,1)}, u32[]{:S(2)}) copy-start(bf16[2,1024,256]{2,1,0:T(8,128)(2,1)} %copy-done.7) | copy-start | bytes 3145732
  111.9 27.5 %all-to-all-start.1 = ((bf16[32,64,256]{2,1,0:T(8,128)(2,1)}), bf16[32,64,256]{2,1,0:T(8,128)(2,1)S(1)}, u32[]{:S(2)}, u32[]{:S(2)}) async-start(bf16[32,64,256]{2,1,0:T(8,128)(2,1)} %adapter_rows.1), calls=%async_computation.1 | async-start | bytes 2097152 | tf_op jit(solution)/shard_map/all_to_all | solution.py:624
  117.4 19.4 %collective-permute-start.24 = (bf16[1024,256]{1,0:T(8,128)(2,1)S(1)}, bf16[1024,256]{1,0:T(8,128)(2,1)S(1)}, u32[]{:S(2)}, u32[]{:S(2)}) collective-permute-start(bf16[1024,256]{1,0:T(8,128)(2,1)S(1)} %fusion.4), channel_id=1, source_target_pairs={{0,2},{1,9},{2,4},{3,11},{4,6},{5,13},{6,0},{7,15},{8,10},{9,17},{... | collective-permute-start | bytes 1572872 | tf_op jit(solution)/shard_map/ppermute | solution.py:42
  119.1 27.4 %collective-permute-start.15 = (f32[1024,256]{1,0:T(8,128)}, f32[1024,256]{1,0:T(8,128)}, u32[]{:S(2)}, u32[]{:S(2)}) collective-permute-start(f32[1024,256]{1,0:T(8,128)} %get-tuple-element.55), channel_id=1, source_target_pairs={{0,1},{1,0},{2,3},{3,2},{4,5},{5,4},{6,7},{7,6},{8,9},{9,8},{10,11... | collective-permute-start | bytes 3145736 | tf_op jit(solution)/shard_map/ppermute | solution.py:42
  135.1 18.7 %collective-permute-start.26 = (bf16[1024,256]{1,0:T(8,128)(2,1)}, bf16[1024,256]{1,0:T(8,128)(2,1)}, u32[]{:S(2)}, u32[]{:S(2)}) collective-permute-start(bf16[1024,256]{1,0:T(8,128)(2,1)} %fusion.5), channel_id=1, source_target_pairs={{0,6},{1,25},{2,0},{3,27},{4,2},{5,29},{6,4},{7,31},{8,14},{9,1},{... | collective-permute-start | bytes 1572872 | tf_op jit(solution)/shard_map/ppermute | solution.py:42
  139.1 14.8 %collective-permute-start.25 = (bf16[1024,256]{1,0:T(8,128)(2,1)}, bf16[1024,256]{1,0:T(8,128)(2,1)}, u32[]{:S(2)}, u32[]{:S(2)}) collective-permute-start(bf16[1024,256]{1,0:T(8,128)(2,1)} %fusion.3), channel_id=1, source_target_pairs={{0,2},{1,9},{2,4},{3,11},{4,6},{5,13},{6,0},{7,15},{8,10},{9,17},{... | collective-permute-start | bytes 1572872 | tf_op jit(solution)/shard_map/ppermute | solution.py:42
  139.4 24.5 %all-to-all-start.2 = ((bf16[32,64,256]{2,1,0:T(8,128)(2,1)}), bf16[32,64,256]{2,1,0:T(8,128)(2,1)S(1)}, u32[]{:S(2)}, u32[]{:S(2)}) async-start(bf16[32,64,256]{2,1,0:T(8,128)(2,1)} %windows.3), calls=%async_computation.2 | async-start | bytes 2097152 | tf_op jit(solution)/shard_map/all_to_all | solution.py:558
  148.8 5.0 %copy-start.6 = (bf16[1,1024,256]{2,1,0:T(8,128)(2,1)S(1)}, bf16[1,1024,256]{2,1,0:T(8,128)(2,1)}, u32[]{:S(2)}) copy-start(bf16[1,1024,256]{2,1,0:T(8,128)(2,1)} %param.16) | copy-start | bytes 1572868
  152.2 21.5 %collective-permute-start.17 = (bf16[1024,256]{1,0:T(8,128)(2,1)}, bf16[1024,256]{1,0:T(8,128)(2,1)}, u32[]{:S(2)}, u32[]{:S(2)}) collective-permute-start(bf16[1024,256]{1,0:T(8,128)(2,1)} %forward_sum.1), channel_id=1, source_target_pairs={{0,32},{32,64},{64,96},{96,0},{1,33},{33,65},{65,97},{97,1},{2,34}... | collective-permute-start | bytes 1572872 | tf_op jit(solution)/shard_map/ppermute | solution.py:48
  156.6 17.2 %collective-permute-start.27 = (bf16[1024,256]{1,0:T(8,128)(2,1)}, bf16[1024,256]{1,0:T(8,128)(2,1)S(1)}, u32[]{:S(2)}, u32[]{:S(2)}) collective-permute-start(bf16[1024,256]{1,0:T(8,128)(2,1)} %fusion.2), channel_id=1, source_target_pairs={{0,96},{32,0},{64,32},{96,64},{1,97},{33,1},{65,33},{97,65},{2,98}... | collective-permute-start | bytes 1572872 | tf_op jit(solution)/shard_map/ppermute | solution.py:48
  (9 other events, 12.4 us)
